TPU v7x, 256 devices: a whole 4x4x8 slice. The times are simulated.
256 devices in a mesh: chan: 8 (over z_lo, core), bl: 32 (over y, z_hi, x).
Axes of the slice: x: 4, y: 4, z: 8 (z_hi: 2, z_lo: 4; z = z_hi * 4 + z_lo), core: 2. Of those that a mesh axis runs over, the one named last changes fastest.
Arguments:
- visibility: bfloat16 [2, 1024, 1024], P(None, ('chan', 'bl')), may hold values from -6 to 6
- weights: bfloat16 [1024, 1024], P(('chan', 'bl')), may hold values from 0.25 to 1
- positions: float32 [2, 512], replicated, may hold values from -96 to 96
- station_pairs: int32 [2, 1024], P(None, ('chan', 'bl')), may hold values from 0 to 511
- facet_shift: int32 [2, 2], replicated, may hold values from -512 to 512
Outputs:
- subband_images: float32 [8, 512, 1024], P('chan', 'bl')
All inputs are finite; a program needn't handle non-finite values.
Results may differ from a plain program's by a relative error of at most 0.0037.
Values may be sent and summed in bfloat16 or wider, within the bound.
No kernel may reach another device: no remote copies, remote signals or barrier semaphores. Data moves between devices by JAX's collectives and lax.ppermute only.
A program may use at most 64 MiB of HBM per device.

v0:
```python
import math

import jax
import jax.numpy as jnp
from jax import lax
from jax.sharding import PartitionSpec as P

PIX = 512
FACETS = 2


two_pi = 2.0 * math.pi


def facet_term(data, offsets, facet, row_total):
    real_flat, imag_flat, east_flat, north_flat = data
    total_rows = real_flat.shape[0]
    block_size = math.gcd(total_rows, 1024)
    block_total = total_rows // block_size
    columns = lax.iota(jnp.float32, PIX)
    contract = (((0,), (0,)), ((), ()))
    row_index = lax.iota(jnp.int32, row_total).astype(jnp.float32)
    left_coord = (offsets[0, facet] + row_index - PIX // 2) / PIX
    right_coord = (offsets[1, facet] + columns - PIX // 2) / PIX

    def accumulate(block, total):
        first_row = block * block_size

        def select(values):
            return lax.dynamic_slice_in_dim(values, first_row, block_size)

        real_blk = select(real_flat)
        imag_blk = select(imag_flat)
        angle_left = select(east_flat)[:, None] * left_coord[None, :]
        cos_left = jnp.cos(angle_left)
        sin_left = jnp.sin(angle_left)
        left_real = (real_blk[:, None] * cos_left - imag_blk[:, None] * sin_left).astype(
            jnp.bfloat16
        )
        left_imag = (real_blk[:, None] * sin_left + imag_blk[:, None] * cos_left).astype(
            jnp.bfloat16
        )
        angle_right = select(north_flat)[:, None] * right_coord[None, :]
        cos_right = jnp.cos(angle_right).astype(jnp.bfloat16)
        sin_right = jnp.sin(angle_right).astype(jnp.bfloat16)
        total = total + lax.dot_general(
            left_real, cos_right, contract, preferred_element_type=jnp.float32
        )
        return total - lax.dot_general(
            left_imag, sin_right, contract, preferred_element_type=jnp.float32
        )

    return lax.fori_loop(0, block_total, accumulate, jnp.zeros((row_total, PIX), jnp.float32))


def body(visibility, weights, positions, station_pairs, facet_shift):
    chan_count = lax.axis_size("chan")
    line_count = lax.axis_size("bl")
    read_rows = visibility.shape[1]
    channels = visibility.shape[2]
    group_width = channels // chan_count
    stacked = jnp.concatenate([visibility, weights[None]], axis=0)
    arrived = lax.all_to_all(stacked, "chan", split_axis=2, concat_axis=1, tiled=True)
    owned_pairs = lax.all_gather(station_pairs, "chan", axis=1, tiled=True)
    east_span = jnp.take(positions[0], owned_pairs[0]) - jnp.take(positions[0], owned_pairs[1])
    north_span = jnp.take(positions[1], owned_pairs[0]) - jnp.take(positions[1], owned_pairs[1])
    channel_ids = lax.axis_index("chan") * group_width + lax.iota(jnp.int32, group_width)
    frequency = 1.0 + channel_ids.astype(jnp.float32) / channels
    east_turns = two_pi * (east_span[:, None] * frequency[None, :])
    north_turns = two_pi * (north_span[:, None] * frequency[None, :])
    weight_part = arrived[2].astype(jnp.float32)
    real_part = weight_part * arrived[0].astype(jnp.float32)
    imag_part = weight_part * arrived[1].astype(jnp.float32)
    total_rows = real_part.shape[0] * real_part.shape[1]
    data = (
        real_part.reshape(total_rows),
        imag_part.reshape(total_rows),
        east_turns.reshape(total_rows),
        north_turns.reshape(total_rows),
    )
    offsets = facet_shift.astype(jnp.float32)
    image_scale = 1.0 / math.sqrt(read_rows * chan_count * line_count * group_width)
    row_count = PIX // line_count
    image = lax.psum_scatter(
        jnp.concatenate(
            [
                facet_term(data, offsets, facet, row_count * lax.axis_size("bl"))
                for facet in range(FACETS)
            ],
            axis=1,
        ),
        "bl",
        scatter_dimension=0,
        tiled=True,
    )
    return (image * image_scale)[None]


def solution(mesh):
    in_specs = (
        P(None, ("chan", "bl"), None),
        P(("chan", "bl"), None),
        P(),
        P(None, ("chan", "bl")),
        P(),
    )
    out_specs = P("chan", "bl", None)
    return jax.shard_map(body, mesh=mesh, in_specs=in_specs, out_specs=out_specs, check_vma=False)
```

profile of v0, /device:TPU:32, one launch (start us, length us, event | category | flops | bytes accessed | tf_op | source)
XLA Modules:
  0.0 540.6 jit_solution(17055732578637854569)
XLA Ops:
  6.5 0.8 pad_maximum_fusion.1
  7.3 0.0 copy-start.2
  7.3 0.7 copy.17
  8.1 1.5 reshape.101
  9.6 6.0 %all-to-all-start = ((bf16[8,2,768]{2,1,0:T(2,128)(2,1)}), bf16[8,2,768]{2,1,0:T(2,128)(2,1)S(1)}, u32[]{:S(2)}, u32[]{:S(2)}) async-start(bf16[8,2,768]{2,1,0:T(2,128)(2,1)} %reshape.101), calls=%async_computation | async-start | bytes 49152 | tf_op jit(solution)/shard_map/all_to_all | solution.py:63
  15.6 0.0 reduce-scatter.2.cloned.1.call-start
  15.6 0.0 copy-done
  15.6 8.9 %all-gather = s32[8,4,2]{1,2,0:T(2,128)S(1)} all-gather(s32[1,4,2]{1,2,0:T(2,128)S(1)} %bitcast.49), channel_id=1, replica_groups=mesh['chan'=8,'bl'=32] {'chan'}, dimensions={0}, use_global_device_ids=true | all-gather | bytes 288 | tf_op jit(solution)/shard_map/all_gather | solution.py:64
  24.5 0.1 reshape.92
  24.6 0.7 gather_fusion.3
  25.4 0.7 gather_fusion.1
  26.1 0.7 gather_fusion
  26.8 0.7 gather_fusion.2
  27.5 0.1 multiply_bitcast_fusion.1
  27.6 0.7 fusion.61
  28.3 0.0 all-to-all-done
  28.3 0.9 reshape.102
  29.2 0.6 copy.18
  29.8 124.3 %while.29 = (s32[]{:T(128)}, f32[512,512]{1,0:T(8,128)S(1)}, f32[4096]{0:T(1024)S(1)}, f32[4096]{0:T(1024)S(1)}, f32[4096]{0:T(1024)S(1)}, /*index=5*/f32[4096]{...) while((s32[]{:T(128)}, f32[512,512]{1,0:T(8,128)S(1)}, ...), condition=%wide.region_3.5_spmd.clone, body=%wide.region_2.4_spmd.clone.sunk | while | flops 1081871872 | bytes 4272333 | solution.py:53
  30.1 1.3 add_multiply_fusion.7
  31.3 14.8 %convolution_add_fusion.5 = f32[512,512]{1,0:T(8,128)S(1)} fusion(f32[512,512]{1,0:T(8,128)S(1)} %get-tuple-element.523, f32[512]{0:T(512)S(1)} %get-tuple-element.508, f32[1024]{0:T(1024)S(1)} %dynamic_slice.76, f32[1024]{0:T(1024)S(1)} %dynamic_slice.77, f32[512]{0:T(512)S(1)} %get-tuple-element.509, f32[1024]{0:T(1024)S(1)} %dynamic_slice.78, ...), kind=kOutput, calls=%fused_computation.53.clone.1 | convolution fusion | flops 541065216 | bytes 2117633 | tf_op jit(solution)/shard_map/while/body/eval_jaxpr/dot_general | solution.py:46
  46.1 14.9 %convolution_subtract_fusion.5 = f32[512,512]{1,0:T(8,128)S(1)} fusion(f32[512,512]{1,0:T(8,128)S(1)} %convolution_add_fusion.5, f32[512]{0:T(512)S(1)} %get-tuple-element.508, f32[1024]{0:T(1024)S(1)} %dynamic_slice.76, f32[1024]{0:T(1024)S(1)} %dynamic_slice.77, f32[512]{0:T(512)S(1)} %get-tuple-element.509, f32[1024]{0:T(1024)S(1)} %dynamic_slice.78, ...), kind=kOutput, calls=%fused_computation.52.clone.1 | convolution fusion | flops 540803072 | bytes 2117632 | tf_op jit(solution)/shard_map/while/body/eval_jaxpr/dot_general | solution.py:49
  61.1 1.3 add_multiply_fusion.7
  62.4 14.8 %convolution_add_fusion.5 = f32[512,512]{1,0:T(8,128)S(1)} fusion(f32[512,512]{1,0:T(8,128)S(1)} %get-tuple-element.523, f32[512]{0:T(512)S(1)} %get-tuple-element.508, f32[1024]{0:T(1024)S(1)} %dynamic_slice.76, f32[1024]{0:T(1024)S(1)} %dynamic_slice.77, f32[512]{0:T(512)S(1)} %get-tuple-element.509, f32[1024]{0:T(1024)S(1)} %dynamic_slice.78, ...), kind=kOutput, calls=%fused_computation.53.clone.1 | convolution fusion | flops 541065216 | bytes 2117633 | tf_op jit(solution)/shard_map/while/body/eval_jaxpr/dot_general | solution.py:46
  77.2 14.9 %convolution_subtract_fusion.5 = f32[512,512]{1,0:T(8,128)S(1)} fusion(f32[512,512]{1,0:T(8,128)S(1)} %convolution_add_fusion.5, f32[512]{0:T(512)S(1)} %get-tuple-element.508, f32[1024]{0:T(1024)S(1)} %dynamic_slice.76, f32[1024]{0:T(1024)S(1)} %dynamic_slice.77, f32[512]{0:T(512)S(1)} %get-tuple-element.509, f32[1024]{0:T(1024)S(1)} %dynamic_slice.78, ...), kind=kOutput, calls=%fused_computation.52.clone.1 | convolution fusion | flops 540803072 | bytes 2117632 | tf_op jit(solution)/shard_map/while/body/eval_jaxpr/dot_general | solution.py:49
  92.1 1.3 add_multiply_fusion.7
  93.4 14.8 %convolution_add_fusion.5 = f32[512,512]{1,0:T(8,128)S(1)} fusion(f32[512,512]{1,0:T(8,128)S(1)} %get-tuple-element.523, f32[512]{0:T(512)S(1)} %get-tuple-element.508, f32[1024]{0:T(1024)S(1)} %dynamic_slice.76, f32[1024]{0:T(1024)S(1)} %dynamic_slice.77, f32[512]{0:T(512)S(1)} %get-tuple-element.509, f32[1024]{0:T(1024)S(1)} %dynamic_slice.78, ...), kind=kOutput, calls=%fused_computation.53.clone.1 | convolution fusion | flops 541065216 | bytes 2117633 | tf_op jit(solution)/shard_map/while/body/eval_jaxpr/dot_general | solution.py:46
  108.2 14.9 %convolution_subtract_fusion.5 = f32[512,512]{1,0:T(8,128)S(1)} fusion(f32[512,512]{1,0:T(8,128)S(1)} %convolution_add_fusion.5, f32[512]{0:T(512)S(1)} %get-tuple-element.508, f32[1024]{0:T(1024)S(1)} %dynamic_slice.76, f32[1024]{0:T(1024)S(1)} %dynamic_slice.77, f32[512]{0:T(512)S(1)} %get-tuple-element.509, f32[1024]{0:T(1024)S(1)} %dynamic_slice.78, ...), kind=kOutput, calls=%fused_computation.52.clone.1 | convolution fusion | flops 540803072 | bytes 2117632 | tf_op jit(solution)/shard_map/while/body/eval_jaxpr/dot_general | solution.py:49
  123.2 1.3 add_multiply_fusion.7
  124.4 14.8 %convolution_add_fusion.5 = f32[512,512]{1,0:T(8,128)S(1)} fusion(f32[512,512]{1,0:T(8,128)S(1)} %get-tuple-element.523, f32[512]{0:T(512)S(1)} %get-tuple-element.508, f32[1024]{0:T(1024)S(1)} %dynamic_slice.76, f32[1024]{0:T(1024)S(1)} %dynamic_slice.77, f32[512]{0:T(512)S(1)} %get-tuple-element.509, f32[1024]{0:T(1024)S(1)} %dynamic_slice.78, ...), kind=kOutput, calls=%fused_computation.53.clone.1 | convolution fusion | flops 541065216 | bytes 2117633 | tf_op jit(solution)/shard_map/while/body/eval_jaxpr/dot_general | solution.py:46
  139.2 14.9 %convolution_subtract_fusion.5 = f32[512,512]{1,0:T(8,128)S(1)} fusion(f32[512,512]{1,0:T(8,128)S(1)} %convolution_add_fusion.5, f32[512]{0:T(512)S(1)} %get-tuple-element.508, f32[1024]{0:T(1024)S(1)} %dynamic_slice.76, f32[1024]{0:T(1024)S(1)} %dynamic_slice.77, f32[512]{0:T(512)S(1)} %get-tuple-element.509, f32[1024]{0:T(1024)S(1)} %dynamic_slice.78, ...), kind=kOutput, calls=%fused_computation.52.clone.1 | convolution fusion | flops 540803072 | bytes 2117632 | tf_op jit(solution)/shard_map/while/body/eval_jaxpr/dot_general | solution.py:49
  154.1 144.6 %while.28 = (s32[]{:T(128)}, f32[512,512]{1,0:T(8,128)S(1)}, f32[4096]{0:T(1024)S(1)}, f32[4096]{0:T(1024)S(1)}, f32[4096]{0:T(1024)S(1)}, /*index=5*/f32[4096]{...) while((s32[]{:T(128)}, f32[512,512]{1,0:T(8,128)S(1)}, ...), condition=%wide.region_1.3_spmd.clone, body=%wide.region_0.0_spmd.clone.sunk | while | flops 1081871872 | bytes 4272333 | solution.py:53
  175.0 1.2 add_multiply_fusion.6
  176.2 14.8 %convolution_add_fusion.4 = f32[512,512]{1,0:T(8,128)S(1)} fusion(f32[512,512]{1,0:T(8,128)S(1)} %get-tuple-element.559, f32[512]{0:T(512)S(1)} %get-tuple-element.498, f32[1024]{0:T(1024)S(1)} %dynamic_slice.72, f32[1024]{0:T(1024)S(1)} %dynamic_slice.73, f32[512]{0:T(512)S(1)} %get-tuple-element.499, f32[1024]{0:T(1024)S(1)} %dynamic_slice.74, ...), kind=kOutput, calls=%fused_computation.23.clone.1 | convolution fusion | flops 541065216 | bytes 2117633 | tf_op jit(solution)/shard_map/while/body/eval_jaxpr/dot_general | solution.py:46
  191.0 14.9 %convolution_subtract_fusion.4 = f32[512,512]{1,0:T(8,128)S(1)} fusion(f32[512,512]{1,0:T(8,128)S(1)} %convolution_add_fusion.4, f32[512]{0:T(512)S(1)} %get-tuple-element.498, f32[1024]{0:T(1024)S(1)} %dynamic_slice.72, f32[1024]{0:T(1024)S(1)} %dynamic_slice.73, f32[512]{0:T(512)S(1)} %get-tuple-element.499, f32[1024]{0:T(1024)S(1)} %dynamic_slice.74, ...), kind=kOutput, calls=%fused_computation.22.clone.1 | convolution fusion | flops 540803072 | bytes 2117632 | tf_op jit(solution)/shard_map/while/body/eval_jaxpr/dot_general | solution.py:49
  206.0 1.2 add_multiply_fusion.6
  207.2 14.8 %convolution_add_fusion.4 = f32[512,512]{1,0:T(8,128)S(1)} fusion(f32[512,512]{1,0:T(8,128)S(1)} %get-tuple-element.559, f32[512]{0:T(512)S(1)} %get-tuple-element.498, f32[1024]{0:T(1024)S(1)} %dynamic_slice.72, f32[1024]{0:T(1024)S(1)} %dynamic_slice.73, f32[512]{0:T(512)S(1)} %get-tuple-element.499, f32[1024]{0:T(1024)S(1)} %dynamic_slice.74, ...), kind=kOutput, calls=%fused_computation.23.clone.1 | convolution fusion | flops 541065216 | bytes 2117633 | tf_op jit(solution)/shard_map/while/body/eval_jaxpr/dot_general | solution.py:46
  222.0 14.9 %convolution_subtract_fusion.4 = f32[512,512]{1,0:T(8,128)S(1)} fusion(f32[512,512]{1,0:T(8,128)S(1)} %convolution_add_fusion.4, f32[512]{0:T(512)S(1)} %get-tuple-element.498, f32[1024]{0:T(1024)S(1)} %dynamic_slice.72, f32[1024]{0:T(1024)S(1)} %dynamic_slice.73, f32[512]{0:T(512)S(1)} %get-tuple-element.499, f32[1024]{0:T(1024)S(1)} %dynamic_slice.74, ...), kind=kOutput, calls=%fused_computation.22.clone.1 | convolution fusion | flops 540803072 | bytes 2117632 | tf_op jit(solution)/shard_map/while/body/eval_jaxpr/dot_general | solution.py:49
  236.9 1.2 add_multiply_fusion.6
  238.1 14.8 %convolution_add_fusion.4 = f32[512,512]{1,0:T(8,128)S(1)} fusion(f32[512,512]{1,0:T(8,128)S(1)} %get-tuple-element.559, f32[512]{0:T(512)S(1)} %get-tuple-element.498, f32[1024]{0:T(1024)S(1)} %dynamic_slice.72, f32[1024]{0:T(1024)S(1)} %dynamic_slice.73, f32[512]{0:T(512)S(1)} %get-tuple-element.499, f32[1024]{0:T(1024)S(1)} %dynamic_slice.74, ...), kind=kOutput, calls=%fused_computation.23.clone.1 | convolution fusion | flops 541065216 | bytes 2117633 | tf_op jit(solution)/shard_map/while/body/eval_jaxpr/dot_general | solution.py:46
  252.9 14.9 %convolution_subtract_fusion.4 = f32[512,512]{1,0:T(8,128)S(1)} fusion(f32[512,512]{1,0:T(8,128)S(1)} %convolution_add_fusion.4, f32[512]{0:T(512)S(1)} %get-tuple-element.498, f32[1024]{0:T(1024)S(1)} %dynamic_slice.72, f32[1024]{0:T(1024)S(1)} %dynamic_slice.73, f32[512]{0:T(512)S(1)} %get-tuple-element.499, f32[1024]{0:T(1024)S(1)} %dynamic_slice.74, ...), kind=kOutput, calls=%fused_computation.22.clone.1 | convolution fusion | flops 540803072 | bytes 2117632 | tf_op jit(solution)/shard_map/while/body/eval_jaxpr/dot_general | solution.py:49
  267.9 1.2 add_multiply_fusion.6
  269.1 14.8 %convolution_add_fusion.4 = f32[512,512]{1,0:T(8,128)S(1)} fusion(f32[512,512]{1,0:T(8,128)S(1)} %get-tuple-element.559, f32[512]{0:T(512)S(1)} %get-tuple-element.498, f32[1024]{0:T(1024)S(1)} %dynamic_slice.72, f32[1024]{0:T(1024)S(1)} %dynamic_slice.73, f32[512]{0:T(512)S(1)} %get-tuple-element.499, f32[1024]{0:T(1024)S(1)} %dynamic_slice.74, ...), kind=kOutput, calls=%fused_computation.23.clone.1 | convolution fusion | flops 541065216 | bytes 2117633 | tf_op jit(solution)/shard_map/while/body/eval_jaxpr/dot_general | solution.py:46
  283.9 14.9 %convolution_subtract_fusion.4 = f32[512,512]{1,0:T(8,128)S(1)} fusion(f32[512,512]{1,0:T(8,128)S(1)} %convolution_add_fusion.4, f32[512]{0:T(512)S(1)} %get-tuple-element.498, f32[1024]{0:T(1024)S(1)} %dynamic_slice.72, f32[1024]{0:T(1024)S(1)} %dynamic_slice.73, f32[512]{0:T(512)S(1)} %get-tuple-element.499, f32[1024]{0:T(1024)S(1)} %dynamic_slice.74, ...), kind=kOutput, calls=%fused_computation.22.clone.1 | convolution fusion | flops 540803072 | bytes 2117632 | tf_op jit(solution)/shard_map/while/body/eval_jaxpr/dot_general | solution.py:49
  298.8 1.5 pad_maximum_fusion
  300.3 0.0 reduce-scatter.2.cloned.1.call-update
  300.3 231.8 %reduce-scatter.2.cloned.1.call-done = f32[16,1024]{1,0:T(8,128)} async-done(((f32[512,1024]{1,0:T(8,128)}), f32[16,1024]{1,0:T(8,128)}) %reduce-scatter.2.cloned.1.call-update) | async-done | bytes 65552 | tf_op jit(solution)/shard_map/reduce_scatter | solution.py:84
  532.1 1.5 multiply_bitcast_fusion
  (46 shorter events, 0.4 us)
Async XLA Ops:
  6.5 9.0 %copy-start = (f32[2,512]{1,0:T(2,128)S(1)}, f32[2,512]{1,0:T(2,128)}, u32[]{:S(2)}) copy-start(f32[2,512]{1,0:T(2,128)} %param.13) | copy-start | bytes 12292
  6.5 9.0 %copy-start.1 = (s32[2,4]{1,0:T(2,128)S(1)}, s32[2,4]{1,0:T(2,128)}, u32[]{:S(2)}) copy-start(s32[2,4]{1,0:T(2,128)} %param.14) | copy-start | bytes 100
  7.3 20.2 %copy-start.2 = (s32[2,2]{1,0:T(2,128)S(1)}, s32[2,2]{1,0:T(2,128)}, u32[]{:S(2)}) copy-start(s32[2,2]{1,0:T(2,128)} %param.15) | copy-start | bytes 52
  9.6 18.7 %all-to-all-start = ((bf16[8,2,768]{2,1,0:T(2,128)(2,1)}), bf16[8,2,768]{2,1,0:T(2,128)(2,1)S(1)}, u32[]{:S(2)}, u32[]{:S(2)}) async-start(bf16[8,2,768]{2,1,0:T(2,128)(2,1)} %reshape.101), calls=%async_computation | async-start | bytes 49152 | tf_op jit(solution)/shard_map/all_to_all | solution.py:63
  15.6 516.5 %reduce-scatter.2.cloned.1.call-start = ((), (), s32[]{:S(2)}) async-start(), calls=%async_computation.2 | async-start | bytes 2162688 | tf_op jit(solution)/shard_map/reduce_scatter | solution.py:84
Sparse Core Ops, SparseCore 0:
  300.4 231.6 reduce-scatter.1
where the time goes:
time: 544 us; the launch traced here: 541 us
  matrix products  237 us (44%)
  waiting for transfers between devices  232 us (43%)
  loops' own time  21.6 us (4%)
  other arithmetic  13.7 us (3%)
  between operations  13.7 us (3%)
  blocking collectives  8.95 us (2%)
  local copies, waits for them, and re-layouts  7.63 us (1%)
  starting transfers between devices  6.01 us (1%)
    reduce_scatter x1, waiting for transfers between devices, body(): lax.psum_scatter(jnp.concatenate([facet_term(data, offsets, facet, row_co...  232 us
    dot_general x8, matrix products, accumulate(): lax.dot_general(left_imag, sin_right, contract, preferred_element_type=jn...  119 us
    dot_general x8, matrix products, accumulate(): lax.dot_general(left_real, cos_right, contract, preferred_element_type=jn...  118 us
    another operation x2, loops' own time, facet_term(): lax.fori_loop(0, block_total, accumulate, jnp.zeros((row_total, PIX), jnp...  21.6 us
  transfers between devices with their start and end apart: 2, of which 1 were waited for; matrix products, arithmetic and copies ran while one was open for 1% of the time, Pallas kernels for 0%

commit v1 on v0

v1 whole, which is shorter than its diff:
```python
import functools
import math

import jax
import jax.numpy as jnp
from jax import lax
from jax.experimental import pallas as pl
from jax.experimental.pallas import tpu as pltpu
from jax.sharding import Mesh, PartitionSpec as P

PIX = 512
HALF = PIX // 2
FACETS = 2
CHANNELS = 1024
GROUPS = 8
LANES = 128
READ_ROWS = 4
RUN_ROWS = 64
RUNS = 4
STEPS = RUN_ROWS // 8
HALVES = 2
SOURCES = GROUPS * HALVES
BLOCKS = SOURCES * READ_ROWS
CHUNK_BLOCKS = 8
CHUNK = CHUNK_BLOCKS * LANES
CHUNKS = BLOCKS // CHUNK_BLOCKS
PEERS = 16
OUT_ROWS = 16
COS_COEF = (
    1.0, -19.739208221435547, 64.93939208984375, -85.45665740966797,
    60.242130279541016, -26.4046688079834, 7.800131797790527, -1.4531123638153076,
)
SIN_COEF = (
    6.2831854820251465, -41.34170150756836, 81.60513305664062, -76.70301818847656,
    42.02592849731445, -14.899847984313965, 3.238137722015381,
)


def poly(coef, z):
    total = jnp.full_like(z, coef[-1])
    for c in coef[-2::-1]:
        total = total * z + c
    return total


def frac(turns):
    return turns - jnp.floor(turns + 0.5)


def cos_sin_reduced(r):
    z = r * r
    return poly(COS_COEF, z), poly(SIN_COEF, z) * r


def cos_sin(turns):
    return cos_sin_reduced(frac(turns))


def pack_kernel(vis_ref, weight_ref, pos_ref, pair_ref, out_ref):
    weight = weight_ref[...].astype(jnp.float32)
    real = weight * vis_ref[0].astype(jnp.float32)
    imag = weight * vis_ref[1].astype(jnp.float32)
    shape = (READ_ROWS, CHANNELS)
    channel = lax.broadcasted_iota(jnp.int32, shape, 1).astype(jnp.float32)
    frequency = 1.0 + channel / CHANNELS
    row = lax.broadcasted_iota(jnp.int32, shape, 0)
    spans = []
    for axis in range(2):
        span = jnp.zeros(shape, jnp.float32)
        for b in range(READ_ROWS):
            value = pos_ref[axis, pair_ref[0, b]] - pos_ref[axis, pair_ref[1, b]]
            span = jnp.where(row == b, value, span)
        spans.append(span * frequency)
    for a, values in enumerate((real, imag, *spans)):
        for g in range(GROUPS):
            part = values[:, g * LANES : (g + 1) * LANES]
            for h in range(HALVES):
                out_ref[g * HALVES + h, a * READ_ROWS : (a + 1) * READ_ROWS, :] = part


(V0R, V0I, V1R, V1I, EAST, NORTH, C8E, S8E, C128E, S128E, C8N, S8N, C64N, S64N, TABLE) = range(15)


def image_kernel(half_ref, shift_ref, data_ref, out_ref, table, acc, *slots):
    for s in range(SOURCES):
        for a, t in enumerate((V0R, V0I, EAST, NORTH)):
            table[t, s * READ_ROWS : (s + 1) * READ_ROWS, :] = data_ref[
                s, a * READ_ROWS : (a + 1) * READ_ROWS, :
            ]
    base_row = half_ref[0] * RUN_ROWS - HALF

    def prepare(i, carry):
        rows = pl.ds(pl.multiple_of(i * 8, 8), 8)
        east = table[EAST, rows, :]
        north = table[NORTH, rows, :]
        real = table[V0R, rows, :]
        imag = table[V0I, rows, :]
        for f in range(FACETS):
            left = (shift_ref[0, f] + base_row).astype(jnp.float32) * (1.0 / PIX)
            right = (shift_ref[1, f].astype(jnp.float32) - 0.5) * (1.0 / PIX)
            cos, sin = cos_sin(frac(east * left) + frac(north * right))
            table[V0R + 2 * f, rows, :] = real * cos - imag * sin
            table[V0I + 2 * f, rows, :] = real * sin + imag * cos
        for t, turns in (
            (C8E, east * (8.0 / PIX)),
            (C128E, east * (128.0 / PIX)),
            (C8N, north * (8.0 / PIX)),
            (C64N, north * (64.0 / PIX)),
        ):
            cos, sin = cos_sin(turns)
            table[t, rows, :] = cos
            table[t + 1, rows, :] = sin
        return carry

    lax.fori_loop(0, BLOCKS // 8, prepare, 0)

    lane_row = lax.broadcasted_iota(jnp.int32, (8, LANES), 0).astype(jnp.float32)

    def rotate(u, turn):
        (ur, ui), (c, s) = u, turn
        return ur * c - ui * s, ur * s + ui * c

    def generate(first_block, slot):
        left_re, left_im, right_re, right_im = slot
        for t in range(CHUNK_BLOCKS):
            block = first_block + t
            lanes = slice(t * LANES, (t + 1) * LANES)

            def row(i):
                return jnp.broadcast_to(table[i, pl.ds(block, 1), :], (8, LANES))

            def emit(refs, first_row, stride, start, turn_run, turn_step):
                anchors = [(start, rotate(start, turn_step))]
                anchors.append(tuple(rotate(u, turn_run) for u in anchors[0]))
                twice_run = 2.0 * turn_run[0]
                for _ in range(RUNS - 2):
                    anchors.append(
                        tuple(
                            tuple(twice_run * b - a for a, b in zip(old, new))
                            for old, new in zip(anchors[-2], anchors[-1])
                        )
                    )
                twice = 2.0 * turn_step[0]
                for r, (first, second) in enumerate(anchors):
                    for part, ref in enumerate(refs):
                        before, now = first[part], second[part]
                        for j in range(0, STEPS, 2):
                            if j:
                                before = twice * now - before
                                now = twice * before - now
                            at = first_row + r * stride + j * 8
                            ref[at : at + 16, lanes] = jnp.concatenate(
                                [before, now], axis=0
                            ).astype(jnp.bfloat16)

            base = cos_sin(row(EAST) * (lane_row * (1.0 / PIX)))
            turn_run = (row(C128E), row(S128E))
            turn_step = (row(C8E), row(S8E))
            for f in range(FACETS):
                start = rotate(base, (row(V0R + 2 * f), row(V0I + 2 * f)))
                emit((left_re, left_im), f * HALF, RUN_ROWS, start, turn_run, turn_step)
            start = cos_sin(row(NORTH) * ((lane_row + 0.5) * (1.0 / PIX)))
            emit(
                (right_re, right_im), 0, RUN_ROWS, start,
                (row(C64N), row(S64N)), (row(C8N), row(S8N)),
            )

    def multiply(slot):
        left_re, left_im, right_re, right_im = slot
        contract = (((1,), (1,)), ((), ()))
        for i, (left, right) in enumerate(((left_re, right_re), (left_im, right_im))):
            acc[i] += lax.dot_general(
                left[...], right[...], contract, preferred_element_type=jnp.float32
            )

    slot_a, slot_b = slots[:4], slots[4:]
    acc[...] = jnp.zeros_like(acc)
    generate(0, slot_a)

    def step(i, carry):
        first = i * (2 * CHUNK_BLOCKS)
        generate(first + CHUNK_BLOCKS, slot_b)
        multiply(slot_a)
        generate(lax.rem(first + 2 * CHUNK_BLOCKS, BLOCKS), slot_a)
        multiply(slot_b)
        return carry

    lax.fori_loop(0, CHUNKS // 2, step, 0)
    for f in range(FACETS):
        for i in range(2):
            column = (f * 2 + i) * HALF
            out_ref[:, column : column + HALF] = acc[i, f * HALF : (f + 1) * HALF].astype(
                jnp.bfloat16
            )


def combine_kernel(scale, data_ref, out_ref):
    total = data_ref[0].astype(jnp.float32)
    for i in range(1, PEERS):
        total = total + data_ref[i].astype(jnp.float32)
    total = total * scale
    flip = (
        lax.broadcasted_iota(jnp.int32, (HALF, HALF), 0)
        + lax.broadcasted_iota(jnp.int32, (HALF, HALF), 1)
        == HALF - 1
    ).astype(jnp.bfloat16)
    for f in range(FACETS):
        even = total[:, f * PIX : f * PIX + HALF]
        odd = total[:, f * PIX + HALF : (f + 1) * PIX]
        rest = even + odd
        mirrored = jnp.zeros_like(rest)
        for _ in range(3):
            part = rest.astype(jnp.bfloat16)
            rest = rest - part.astype(jnp.float32)
            mirrored = mirrored + jnp.dot(part, flip, preferred_element_type=jnp.float32)
        out_ref[0, :, f * PIX : f * PIX + HALF] = mirrored
        out_ref[0, :, f * PIX + HALF : (f + 1) * PIX] = even - odd


VMEM = pl.BlockSpec(memory_space=pltpu.VMEM)
SMEM = pl.BlockSpec(memory_space=pltpu.SMEM)


def pack(visibility, weights, positions, station_pairs):
    return pl.pallas_call(
        pack_kernel,
        out_shape=jax.ShapeDtypeStruct((SOURCES, 4 * READ_ROWS, LANES), jnp.float32),
        in_specs=[VMEM, VMEM, SMEM, SMEM],
        out_specs=VMEM,
        name="pack",
    )(visibility, weights, positions, station_pairs)


def make_images(half, facet_shift, arrived):
    slot = [
        pltpu.VMEM((FACETS * HALF, CHUNK), jnp.bfloat16),
        pltpu.VMEM((FACETS * HALF, CHUNK), jnp.bfloat16),
        pltpu.VMEM((HALF, CHUNK), jnp.bfloat16),
        pltpu.VMEM((HALF, CHUNK), jnp.bfloat16),
    ]
    return pl.pallas_call(
        image_kernel,
        out_shape=jax.ShapeDtypeStruct((HALF, FACETS * PIX), jnp.bfloat16),
        in_specs=[SMEM, SMEM, VMEM],
        out_specs=VMEM,
        scratch_shapes=[
            pltpu.VMEM((TABLE, BLOCKS, LANES), jnp.float32),
            pltpu.VMEM((2, FACETS * HALF, HALF), jnp.float32),
            *slot,
            *slot,
        ],
        compiler_params=pltpu.CompilerParams(vmem_limit_bytes=40 * 1024 * 1024),
        name="images",
    )(half, facet_shift, arrived)


def combine(scale, parts):
    return pl.pallas_call(
        functools.partial(combine_kernel, scale),
        out_shape=jax.ShapeDtypeStruct((1, OUT_ROWS, FACETS * PIX), jnp.float32),
        in_specs=[VMEM],
        out_specs=VMEM,
        name="combine",
    )(parts)


def body(visibility, weights, positions, station_pairs, facet_shift):
    packed = pack(visibility, weights, positions, station_pairs)
    arrived = lax.all_to_all(packed, ("chan", "zh"), split_axis=0, concat_axis=0, tiled=True)
    half = lax.axis_index("zh").astype(jnp.int32).reshape(1)
    images = make_images(half, facet_shift, arrived)
    parts = lax.all_to_all(
        images.reshape(PEERS, OUT_ROWS, FACETS * PIX),
        ("y", "x"), split_axis=0, concat_axis=0, tiled=True,
    )
    scale = 1.0 / math.sqrt(READ_ROWS * GROUPS * 32 * LANES)
    return combine(scale, parts)


def solution(mesh):
    fine = Mesh(mesh.devices.reshape(GROUPS, 4, HALVES, 4), ("chan", "y", "zh", "x"))
    line = ("y", "zh", "x")
    in_specs = (
        P(None, ("chan", *line), None),
        P(("chan", *line), None),
        P(),
        P(None, ("chan", *line)),
        P(),
    )
    out_specs = P("chan", line, None)
    return jax.shard_map(body, mesh=fine, in_specs=in_specs, out_specs=out_specs, check_vma=False)
```

time: 544 us -> 52 us (0.10)
  the two profiles are of different devices: /device:TPU:32 before, /device:TPU:1 now
where the time goes in v1:
time: 52 us; the launch traced here: 51.6 us
  blocking collectives  17.2 us (33%)
  Pallas kernels  15.5 us (30%)
  starting transfers between devices  9.98 us (19%)
  waiting for transfers between devices  8.95 us (17%)
    all_to_all x1, blocking collectives, body(): lax.all_to_all(images.reshape(PEERS, OUT_ROWS, FACETS * PIX), ('y', 'x'),...  17.2 us
    pallas_call x1, Pallas kernels, make_images(): pl.pallas_call(image_kernel, out_shape=jax.ShapeDtypeStruct((HALF, FACETS...  12 us
    all_to_all x1, starting transfers between devices, body(): lax.all_to_all(packed, ('chan', 'zh'), split_axis=0, concat_axis=0, tiled...  9.98 us
    all_to_all x1, waiting for transfers between devices, body(): lax.all_to_all(packed, ('chan', 'zh'), split_axis=0, concat_axis=0, tiled...  8.95 us
    pallas_call x1, Pallas kernels, combine(): pl.pallas_call(functools.partial(combine_kernel, scale), out_shape=jax.Sh...  1.95 us
    pallas_call x1, Pallas kernels, pack(): pl.pallas_call(pack_kernel, out_shape=jax.ShapeDtypeStruct((SOURCES, 4 *...  1.57 us
  transfers between devices with their start and end apart: 1, of which 1 were waited for; matrix products, arithmetic and copies ran while one was open for 0% of the time, Pallas kernels for 0%

profile of v1, /device:TPU:1, one launch (start us, length us, event | category | flops | bytes accessed | tf_op | source)
XLA Modules:
  0.0 51.6 jit_solution(2626202593178779275)
XLA Ops:
  0.0 1.6 %pack.1 = f32[16,16,128]{2,1,0:T(8,128)} custom-call(bf16[2,4,1024]{2,1,0:T(4,128)(2,1)} %vis_ref.1, bf16[4,1024]{1,0:T(4,128)(2,1)} %weight_ref.1, f32[2,512]{1,0:T(2,128)} %pos_ref.1, s32[2,4]{1,0:T(2,128)} %pair_ref.1), custom_call_target="tpu_custom_call" | custom-call | tf_op jit(solution)/shard_map/pack/pallas_call | solution.py:225
  1.6 10.0 %all-to-all-start = ((f32[16,16,128]{2,1,0:T(8,128)}), f32[16,16,128]{2,1,0:T(8,128)S(1)}, u32[]{:S(2)}, u32[]{:S(2)}) async-start(f32[16,16,128]{2,1,0:T(8,128)} %pack.1), calls=%async_computation | async-start | bytes 262144 | tf_op jit(solution)/shard_map/all_to_all | solution.py:269
  11.6 0.0 copy-start
  11.6 8.9 %all-to-all-done.data_ref = f32[16,16,128]{2,1,0:T(8,128)S(1)} async-done(((f32[16,16,128]{2,1,0:T(8,128)}), f32[16,16,128]{2,1,0:T(8,128)S(1)}, u32[]{:S(2)}, u32[]{:S(2)}) %all-to-all-start) | async-done | bytes 131104 | tf_op jit(solution)/shard_map/all_to_all | solution.py:269
  20.5 0.0 copy-done
  20.5 12.0 %images.1 = bf16[256,1024]{1,0:T(8,128)(2,1)S(1)} custom-call(s32[1]{0:T(128)} %bitcast.half_ref, s32[2,2]{1,0:T(2,128)S(1)} %copy-done, f32[16,16,128]{2,1,0:T(8,128)S(1)} %all-to-all-done.data_ref), custom_call_target="tpu_custom_call" | custom-call | tf_op jit(solution)/shard_map/images/pallas_call | solution.py:241
  32.5 17.2 %all_to_all.10.data_ref = bf16[16,16,1024]{2,1,0:T(8,128)(2,1)} all-to-all(bf16[16,16,1024]{2,1,0:T(8,128)(2,1)S(1)} %bitcast.2), channel_id=1, replica_groups=mesh['chan'=8,'y'=4,'zh'=2,'x'=4] {'y','x'}, dimensions={0} | all-to-all | bytes 1048576 | tf_op jit(solution)/shard_map/all_to_all | solution.py:272
  49.7 1.9 %combine.1 = f32[1,16,1024]{2,1,0:T(8,128)} custom-call(bf16[16,16,1024]{2,1,0:T(8,128)(2,1)} %all_to_all.10.data_ref), custom_call_target="tpu_custom_call" | custom-call | tf_op jit(solution)/shard_map/combine/pallas_call | solution.py:258
Async XLA Ops:
  1.6 18.9 %all-to-all-start = ((f32[16,16,128]{2,1,0:T(8,128)}), f32[16,16,128]{2,1,0:T(8,128)S(1)}, u32[]{:S(2)}, u32[]{:S(2)}) async-start(f32[16,16,128]{2,1,0:T(8,128)} %pack.1), calls=%async_computation | async-start | bytes 262144 | tf_op jit(solution)/shard_map/all_to_all | solution.py:269
  11.6 9.0 %copy-start = (s32[2,2]{1,0:T(2,128)S(1)}, s32[2,2]{1,0:T(2,128)}, u32[]{:S(2)}) copy-start(s32[2,2]{1,0:T(2,128)} %shift_ref.1) | copy-start | bytes 52

commit v2 on v1

--- a/solution.py
+++ b/solution.py
@@ -18,10 +18,11 @@
 RUN_ROWS = 64
 RUNS = 4
 STEPS = RUN_ROWS // 8
+RUN_HALF = RUN_ROWS // 2
 HALVES = 2
 SOURCES = GROUPS * HALVES
 BLOCKS = SOURCES * READ_ROWS
-CHUNK_BLOCKS = 8
+CHUNK_BLOCKS = 4
 CHUNK = CHUNK_BLOCKS * LANES
 CHUNKS = BLOCKS // CHUNK_BLOCKS
 PEERS = 16
@@ -78,32 +79,40 @@
                 out_ref[g * HALVES + h, a * READ_ROWS : (a + 1) * READ_ROWS, :] = part
 
 
-(V0R, V0I, V1R, V1I, EAST, NORTH, C8E, S8E, C128E, S128E, C8N, S8N, C64N, S64N, TABLE) = range(15)
+PHASED = 0
+EAST, NORTH, C8E, S8E, C8N, S8N, C64N, S64N, TABLE = range(2 * FACETS * RUNS, 2 * FACETS * RUNS + 9)
+
+
+def rotate(u, turn):
+    (ur, ui), (c, s) = u, turn
+    return ur * c - ui * s, ur * s + ui * c
 
 
 def image_kernel(half_ref, shift_ref, data_ref, out_ref, table, acc, *slots):
     for s in range(SOURCES):
-        for a, t in enumerate((V0R, V0I, EAST, NORTH)):
+        for a, t in enumerate((PHASED, PHASED + 1, EAST, NORTH)):
             table[t, s * READ_ROWS : (s + 1) * READ_ROWS, :] = data_ref[
                 s, a * READ_ROWS : (a + 1) * READ_ROWS, :
             ]
-    base_row = half_ref[0] * RUN_ROWS - HALF
+    base_row = (half_ref[0] * RUN_ROWS - HALF).astype(jnp.float32) + (RUN_HALF - 0.5)
 
     def prepare(i, carry):
         rows = pl.ds(pl.multiple_of(i * 8, 8), 8)
         east = table[EAST, rows, :]
         north = table[NORTH, rows, :]
-        real = table[V0R, rows, :]
-        imag = table[V0I, rows, :]
+        seen = table[PHASED, rows, :], table[PHASED + 1, rows, :]
+        next_run = cos_sin(east * (2.0 * RUN_ROWS / PIX))
         for f in range(FACETS):
-            left = (shift_ref[0, f] + base_row).astype(jnp.float32) * (1.0 / PIX)
+            left = (shift_ref[0, f].astype(jnp.float32) + base_row) * (1.0 / PIX)
             right = (shift_ref[1, f].astype(jnp.float32) - 0.5) * (1.0 / PIX)
-            cos, sin = cos_sin(frac(east * left) + frac(north * right))
-            table[V0R + 2 * f, rows, :] = real * cos - imag * sin
-            table[V0I + 2 * f, rows, :] = real * sin + imag * cos
+            phased = rotate(seen, cos_sin(frac(east * left) + frac(north * right)))
+            for r in range(RUNS):
+                if r:
+                    phased = rotate(phased, next_run)
+                at = PHASED + 2 * (f * RUNS + r)
+                table[at, rows, :], table[at + 1, rows, :] = phased
         for t, turns in (
             (C8E, east * (8.0 / PIX)),
-            (C128E, east * (128.0 / PIX)),
             (C8N, north * (8.0 / PIX)),
             (C64N, north * (64.0 / PIX)),
         ):
@@ -114,14 +123,11 @@
 
     lax.fori_loop(0, BLOCKS // 8, prepare, 0)
 
-    lane_row = lax.broadcasted_iota(jnp.int32, (8, LANES), 0).astype(jnp.float32)
-
-    def rotate(u, turn):
-        (ur, ui), (c, s) = u, turn
-        return ur * c - ui * s, ur * s + ui * c
+    offsets = lax.broadcasted_iota(jnp.int32, (8, LANES), 0).astype(jnp.float32) + 0.5
+    offsets = offsets * (1.0 / PIX)
 
     def generate(first_block, slot):
-        left_re, left_im, right_re, right_im = slot
+        left_cos, left_sin, right_cos, right_sin = slot
         for t in range(CHUNK_BLOCKS):
             block = first_block + t
             lanes = slice(t * LANES, (t + 1) * LANES)
@@ -129,46 +135,56 @@
             def row(i):
                 return jnp.broadcast_to(table[i, pl.ds(block, 1), :], (8, LANES))
 
-            def emit(refs, first_row, stride, start, turn_run, turn_step):
-                anchors = [(start, rotate(start, turn_step))]
-                anchors.append(tuple(rotate(u, turn_run) for u in anchors[0]))
-                twice_run = 2.0 * turn_run[0]
-                for _ in range(RUNS - 2):
-                    anchors.append(
-                        tuple(
-                            tuple(twice_run * b - a for a, b in zip(old, new))
-                            for old, new in zip(anchors[-2], anchors[-1])
-                        )
+            def put(ref, at, first, second):
+                ref[at : at + 16, lanes] = jnp.concatenate([first, second], axis=0).astype(
+                    jnp.bfloat16
+                )
+
+            base = cos_sin(row(EAST) * offsets)
+            turn = (row(C8E), row(S8E))
+            wave = [base, rotate(base, turn)]
+            twice = 2.0 * turn[0]
+            for _ in range(2, RUN_HALF // 8):
+                wave.append(tuple(twice * b - a for a, b in zip(wave[-2], wave[-1])))
+            for f in range(FACETS):
+                for r in range(RUNS):
+                    index = PHASED + 2 * (f * RUNS + r)
+                    real, imag = row(index), row(index + 1)
+                    at = (f * RUNS + r) * RUN_HALF
+                    for j in range(0, RUN_HALF // 8, 2):
+                        (c0, s0), (c1, s1) = wave[j], wave[j + 1]
+                        put(left_cos, at + j * 8, real * c0, real * c1)
+                        put(left_cos, at + HALF + j * 8, imag * s0, imag * s1)
+                        put(left_sin, at + j * 8, real * s0, real * s1)
+                        put(left_sin, at + HALF + j * 8, imag * c0, imag * c1)
+
+            start = cos_sin(row(NORTH) * offsets)
+            turn = (row(C8N), row(S8N))
+            next_run = (row(C64N), row(S64N))
+            anchors = [(start, rotate(start, turn))]
+            anchors.append(tuple(rotate(u, next_run) for u in anchors[0]))
+            twice = 2.0 * next_run[0]
+            for _ in range(2, RUNS):
+                anchors.append(
+                    tuple(
+                        tuple(twice * b - a for a, b in zip(old, new))
+                        for old, new in zip(anchors[-2], anchors[-1])
                     )
-                twice = 2.0 * turn_step[0]
-                for r, (first, second) in enumerate(anchors):
-                    for part, ref in enumerate(refs):
-                        before, now = first[part], second[part]
-                        for j in range(0, STEPS, 2):
-                            if j:
-                                before = twice * now - before
-                                now = twice * before - now
-                            at = first_row + r * stride + j * 8
-                            ref[at : at + 16, lanes] = jnp.concatenate(
-                                [before, now], axis=0
-                            ).astype(jnp.bfloat16)
-
-            base = cos_sin(row(EAST) * (lane_row * (1.0 / PIX)))
-            turn_run = (row(C128E), row(S128E))
-            turn_step = (row(C8E), row(S8E))
-            for f in range(FACETS):
-                start = rotate(base, (row(V0R + 2 * f), row(V0I + 2 * f)))
-                emit((left_re, left_im), f * HALF, RUN_ROWS, start, turn_run, turn_step)
-            start = cos_sin(row(NORTH) * ((lane_row + 0.5) * (1.0 / PIX)))
-            emit(
-                (right_re, right_im), 0, RUN_ROWS, start,
-                (row(C64N), row(S64N)), (row(C8N), row(S8N)),
-            )
+                )
+            twice = 2.0 * turn[0]
+            for r, (first, second) in enumerate(anchors):
+                for part, ref in enumerate((right_cos, right_sin)):
+                    before, now = first[part], second[part]
+                    for j in range(0, STEPS, 2):
+                        if j:
+                            before = twice * now - before
+                            now = twice * before - now
+                        put(ref, r * RUN_ROWS + j * 8, before, now)
 
     def multiply(slot):
-        left_re, left_im, right_re, right_im = slot
+        left_cos, left_sin, right_cos, right_sin = slot
         contract = (((1,), (1,)), ((), ()))
-        for i, (left, right) in enumerate(((left_re, right_re), (left_im, right_im))):
+        for i, (left, right) in enumerate(((left_cos, right_cos), (left_sin, right_sin))):
             acc[i] += lax.dot_general(
                 left[...], right[...], contract, preferred_element_type=jnp.float32
             )
@@ -187,18 +203,26 @@
 
     lax.fori_loop(0, CHUNKS // 2, step, 0)
     for f in range(FACETS):
-        for i in range(2):
-            column = (f * 2 + i) * HALF
-            out_ref[:, column : column + HALF] = acc[i, f * HALF : (f + 1) * HALF].astype(
-                jnp.bfloat16
-            )
-
-
-def combine_kernel(scale, data_ref, out_ref):
-    total = data_ref[0].astype(jnp.float32)
-    for i in range(1, PEERS):
-        total = total + data_ref[i].astype(jnp.float32)
-    total = total * scale
+        for r in range(RUNS):
+            at = (f * RUNS + r) * RUN_HALF
+            for i in range(2):
+                column = (f * 2 + i) * HALF
+                for k in range(RUN_HALF // OUT_ROWS):
+                    rows = slice(at + k * OUT_ROWS, at + (k + 1) * OUT_ROWS)
+                    rows_imag = slice(at + HALF + k * OUT_ROWS, at + HALF + (k + 1) * OUT_ROWS)
+                    a, b = acc[i, rows], acc[i, rows_imag]
+                    below, above = (a - b, a + b) if i == 0 else (b + a, b - a)
+                    for place, values in ((2 + k, below), (1 - k, above)):
+                        out_ref[r * 4 + place, :, column : column + HALF] = values.astype(jnp.bfloat16)
+
+
+def combine_kernel(scale, place_ref, data_ref, out_ref):
+    shape = (OUT_ROWS, PEERS * OUT_ROWS)
+    out_row = lax.broadcasted_iota(jnp.int32, shape, 0)
+    sent_row = lax.broadcasted_iota(jnp.int32, shape, 1) % OUT_ROWS
+    wanted = jnp.where(place_ref[0] < 2, OUT_ROWS - 1 - out_row, out_row)
+    pick = (sent_row == wanted).astype(jnp.bfloat16)
+    total = jnp.dot(pick, data_ref[...], preferred_element_type=jnp.float32) * scale
     flip = (
         lax.broadcasted_iota(jnp.int32, (HALF, HALF), 0)
         + lax.broadcasted_iota(jnp.int32, (HALF, HALF), 1)
@@ -240,7 +264,7 @@
     ]
     return pl.pallas_call(
         image_kernel,
-        out_shape=jax.ShapeDtypeStruct((HALF, FACETS * PIX), jnp.bfloat16),
+        out_shape=jax.ShapeDtypeStruct((PEERS, OUT_ROWS, FACETS * PIX), jnp.bfloat16),
         in_specs=[SMEM, SMEM, VMEM],
         out_specs=VMEM,
         scratch_shapes=[
@@ -254,14 +278,14 @@
     )(half, facet_shift, arrived)
 
 
-def combine(scale, parts):
+def combine(scale, place, parts):
     return pl.pallas_call(
         functools.partial(combine_kernel, scale),
         out_shape=jax.ShapeDtypeStruct((1, OUT_ROWS, FACETS * PIX), jnp.float32),
-        in_specs=[VMEM],
+        in_specs=[SMEM, VMEM],
         out_specs=VMEM,
         name="combine",
-    )(parts)
+    )(place, parts.reshape(PEERS * OUT_ROWS, FACETS * PIX))
 
 
 def body(visibility, weights, positions, station_pairs, facet_shift):
@@ -270,11 +294,11 @@
     half = lax.axis_index("zh").astype(jnp.int32).reshape(1)
     images = make_images(half, facet_shift, arrived)
     parts = lax.all_to_all(
-        images.reshape(PEERS, OUT_ROWS, FACETS * PIX),
-        ("y", "x"), split_axis=0, concat_axis=0, tiled=True,
+        images, ("y", "x"), split_axis=0, concat_axis=0, tiled=True
     )
     scale = 1.0 / math.sqrt(READ_ROWS * GROUPS * 32 * LANES)
-    return combine(scale, parts)
+    place = lax.axis_index("x").astype(jnp.int32).reshape(1)
+    return combine(scale, place, parts)
 
 
 def solution(mesh):

time: 52 us -> 51.2 us (0.985)
  blocking collectives: 17.2 us -> 0 us
  waiting for transfers between devices: 8.95 us -> 19.5 us
  starting transfers between devices: 9.98 us -> 16.7 us
  Pallas kernels: 15.5 us -> 13.8 us
  local copies, waits for them, and re-layouts: 0.01 us -> 0.79 us
    all_to_all x1 -> x0, blocking collectives: 17.2 us -> none  [body(): lax.all_to_all(images.reshape(PEERS, OUT_ROWS, FACETS * PIX), ('y', 'x'),...]
    all_to_all x0 -> x1, waiting for transfers between devices: none -> 10.5 us  [body(): lax.all_to_all(images, ('y', 'x'), split_axis=0, concat_axis=0, tiled=True)]
    all_to_all x0 -> x1, starting transfers between devices: none -> 6.74 us  [body(): lax.all_to_all(images, ('y', 'x'), split_axis=0, concat_axis=0, tiled=True)]
    pallas_call x1, Pallas kernels: 12 us -> 10.2 us  [make_images(): pl.pallas_call(image_kernel, out_shape=jax.ShapeDtypeStruct((PEERS, OUT_R...]
    unnamed x2 -> x4, local copies, waits for them, and re-layouts: 0.01 us -> 0.79 us
  transfers between devices with their start and end apart: 1 -> 2, of which waited for: 1 -> 2; matrix products, arithmetic and copies ran while one was open for 0% -> 0% of each run, Pallas kernels for 0% -> 0%
where the time goes in v2:
time: 51.2 us; the launch traced here: 50.8 us
  waiting for transfers between devices  19.5 us (38%)
  starting transfers between devices  16.7 us (33%)
  Pallas kernels  13.8 us (27%)
  local copies, waits for them, and re-layouts  0.79 us (2%)
    all_to_all x1, waiting for transfers between devices, body(): lax.all_to_all(images, ('y', 'x'), split_axis=0, concat_axis=0, tiled=True)  10.5 us
    pallas_call x1, Pallas kernels, make_images(): pl.pallas_call(image_kernel, out_shape=jax.ShapeDtypeStruct((PEERS, OUT_R...  10.2 us
    all_to_all x1, starting transfers between devices, body(): lax.all_to_all(packed, ('chan', 'zh'), split_axis=0, concat_axis=0, tiled...  9.98 us
    all_to_all x1, waiting for transfers between devices, body(): lax.all_to_all(packed, ('chan', 'zh'), split_axis=0, concat_axis=0, tiled...  8.95 us
    all_to_all x1, starting transfers between devices, body(): lax.all_to_all(images, ('y', 'x'), split_axis=0, concat_axis=0, tiled=True)  6.74 us
    pallas_call x1, Pallas kernels, combine(): pl.pallas_call(functools.partial(combine_kernel, scale), out_shape=jax.Sh...  2.04 us
    pallas_call x1, Pallas kernels, pack(): pl.pallas_call(pack_kernel, out_shape=jax.ShapeDtypeStruct((SOURCES, 4 *...  1.57 us
  transfers between devices with their start and end apart: 2, of which 2 were waited for; matrix products, arithmetic and copies ran while one was open for 0% of the time, Pallas kernels for 0%

profile of v2, /device:TPU:1, one launch (start us, length us, event | category | flops | bytes accessed | tf_op | source)
XLA Modules:
  0.0 50.8 jit_solution(2296930552432851133)
XLA Ops:
  0.0 1.6 %pack.1 = f32[16,16,128]{2,1,0:T(8,128)} custom-call(bf16[2,4,1024]{2,1,0:T(4,128)(2,1)} %vis_ref.1, bf16[4,1024]{1,0:T(4,128)(2,1)} %weight_ref.1, f32[2,512]{1,0:T(2,128)} %pos_ref.1, s32[2,4]{1,0:T(2,128)} %pair_ref.1), custom_call_target="tpu_custom_call" | custom-call | tf_op jit(solution)/shard_map/pack/pallas_call | solution.py:249
  1.6 10.0 %all-to-all-start = ((f32[16,16,128]{2,1,0:T(8,128)}), f32[16,16,128]{2,1,0:T(8,128)S(1)}, u32[]{:S(2)}, u32[]{:S(2)}) async-start(f32[16,16,128]{2,1,0:T(8,128)} %pack.1), calls=%async_computation | async-start | bytes 262144 | tf_op jit(solution)/shard_map/all_to_all | solution.py:293
  11.6 0.0 copy-start
  11.6 8.9 %all-to-all-done.data_ref = f32[16,16,128]{2,1,0:T(8,128)S(1)} async-done(((f32[16,16,128]{2,1,0:T(8,128)}), f32[16,16,128]{2,1,0:T(8,128)S(1)}, u32[]{:S(2)}, u32[]{:S(2)}) %all-to-all-start) | async-done | bytes 131104 | tf_op jit(solution)/shard_map/all_to_all | solution.py:293
  20.5 0.0 copy-done
  20.5 10.2 %images.1 = bf16[16,16,1024]{2,1,0:T(8,128)(2,1)} custom-call(s32[1]{0:T(128)} %bitcast.1.half_ref, s32[2,2]{1,0:T(2,128)S(1)} %copy-done, f32[16,16,128]{2,1,0:T(8,128)S(1)} %all-to-all-done.data_ref), custom_call_target="tpu_custom_call" | custom-call | tf_op jit(solution)/shard_map/images/pallas_call | solution.py:265
  30.7 6.7 %all-to-all-start.1 = ((bf16[16,16,1024]{2,1,0:T(8,128)(2,1)}), bf16[16,16,1024]{2,1,0:T(8,128)(2,1)S(1)}, u32[]{:S(2)}, u32[]{:S(2)}) async-start(bf16[16,16,1024]{2,1,0:T(8,128)(2,1)} %images.1), calls=%async_computation.1 | async-start | bytes 1048576 | tf_op jit(solution)/shard_map/all_to_all | solution.py:296
  37.5 10.5 %all-to-all-done.1 = bf16[16,16,1024]{2,1,0:T(8,128)(2,1)S(1)} async-done(((bf16[16,16,1024]{2,1,0:T(8,128)(2,1)}), bf16[16,16,1024]{2,1,0:T(8,128)(2,1)S(1)}, u32[]{:S(2)}, u32[]{:S(2)}) %all-to-all-start.1) | async-done | bytes 524320 | tf_op jit(solution)/shard_map/all_to_all | solution.py:296
  48.0 0.0 copy-start.1
  48.0 0.8 %copy-done.1 = bf16[16,16,1024]{2,1,0:T(8,128)(2,1)} copy-done((bf16[16,16,1024]{2,1,0:T(8,128)(2,1)}, bf16[16,16,1024]{2,1,0:T(8,128)(2,1)S(1)}, u32[]{:S(2)}) %copy-start.1) | copy-done | bytes 524312
  48.8 2.0 %combine.1 = f32[1,16,1024]{2,1,0:T(8,128)} custom-call(s32[1]{0:T(128)} %bitcast.place_ref, bf16[256,1024]{1,0:T(8,128)(2,1)} %bitcast.3), custom_call_target="tpu_custom_call" | custom-call | tf_op jit(solution)/shard_map/combine/pallas_call | solution.py:282
Async XLA Ops:
  1.6 18.9 %all-to-all-start = ((f32[16,16,128]{2,1,0:T(8,128)}), f32[16,16,128]{2,1,0:T(8,128)S(1)}, u32[]{:S(2)}, u32[]{:S(2)}) async-start(f32[16,16,128]{2,1,0:T(8,128)} %pack.1), calls=%async_computation | async-start | bytes 262144 | tf_op jit(solution)/shard_map/all_to_all | solution.py:293
  11.6 9.0 %copy-start = (s32[2,2]{1,0:T(2,128)S(1)}, s32[2,2]{1,0:T(2,128)}, u32[]{:S(2)}) copy-start(s32[2,2]{1,0:T(2,128)} %shift_ref.1) | copy-start | bytes 52
  30.7 17.3 %all-to-all-start.1 = ((bf16[16,16,1024]{2,1,0:T(8,128)(2,1)}), bf16[16,16,1024]{2,1,0:T(8,128)(2,1)S(1)}, u32[]{:S(2)}, u32[]{:S(2)}) async-start(bf16[16,16,1024]{2,1,0:T(8,128)(2,1)} %images.1), calls=%async_computation.1 | async-start | bytes 1048576 | tf_op jit(solution)/shard_map/all_to_all | solution.py:296
  48.0 0.8 %copy-start.1 = (bf16[16,16,1024]{2,1,0:T(8,128)(2,1)}, bf16[16,16,1024]{2,1,0:T(8,128)(2,1)S(1)}, u32[]{:S(2)}) copy-start(bf16[16,16,1024]{2,1,0:T(8,128)(2,1)S(1)} %all-to-all-done.1) | copy-start | bytes 1572868

commit v3 on v2

--- a/solution.py
+++ b/solution.py
@@ -121,7 +121,7 @@
             table[t + 1, rows, :] = sin
         return carry
 
-    lax.fori_loop(0, BLOCKS // 8, prepare, 0)
+    lax.fori_loop(0, BLOCKS // 8, prepare, 0, unroll=4)
 
     offsets = lax.broadcasted_iota(jnp.int32, (8, LANES), 0).astype(jnp.float32) + 0.5
     offsets = offsets * (1.0 / PIX)
@@ -222,23 +222,25 @@
     sent_row = lax.broadcasted_iota(jnp.int32, shape, 1) % OUT_ROWS
     wanted = jnp.where(place_ref[0] < 2, OUT_ROWS - 1 - out_row, out_row)
     pick = (sent_row == wanted).astype(jnp.bfloat16)
-    total = jnp.dot(pick, data_ref[...], preferred_element_type=jnp.float32) * scale
+    total = jnp.dot(pick, data_ref[...].reshape(PEERS * OUT_ROWS, FACETS * PIX), preferred_element_type=jnp.float32) * scale
     flip = (
         lax.broadcasted_iota(jnp.int32, (HALF, HALF), 0)
         + lax.broadcasted_iota(jnp.int32, (HALF, HALF), 1)
         == HALF - 1
     ).astype(jnp.bfloat16)
+    evens = [total[:, f * PIX : f * PIX + HALF] for f in range(FACETS)]
+    odds = [total[:, f * PIX + HALF : (f + 1) * PIX] for f in range(FACETS)]
+    rest = jnp.concatenate([even + odd for even, odd in zip(evens, odds)], axis=0)
+    pieces = []
+    for _ in range(3):
+        pieces.append(rest.astype(jnp.bfloat16))
+        rest = rest - pieces[-1].astype(jnp.float32)
+    turned = jnp.dot(jnp.concatenate(pieces, axis=0), flip, preferred_element_type=jnp.float32)
+    rows = FACETS * OUT_ROWS
+    mirrored = turned[:rows] + turned[rows : 2 * rows] + turned[2 * rows :]
     for f in range(FACETS):
-        even = total[:, f * PIX : f * PIX + HALF]
-        odd = total[:, f * PIX + HALF : (f + 1) * PIX]
-        rest = even + odd
-        mirrored = jnp.zeros_like(rest)
-        for _ in range(3):
-            part = rest.astype(jnp.bfloat16)
-            rest = rest - part.astype(jnp.float32)
-            mirrored = mirrored + jnp.dot(part, flip, preferred_element_type=jnp.float32)
-        out_ref[0, :, f * PIX : f * PIX + HALF] = mirrored
-        out_ref[0, :, f * PIX + HALF : (f + 1) * PIX] = even - odd
+        out_ref[0, :, f * PIX : f * PIX + HALF] = mirrored[f * OUT_ROWS : (f + 1) * OUT_ROWS]
+        out_ref[0, :, f * PIX + HALF : (f + 1) * PIX] = evens[f] - odds[f]
 
 
 VMEM = pl.BlockSpec(memory_space=pltpu.VMEM)
@@ -284,20 +286,21 @@
         out_shape=jax.ShapeDtypeStruct((1, OUT_ROWS, FACETS * PIX), jnp.float32),
         in_specs=[SMEM, VMEM],
         out_specs=VMEM,
+        compiler_params=pltpu.CompilerParams(vmem_limit_bytes=8 * 1024 * 1024),
         name="combine",
-    )(place, parts.reshape(PEERS * OUT_ROWS, FACETS * PIX))
+    )(place, parts)
 
 
 def body(visibility, weights, positions, station_pairs, facet_shift):
+    half = lax.axis_index("zh").astype(jnp.int32).reshape(1)
+    place = lax.axis_index("x").astype(jnp.int32).reshape(1)
     packed = pack(visibility, weights, positions, station_pairs)
     arrived = lax.all_to_all(packed, ("chan", "zh"), split_axis=0, concat_axis=0, tiled=True)
-    half = lax.axis_index("zh").astype(jnp.int32).reshape(1)
     images = make_images(half, facet_shift, arrived)
     parts = lax.all_to_all(
         images, ("y", "x"), split_axis=0, concat_axis=0, tiled=True
     )
     scale = 1.0 / math.sqrt(READ_ROWS * GROUPS * 32 * LANES)
-    place = lax.axis_index("x").astype(jnp.int32).reshape(1)
     return combine(scale, place, parts)
 
 

time: 51.2 us -> 49.3 us (0.963)
  Pallas kernels: 13.8 us -> 12.7 us
  local copies, waits for them, and re-layouts: 0.79 us -> 0.01 us
    pallas_call x1, Pallas kernels: 2.04 us -> 0.99 us  [combine(): pl.pallas_call(functools.partial(combine_kernel, scale), out_shape=jax.Sh...]
    unnamed x4 -> x2, local copies, waits for them, and re-layouts: 0.79 us -> 0.01 us
where the time goes in v3:
time: 49.3 us; the launch traced here: 49 us
  waiting for transfers between devices  19.5 us (40%)
  starting transfers between devices  16.7 us (34%)
  Pallas kernels  12.7 us (26%)
    all_to_all x1, waiting for transfers between devices, body(): lax.all_to_all(images, ('y', 'x'), split_axis=0, concat_axis=0, tiled=True)  10.5 us
    pallas_call x1, Pallas kernels, make_images(): pl.pallas_call(image_kernel, out_shape=jax.ShapeDtypeStruct((PEERS, OUT_R...  10.2 us
    all_to_all x1, starting transfers between devices, body(): lax.all_to_all(packed, ('chan', 'zh'), split_axis=0, concat_axis=0, tiled...  9.98 us
    all_to_all x1, waiting for transfers between devices, body(): lax.all_to_all(packed, ('chan', 'zh'), split_axis=0, concat_axis=0, tiled...  8.95 us
    all_to_all x1, starting transfers between devices, body(): lax.all_to_all(images, ('y', 'x'), split_axis=0, concat_axis=0, tiled=True)  6.75 us
    pallas_call x1, Pallas kernels, pack(): pl.pallas_call(pack_kernel, out_shape=jax.ShapeDtypeStruct((SOURCES, 4 *...  1.57 us
    pallas_call x1, Pallas kernels, combine(): pl.pallas_call(functools.partial(combine_kernel, scale), out_shape=jax.Sh...  0.99 us
  transfers between devices with their start and end apart: 2, of which 2 were waited for; matrix products, arithmetic and copies ran while one was open for 0% of the time, Pallas kernels for 0%

profile of v3, /device:TPU:1, one launch (start us, length us, event | category | flops | bytes accessed | tf_op | source)
XLA Modules:
  0.0 49.0 jit_solution(4885344204023623913)
XLA Ops:
  0.0 1.6 %pack.1 = f32[16,16,128]{2,1,0:T(8,128)} custom-call(bf16[2,4,1024]{2,1,0:T(4,128)(2,1)} %vis_ref.1, bf16[4,1024]{1,0:T(4,128)(2,1)} %weight_ref.1, f32[2,512]{1,0:T(2,128)} %pos_ref.1, s32[2,4]{1,0:T(2,128)} %pair_ref.1), custom_call_target="tpu_custom_call" | custom-call | tf_op jit(solution)/shard_map/pack/pallas_call | solution.py:251
  1.6 10.0 %all-to-all-start = ((f32[16,16,128]{2,1,0:T(8,128)}), f32[16,16,128]{2,1,0:T(8,128)S(1)}, u32[]{:S(2)}, u32[]{:S(2)}) async-start(f32[16,16,128]{2,1,0:T(8,128)} %pack.1), calls=%async_computation | async-start | bytes 262144 | tf_op jit(solution)/shard_map/all_to_all | solution.py:298
  11.6 0.0 copy-start
  11.6 8.9 %all-to-all-done.data_ref = f32[16,16,128]{2,1,0:T(8,128)S(1)} async-done(((f32[16,16,128]{2,1,0:T(8,128)}), f32[16,16,128]{2,1,0:T(8,128)S(1)}, u32[]{:S(2)}, u32[]{:S(2)}) %all-to-all-start) | async-done | bytes 131104 | tf_op jit(solution)/shard_map/all_to_all | solution.py:298
  20.5 0.0 copy-done
  20.5 10.2 %images.1 = bf16[16,16,1024]{2,1,0:T(8,128)(2,1)} custom-call(s32[1]{0:T(128)} %bitcast.1.half_ref, s32[2,2]{1,0:T(2,128)S(1)} %copy-done, f32[16,16,128]{2,1,0:T(8,128)S(1)} %all-to-all-done.data_ref), custom_call_target="tpu_custom_call" | custom-call | tf_op jit(solution)/shard_map/images/pallas_call | solution.py:267
  30.7 6.8 %all-to-all-start.1 = ((bf16[16,16,1024]{2,1,0:T(8,128)(2,1)}), bf16[16,16,1024]{2,1,0:T(8,128)(2,1)S(1)}, u32[]{:S(2)}, u32[]{:S(2)}) async-start(bf16[16,16,1024]{2,1,0:T(8,128)(2,1)} %images.1), calls=%async_computation.1 | async-start | bytes 1048576 | tf_op jit(solution)/shard_map/all_to_all | solution.py:300
  37.5 10.5 %all-to-all-done.1.data_ref = bf16[16,16,1024]{2,1,0:T(8,128)(2,1)S(1)} async-done(((bf16[16,16,1024]{2,1,0:T(8,128)(2,1)}), bf16[16,16,1024]{2,1,0:T(8,128)(2,1)S(1)}, u32[]{:S(2)}, u32[]{:S(2)}) %all-to-all-start.1) | async-done | bytes 524320 | tf_op jit(solution)/shard_map/all_to_all | solution.py:300
  48.0 1.0 %combine.1 = f32[1,16,1024]{2,1,0:T(8,128)} custom-call(s32[1]{0:T(128)} %bitcast.place_ref, bf16[16,16,1024]{2,1,0:T(8,128)(2,1)S(1)} %all-to-all-done.1.data_ref), custom_call_target="tpu_custom_call" | custom-call | tf_op jit(solution)/shard_map/combine/pallas_call | solution.py:284
Async XLA Ops:
  1.6 18.9 %all-to-all-start = ((f32[16,16,128]{2,1,0:T(8,128)}), f32[16,16,128]{2,1,0:T(8,128)S(1)}, u32[]{:S(2)}, u32[]{:S(2)}) async-start(f32[16,16,128]{2,1,0:T(8,128)} %pack.1), calls=%async_computation | async-start | bytes 262144 | tf_op jit(solution)/shard_map/all_to_all | solution.py:298
  11.6 9.0 %copy-start = (s32[2,2]{1,0:T(2,128)S(1)}, s32[2,2]{1,0:T(2,128)}, u32[]{:S(2)}) copy-start(s32[2,2]{1,0:T(2,128)} %shift_ref.1) | copy-start | bytes 52
  30.7 17.3 %all-to-all-start.1 = ((bf16[16,16,1024]{2,1,0:T(8,128)(2,1)}), bf16[16,16,1024]{2,1,0:T(8,128)(2,1)S(1)}, u32[]{:S(2)}, u32[]{:S(2)}) async-start(bf16[16,16,1024]{2,1,0:T(8,128)(2,1)} %images.1), calls=%async_computation.1 | async-start | bytes 1048576 | tf_op jit(solution)/shard_map/all_to_all | solution.py:300

commit v4 on v3

--- a/solution.py
+++ b/solution.py
@@ -20,8 +20,7 @@
 STEPS = RUN_ROWS // 8
 RUN_HALF = RUN_ROWS // 2
 HALVES = 2
-SOURCES = GROUPS * HALVES
-BLOCKS = SOURCES * READ_ROWS
+BLOCKS = GROUPS * READ_ROWS
 CHUNK_BLOCKS = 4
 CHUNK = CHUNK_BLOCKS * LANES
 CHUNKS = BLOCKS // CHUNK_BLOCKS
@@ -75,8 +74,7 @@
     for a, values in enumerate((real, imag, *spans)):
         for g in range(GROUPS):
             part = values[:, g * LANES : (g + 1) * LANES]
-            for h in range(HALVES):
-                out_ref[g * HALVES + h, a * READ_ROWS : (a + 1) * READ_ROWS, :] = part
+            out_ref[g, a * READ_ROWS : (a + 1) * READ_ROWS, :] = part
 
 
 PHASED = 0
@@ -88,8 +86,34 @@
     return ur * c - ui * s, ur * s + ui * c
 
 
-def image_kernel(half_ref, shift_ref, data_ref, out_ref, table, acc, *slots):
-    for s in range(SOURCES):
+def first_kernel(half_ref, shift_ref, data_ref, acc, table, *slots):
+    add_rows(half_ref, shift_ref, data_ref, table, acc, slots)
+
+
+def last_kernel(
+    half_ref, shift_ref, data_ref, earlier_ref, out_ref, table, acc, earlier, arrived, *slots
+):
+    copy = pltpu.make_async_copy(earlier_ref, earlier, arrived)
+    copy.start()
+    add_rows(half_ref, shift_ref, data_ref, table, acc, slots)
+    copy.wait()
+    for f in range(FACETS):
+        for r in range(RUNS):
+            at = (f * RUNS + r) * RUN_HALF
+            for i in range(2):
+                column = (f * 2 + i) * HALF
+                for k in range(RUN_HALF // OUT_ROWS):
+                    rows = slice(at + k * OUT_ROWS, at + (k + 1) * OUT_ROWS)
+                    rows_imag = slice(at + HALF + k * OUT_ROWS, at + HALF + (k + 1) * OUT_ROWS)
+                    a = acc[i, rows] + earlier[i, rows]
+                    b = acc[i, rows_imag] + earlier[i, rows_imag]
+                    below, above = (a - b, a + b) if i == 0 else (b + a, b - a)
+                    for place, values in ((2 + k, below), (1 - k, above)):
+                        out_ref[r * 4 + place, :, column : column + HALF] = values.astype(jnp.bfloat16)
+
+
+def add_rows(half_ref, shift_ref, data_ref, table, acc, slots):
+    for s in range(GROUPS):
         for a, t in enumerate((PHASED, PHASED + 1, EAST, NORTH)):
             table[t, s * READ_ROWS : (s + 1) * READ_ROWS, :] = data_ref[
                 s, a * READ_ROWS : (a + 1) * READ_ROWS, :
@@ -202,18 +226,6 @@
         return carry
 
     lax.fori_loop(0, CHUNKS // 2, step, 0)
-    for f in range(FACETS):
-        for r in range(RUNS):
-            at = (f * RUNS + r) * RUN_HALF
-            for i in range(2):
-                column = (f * 2 + i) * HALF
-                for k in range(RUN_HALF // OUT_ROWS):
-                    rows = slice(at + k * OUT_ROWS, at + (k + 1) * OUT_ROWS)
-                    rows_imag = slice(at + HALF + k * OUT_ROWS, at + HALF + (k + 1) * OUT_ROWS)
-                    a, b = acc[i, rows], acc[i, rows_imag]
-                    below, above = (a - b, a + b) if i == 0 else (b + a, b - a)
-                    for place, values in ((2 + k, below), (1 - k, above)):
-                        out_ref[r * 4 + place, :, column : column + HALF] = values.astype(jnp.bfloat16)
 
 
 def combine_kernel(scale, place_ref, data_ref, out_ref):
@@ -250,34 +262,58 @@
 def pack(visibility, weights, positions, station_pairs):
     return pl.pallas_call(
         pack_kernel,
-        out_shape=jax.ShapeDtypeStruct((SOURCES, 4 * READ_ROWS, LANES), jnp.float32),
+        out_shape=jax.ShapeDtypeStruct((GROUPS, 4 * READ_ROWS, LANES), jnp.float32),
         in_specs=[VMEM, VMEM, SMEM, SMEM],
         out_specs=VMEM,
         name="pack",
     )(visibility, weights, positions, station_pairs)
 
 
-def make_images(half, facet_shift, arrived):
-    slot = [
-        pltpu.VMEM((FACETS * HALF, CHUNK), jnp.bfloat16),
-        pltpu.VMEM((FACETS * HALF, CHUNK), jnp.bfloat16),
-        pltpu.VMEM((HALF, CHUNK), jnp.bfloat16),
-        pltpu.VMEM((HALF, CHUNK), jnp.bfloat16),
-    ]
+SUMS = (2, FACETS * HALF, HALF)
+ROWS_COST = pl.CostEstimate(
+    flops=2 * math.prod(SUMS) * BLOCKS * LANES, bytes_accessed=4 * math.prod(SUMS), transcendentals=0
+)
+TABLE_SCRATCH = pltpu.VMEM((TABLE, BLOCKS, LANES), jnp.float32)
+SLOT = [
+    pltpu.VMEM((FACETS * HALF, CHUNK), jnp.bfloat16),
+    pltpu.VMEM((FACETS * HALF, CHUNK), jnp.bfloat16),
+    pltpu.VMEM((HALF, CHUNK), jnp.bfloat16),
+    pltpu.VMEM((HALF, CHUNK), jnp.bfloat16),
+]
+IMAGE_PARAMS = pltpu.CompilerParams(vmem_limit_bytes=24 * 1024 * 1024)
+
+
+def first_sums(half, facet_shift, arrived):
     return pl.pallas_call(
-        image_kernel,
-        out_shape=jax.ShapeDtypeStruct((PEERS, OUT_ROWS, FACETS * PIX), jnp.bfloat16),
+        first_kernel,
+        out_shape=jax.ShapeDtypeStruct(SUMS, jnp.float32),
         in_specs=[SMEM, SMEM, VMEM],
         out_specs=VMEM,
+        scratch_shapes=[TABLE_SCRATCH, *SLOT, *SLOT],
+        compiler_params=IMAGE_PARAMS,
+        cost_estimate=ROWS_COST,
+        name="first_sums",
+    )(half, facet_shift, arrived)
+
+
+def make_images(half, facet_shift, arrived, earlier):
+    return pl.pallas_call(
+        last_kernel,
+        out_shape=jax.ShapeDtypeStruct((PEERS, OUT_ROWS, FACETS * PIX), jnp.bfloat16),
+        in_specs=[SMEM, SMEM, VMEM, pl.BlockSpec(memory_space=pl.ANY)],
+        out_specs=VMEM,
         scratch_shapes=[
-            pltpu.VMEM((TABLE, BLOCKS, LANES), jnp.float32),
-            pltpu.VMEM((2, FACETS * HALF, HALF), jnp.float32),
-            *slot,
-            *slot,
+            TABLE_SCRATCH,
+            pltpu.VMEM(SUMS, jnp.float32),
+            pltpu.VMEM(SUMS, jnp.float32),
+            pltpu.SemaphoreType.DMA,
+            *SLOT,
+            *SLOT,
         ],
-        compiler_params=pltpu.CompilerParams(vmem_limit_bytes=40 * 1024 * 1024),
+        compiler_params=IMAGE_PARAMS,
+        cost_estimate=ROWS_COST,
         name="images",
-    )(half, facet_shift, arrived)
+    )(half, facet_shift, arrived, earlier)
 
 
 def combine(scale, place, parts):
@@ -295,8 +331,10 @@
     half = lax.axis_index("zh").astype(jnp.int32).reshape(1)
     place = lax.axis_index("x").astype(jnp.int32).reshape(1)
     packed = pack(visibility, weights, positions, station_pairs)
-    arrived = lax.all_to_all(packed, ("chan", "zh"), split_axis=0, concat_axis=0, tiled=True)
-    images = make_images(half, facet_shift, arrived)
+    own = lax.all_to_all(packed, "chan", split_axis=0, concat_axis=0, tiled=True)
+    other = lax.ppermute(own, "zh", [(h, HALVES - 1 - h) for h in range(HALVES)])
+    earlier = first_sums(half, facet_shift, own)
+    images = make_images(half, facet_shift, other, earlier)
     parts = lax.all_to_all(
         images, ("y", "x"), split_axis=0, concat_axis=0, tiled=True
     )

time: 49.3 us -> 47.9 us (0.972)
  waiting for transfers between devices: 19.5 us -> 15.3 us
  starting transfers between devices: 16.7 us -> 18.5 us
  Pallas kernels: 12.7 us -> 13.8 us
    ppermute x0 -> x1, starting transfers between devices: none -> 4.3 us  [body(): lax.ppermute(own, 'zh', [(h, HALVES - 1 - h) for h in range(HALVES)])]
    all_to_all x1, waiting for transfers between devices: 8.95 us -> 5.07 us  [body(): lax.all_to_all(packed, 'chan', split_axis=0, concat_axis=0, tiled=True)]
    all_to_all x1, starting transfers between devices: 9.98 us -> 7.4 us  [body(): lax.all_to_all(packed, 'chan', split_axis=0, concat_axis=0, tiled=True)]
    pallas_call x2 -> x3, Pallas kernels: 11.7 us -> 12.8 us  [the longest x1 6.09 us: make_images(): pl.pallas_call(last_kernel, out_shape=jax.ShapeDtypeStruct((PEERS, OUT_RO...]
  transfers between devices with their start and end apart: 2 -> 3, of which waited for: 2 -> 2; matrix products, arithmetic and copies ran while one was open for 0% -> 0% of each run, Pallas kernels for 0% -> 11%
where the time goes in v4:
time: 47.9 us; the launch traced here: 47.5 us
  starting transfers between devices  18.5 us (39%)
  waiting for transfers between devices  15.3 us (32%)
  Pallas kernels  13.8 us (29%)
    all_to_all x1, waiting for transfers between devices, body(): lax.all_to_all(images, ('y', 'x'), split_axis=0, concat_axis=0, tiled=True)  10.2 us
    all_to_all x1, starting transfers between devices, body(): lax.all_to_all(packed, 'chan', split_axis=0, concat_axis=0, tiled=True)  7.4 us
    all_to_all x1, starting transfers between devices, body(): lax.all_to_all(images, ('y', 'x'), split_axis=0, concat_axis=0, tiled=True)  6.76 us
    pallas_call x1, Pallas kernels, make_images(): pl.pallas_call(last_kernel, out_shape=jax.ShapeDtypeStruct((PEERS, OUT_RO...  6.09 us
    pallas_call x1, Pallas kernels, first_sums(): pl.pallas_call(first_kernel, out_shape=jax.ShapeDtypeStruct(SUMS, jnp.flo...  5.13 us
    all_to_all x1, waiting for transfers between devices, body(): lax.all_to_all(packed, 'chan', split_axis=0, concat_axis=0, tiled=True)  5.07 us
    ppermute x1, starting transfers between devices, body(): lax.ppermute(own, 'zh', [(h, HALVES - 1 - h) for h in range(HALVES)])  4.3 us
    pallas_call x1, Pallas kernels, pack(): pl.pallas_call(pack_kernel, out_shape=jax.ShapeDtypeStruct((GROUPS, 4 * R...  1.55 us
  transfers between devices with their start and end apart: 3, of which 2 were waited for; matrix products, arithmetic and copies ran while one was open for 0% of the time, Pallas kernels for 11%

profile of v4, /device:TPU:1, one launch (start us, length us, event | category | flops | bytes accessed | tf_op | source)
XLA Modules:
  0.0 47.5 jit_solution(7771139734099132662)
XLA Ops:
  0.0 1.5 %pack.1 = f32[8,16,128]{2,1,0:T(8,128)} custom-call(bf16[2,4,1024]{2,1,0:T(4,128)(2,1)} %vis_ref.1, bf16[4,1024]{1,0:T(4,128)(2,1)} %weight_ref.1, f32[2,512]{1,0:T(2,128)} %pos_ref.1, s32[2,4]{1,0:T(2,128)} %pair_ref.1), custom_call_target="tpu_custom_call" | custom-call | tf_op jit(solution)/shard_map/pack/pallas_call | solution.py:263
  1.6 7.4 %all-to-all-start = ((f32[8,16,128]{2,1,0:T(8,128)}), f32[8,16,128]{2,1,0:T(8,128)S(1)}, u32[]{:S(2)}, u32[]{:S(2)}) async-start(f32[8,16,128]{2,1,0:T(8,128)} %pack.1), calls=%async_computation | async-start | bytes 131072 | tf_op jit(solution)/shard_map/all_to_all | solution.py:334
  9.0 0.0 copy-start
  9.0 5.1 %all-to-all-done.data_ref = f32[8,16,128]{2,1,0:T(8,128)S(1)} async-done(((f32[8,16,128]{2,1,0:T(8,128)}), f32[8,16,128]{2,1,0:T(8,128)S(1)}, u32[]{:S(2)}, u32[]{:S(2)}) %all-to-all-start) | async-done | bytes 65568 | tf_op jit(solution)/shard_map/all_to_all | solution.py:334
  14.0 4.3 %collective-permute-start = (f32[8,16,128]{2,1,0:T(8,128)S(1)}, f32[8,16,128]{2,1,0:T(8,128)S(1)}, u32[]{:S(2)}, u32[]{:S(2)}) collective-permute-start(f32[8,16,128]{2,1,0:T(8,128)S(1)} %all-to-all-done.data_ref), channel_id=1, source_target_pairs={{0,4},{4,0},{1,5},{5,1},{2,6},{6,2},{3,7},{7,3},{8,12},{12,8},{9,1... | collective-permute-start | bytes 196616 | tf_op jit(solution)/shard_map/ppermute | solution.py:335
  18.3 0.0 copy-done
  18.3 5.1 %first_sums.1.earlier_ref = f32[2,512,256]{2,1,0:T(8,128)S(1)} custom-call(s32[1]{0:T(128)} %bitcast.1.half_ref, s32[2,2]{1,0:T(2,128)S(1)} %copy-done, f32[8,16,128]{2,1,0:T(8,128)S(1)} %all-to-all-done.data_ref), custom_call_target="tpu_custom_call" | custom-call | flops 2147483648 | bytes 1048576 | tf_op jit(solution)/shard_map/first_sums/pallas_call | solution.py:287
  23.5 0.0 collective-permute-done.data_ref
  23.5 6.1 %images.1 = bf16[16,16,1024]{2,1,0:T(8,128)(2,1)} custom-call(s32[1]{0:T(128)} %bitcast.1.half_ref, s32[2,2]{1,0:T(2,128)S(1)} %copy-done, f32[8,16,128]{2,1,0:T(8,128)S(1)} %collective-permute-done.data_ref, f32[2,512,256]{2,1,0:T(8,128)S(1)} %first_sums.1.earlier_ref), custom_call_target="tpu_custom_call" | custom-call | flops 2147483648 | bytes 1048576 | tf_op jit(solution)/shard_map/images/pallas_call | solution.py:300
  29.6 6.8 %all-to-all-start.1 = ((bf16[16,16,1024]{2,1,0:T(8,128)(2,1)}), bf16[16,16,1024]{2,1,0:T(8,128)(2,1)S(1)}, u32[]{:S(2)}, u32[]{:S(2)}) async-start(bf16[16,16,1024]{2,1,0:T(8,128)(2,1)} %images.1), calls=%async_computation.1 | async-start | bytes 1048576 | tf_op jit(solution)/shard_map/all_to_all | solution.py:338
  36.3 10.2 %all-to-all-done.1.data_ref = bf16[16,16,1024]{2,1,0:T(8,128)(2,1)S(1)} async-done(((bf16[16,16,1024]{2,1,0:T(8,128)(2,1)}), bf16[16,16,1024]{2,1,0:T(8,128)(2,1)S(1)}, u32[]{:S(2)}, u32[]{:S(2)}) %all-to-all-start.1) | async-done | bytes 524320 | tf_op jit(solution)/shard_map/all_to_all | solution.py:338
  46.6 1.0 %combine.1 = f32[1,16,1024]{2,1,0:T(8,128)} custom-call(s32[1]{0:T(128)} %bitcast.place_ref, bf16[16,16,1024]{2,1,0:T(8,128)(2,1)S(1)} %all-to-all-done.1.data_ref), custom_call_target="tpu_custom_call" | custom-call | tf_op jit(solution)/shard_map/combine/pallas_call | solution.py:320
Async XLA Ops:
  1.6 12.5 %all-to-all-start = ((f32[8,16,128]{2,1,0:T(8,128)}), f32[8,16,128]{2,1,0:T(8,128)S(1)}, u32[]{:S(2)}, u32[]{:S(2)}) async-start(f32[8,16,128]{2,1,0:T(8,128)} %pack.1), calls=%async_computation | async-start | bytes 131072 | tf_op jit(solution)/shard_map/all_to_all | solution.py:334
  9.0 9.4 %copy-start = (s32[2,2]{1,0:T(2,128)S(1)}, s32[2,2]{1,0:T(2,128)}, u32[]{:S(2)}) copy-start(s32[2,2]{1,0:T(2,128)} %shift_ref.3) | copy-start | bytes 52
  14.0 9.4 %collective-permute-start = (f32[8,16,128]{2,1,0:T(8,128)S(1)}, f32[8,16,128]{2,1,0:T(8,128)S(1)}, u32[]{:S(2)}, u32[]{:S(2)}) collective-permute-start(f32[8,16,128]{2,1,0:T(8,128)S(1)} %all-to-all-done.data_ref), channel_id=1, source_target_pairs={{0,4},{4,0},{1,5},{5,1},{2,6},{6,2},{3,7},{7,3},{8,12},{12,8},{9,1... | collective-permute-start | bytes 196616 | tf_op jit(solution)/shard_map/ppermute | solution.py:335
  29.6 17.0 %all-to-all-start.1 = ((bf16[16,16,1024]{2,1,0:T(8,128)(2,1)}), bf16[16,16,1024]{2,1,0:T(8,128)(2,1)S(1)}, u32[]{:S(2)}, u32[]{:S(2)}) async-start(bf16[16,16,1024]{2,1,0:T(8,128)(2,1)} %images.1), calls=%async_computation.1 | async-start | bytes 1048576 | tf_op jit(solution)/shard_map/all_to_all | solution.py:338

commit v5 on v4

--- a/solution.py
+++ b/solution.py
@@ -21,9 +21,6 @@
 RUN_HALF = RUN_ROWS // 2
 HALVES = 2
 BLOCKS = GROUPS * READ_ROWS
-CHUNK_BLOCKS = 4
-CHUNK = CHUNK_BLOCKS * LANES
-CHUNKS = BLOCKS // CHUNK_BLOCKS
 PEERS = 16
 OUT_ROWS = 16
 COS_COEF = (
@@ -86,17 +83,16 @@
     return ur * c - ui * s, ur * s + ui * c
 
 
-def first_kernel(half_ref, shift_ref, data_ref, acc, table, *slots):
-    add_rows(half_ref, shift_ref, data_ref, table, acc, slots)
+def first_kernel(half_ref, shift_ref, data_ref, out_ref, table, *panels):
+    for i, sums in enumerate(image_sums(half_ref, shift_ref, data_ref, table, panels)):
+        out_ref[i] = sums
 
 
 def last_kernel(
-    half_ref, shift_ref, data_ref, earlier_ref, out_ref, table, acc, earlier, arrived, *slots
+    half_ref, shift_ref, data_ref, earlier_ref, out_ref, table, acc, *panels
 ):
-    copy = pltpu.make_async_copy(earlier_ref, earlier, arrived)
-    copy.start()
-    add_rows(half_ref, shift_ref, data_ref, table, acc, slots)
-    copy.wait()
+    for i, sums in enumerate(image_sums(half_ref, shift_ref, data_ref, table, panels)):
+        acc[i] = sums + earlier_ref[i]
     for f in range(FACETS):
         for r in range(RUNS):
             at = (f * RUNS + r) * RUN_HALF
@@ -105,14 +101,13 @@
                 for k in range(RUN_HALF // OUT_ROWS):
                     rows = slice(at + k * OUT_ROWS, at + (k + 1) * OUT_ROWS)
                     rows_imag = slice(at + HALF + k * OUT_ROWS, at + HALF + (k + 1) * OUT_ROWS)
-                    a = acc[i, rows] + earlier[i, rows]
-                    b = acc[i, rows_imag] + earlier[i, rows_imag]
+                    a, b = acc[i, rows], acc[i, rows_imag]
                     below, above = (a - b, a + b) if i == 0 else (b + a, b - a)
                     for place, values in ((2 + k, below), (1 - k, above)):
                         out_ref[r * 4 + place, :, column : column + HALF] = values.astype(jnp.bfloat16)
 
 
-def add_rows(half_ref, shift_ref, data_ref, table, acc, slots):
+def image_sums(half_ref, shift_ref, data_ref, table, panels):
     for s in range(GROUPS):
         for a, t in enumerate((PHASED, PHASED + 1, EAST, NORTH)):
             table[t, s * READ_ROWS : (s + 1) * READ_ROWS, :] = data_ref[
@@ -120,8 +115,8 @@
             ]
     base_row = (half_ref[0] * RUN_ROWS - HALF).astype(jnp.float32) + (RUN_HALF - 0.5)
 
-    def prepare(i, carry):
-        rows = pl.ds(pl.multiple_of(i * 8, 8), 8)
+    for i in range(BLOCKS // 8):
+        rows = slice(i * 8, (i + 1) * 8)
         east = table[EAST, rows, :]
         north = table[NORTH, rows, :]
         seen = table[PHASED, rows, :], table[PHASED + 1, rows, :]
@@ -143,89 +138,66 @@
             cos, sin = cos_sin(turns)
             table[t, rows, :] = cos
             table[t + 1, rows, :] = sin
-        return carry
-
-    lax.fori_loop(0, BLOCKS // 8, prepare, 0, unroll=4)
 
     offsets = lax.broadcasted_iota(jnp.int32, (8, LANES), 0).astype(jnp.float32) + 0.5
     offsets = offsets * (1.0 / PIX)
 
-    def generate(first_block, slot):
-        left_cos, left_sin, right_cos, right_sin = slot
-        for t in range(CHUNK_BLOCKS):
-            block = first_block + t
-            lanes = slice(t * LANES, (t + 1) * LANES)
-
-            def row(i):
-                return jnp.broadcast_to(table[i, pl.ds(block, 1), :], (8, LANES))
-
-            def put(ref, at, first, second):
-                ref[at : at + 16, lanes] = jnp.concatenate([first, second], axis=0).astype(
-                    jnp.bfloat16
+    panels = [panels[i : i + 4] for i in range(0, len(panels), 4)]
+    for block, (left_cos, left_sin, right_cos, right_sin) in enumerate(panels):
+
+        def row(i):
+            return jnp.broadcast_to(table[i, block : block + 1, :], (8, LANES))
+
+        def put(ref, at, first, second):
+            ref[at : at + 16, :] = jnp.concatenate([first, second], axis=0).astype(jnp.bfloat16)
+
+        base = cos_sin(row(EAST) * offsets)
+        turn = (row(C8E), row(S8E))
+        wave = [base, rotate(base, turn)]
+        twice = 2.0 * turn[0]
+        for _ in range(2, RUN_HALF // 8):
+            wave.append(tuple(twice * b - a for a, b in zip(wave[-2], wave[-1])))
+        for f in range(FACETS):
+            for r in range(RUNS):
+                index = PHASED + 2 * (f * RUNS + r)
+                real, imag = row(index), row(index + 1)
+                at = (f * RUNS + r) * RUN_HALF
+                for j in range(0, RUN_HALF // 8, 2):
+                    (c0, s0), (c1, s1) = wave[j], wave[j + 1]
+                    put(left_cos, at + j * 8, real * c0, real * c1)
+                    put(left_cos, at + HALF + j * 8, imag * s0, imag * s1)
+                    put(left_sin, at + j * 8, real * s0, real * s1)
+                    put(left_sin, at + HALF + j * 8, imag * c0, imag * c1)
+
+        start = cos_sin(row(NORTH) * offsets)
+        turn = (row(C8N), row(S8N))
+        next_run = (row(C64N), row(S64N))
+        anchors = [(start, rotate(start, turn))]
+        anchors.append(tuple(rotate(u, next_run) for u in anchors[0]))
+        twice = 2.0 * next_run[0]
+        for _ in range(2, RUNS):
+            anchors.append(
+                tuple(
+                    tuple(twice * b - a for a, b in zip(old, new))
+                    for old, new in zip(anchors[-2], anchors[-1])
                 )
-
-            base = cos_sin(row(EAST) * offsets)
-            turn = (row(C8E), row(S8E))
-            wave = [base, rotate(base, turn)]
-            twice = 2.0 * turn[0]
-            for _ in range(2, RUN_HALF // 8):
-                wave.append(tuple(twice * b - a for a, b in zip(wave[-2], wave[-1])))
-            for f in range(FACETS):
-                for r in range(RUNS):
-                    index = PHASED + 2 * (f * RUNS + r)
-                    real, imag = row(index), row(index + 1)
-                    at = (f * RUNS + r) * RUN_HALF
-                    for j in range(0, RUN_HALF // 8, 2):
-                        (c0, s0), (c1, s1) = wave[j], wave[j + 1]
-                        put(left_cos, at + j * 8, real * c0, real * c1)
-                        put(left_cos, at + HALF + j * 8, imag * s0, imag * s1)
-                        put(left_sin, at + j * 8, real * s0, real * s1)
-                        put(left_sin, at + HALF + j * 8, imag * c0, imag * c1)
-
-            start = cos_sin(row(NORTH) * offsets)
-            turn = (row(C8N), row(S8N))
-            next_run = (row(C64N), row(S64N))
-            anchors = [(start, rotate(start, turn))]
-            anchors.append(tuple(rotate(u, next_run) for u in anchors[0]))
-            twice = 2.0 * next_run[0]
-            for _ in range(2, RUNS):
-                anchors.append(
-                    tuple(
-                        tuple(twice * b - a for a, b in zip(old, new))
-                        for old, new in zip(anchors[-2], anchors[-1])
-                    )
-                )
-            twice = 2.0 * turn[0]
-            for r, (first, second) in enumerate(anchors):
-                for part, ref in enumerate((right_cos, right_sin)):
-                    before, now = first[part], second[part]
-                    for j in range(0, STEPS, 2):
-                        if j:
-                            before = twice * now - before
-                            now = twice * before - now
-                        put(ref, r * RUN_ROWS + j * 8, before, now)
-
-    def multiply(slot):
-        left_cos, left_sin, right_cos, right_sin = slot
-        contract = (((1,), (1,)), ((), ()))
-        for i, (left, right) in enumerate(((left_cos, right_cos), (left_sin, right_sin))):
-            acc[i] += lax.dot_general(
-                left[...], right[...], contract, preferred_element_type=jnp.float32
             )
-
-    slot_a, slot_b = slots[:4], slots[4:]
-    acc[...] = jnp.zeros_like(acc)
-    generate(0, slot_a)
-
-    def step(i, carry):
-        first = i * (2 * CHUNK_BLOCKS)
-        generate(first + CHUNK_BLOCKS, slot_b)
-        multiply(slot_a)
-        generate(lax.rem(first + 2 * CHUNK_BLOCKS, BLOCKS), slot_a)
-        multiply(slot_b)
-        return carry
-
-    lax.fori_loop(0, CHUNKS // 2, step, 0)
+        twice = 2.0 * turn[0]
+        for r, (first, second) in enumerate(anchors):
+            for part, ref in enumerate((right_cos, right_sin)):
+                before, now = first[part], second[part]
+                for j in range(0, STEPS, 2):
+                    if j:
+                        before = twice * now - before
+                        now = twice * before - now
+                    put(ref, r * RUN_ROWS + j * 8, before, now)
+
+    left_cos, left_sin, right_cos, right_sin = (
+        jnp.concatenate([ref[...] for ref in refs], axis=1) for refs in zip(*panels)
+    )
+    contract = (((1,), (1,)), ((), ()))
+    for left, right in ((left_cos, right_cos), (left_sin, right_sin)):
+        yield lax.dot_general(left, right, contract, preferred_element_type=jnp.float32)
 
 
 def combine_kernel(scale, place_ref, data_ref, out_ref):
@@ -274,13 +246,13 @@
     flops=2 * math.prod(SUMS) * BLOCKS * LANES, bytes_accessed=4 * math.prod(SUMS), transcendentals=0
 )
 TABLE_SCRATCH = pltpu.VMEM((TABLE, BLOCKS, LANES), jnp.float32)
-SLOT = [
-    pltpu.VMEM((FACETS * HALF, CHUNK), jnp.bfloat16),
-    pltpu.VMEM((FACETS * HALF, CHUNK), jnp.bfloat16),
-    pltpu.VMEM((HALF, CHUNK), jnp.bfloat16),
-    pltpu.VMEM((HALF, CHUNK), jnp.bfloat16),
-]
-IMAGE_PARAMS = pltpu.CompilerParams(vmem_limit_bytes=24 * 1024 * 1024)
+PANELS = [
+    pltpu.VMEM((FACETS * HALF, LANES), jnp.bfloat16),
+    pltpu.VMEM((FACETS * HALF, LANES), jnp.bfloat16),
+    pltpu.VMEM((HALF, LANES), jnp.bfloat16),
+    pltpu.VMEM((HALF, LANES), jnp.bfloat16),
+] * BLOCKS
+IMAGE_PARAMS = pltpu.CompilerParams(vmem_limit_bytes=32 * 1024 * 1024)
 
 
 def first_sums(half, facet_shift, arrived):
@@ -289,7 +261,7 @@
         out_shape=jax.ShapeDtypeStruct(SUMS, jnp.float32),
         in_specs=[SMEM, SMEM, VMEM],
         out_specs=VMEM,
-        scratch_shapes=[TABLE_SCRATCH, *SLOT, *SLOT],
+        scratch_shapes=[TABLE_SCRATCH, *PANELS],
         compiler_params=IMAGE_PARAMS,
         cost_estimate=ROWS_COST,
         name="first_sums",
@@ -300,15 +272,12 @@
     return pl.pallas_call(
         last_kernel,
         out_shape=jax.ShapeDtypeStruct((PEERS, OUT_ROWS, FACETS * PIX), jnp.bfloat16),
-        in_specs=[SMEM, SMEM, VMEM, pl.BlockSpec(memory_space=pl.ANY)],
+        in_specs=[SMEM, SMEM, VMEM, VMEM],
         out_specs=VMEM,
         scratch_shapes=[
             TABLE_SCRATCH,
             pltpu.VMEM(SUMS, jnp.float32),
-            pltpu.VMEM(SUMS, jnp.float32),
-            pltpu.SemaphoreType.DMA,
-            *SLOT,
-            *SLOT,
+            *PANELS,
         ],
         compiler_params=IMAGE_PARAMS,
         cost_estimate=ROWS_COST,

time: 47.9 us -> 45.4 us (0.948); the launches traced: 47.5 us -> 44.6 us
  Pallas kernels: 13.8 us -> 10.8 us
    pallas_call x1, Pallas kernels: 6.09 us -> 4.54 us  [make_images(): pl.pallas_call(last_kernel, out_shape=jax.ShapeDtypeStruct((PEERS, OUT_RO...]
    pallas_call x1, Pallas kernels: 5.13 us -> 3.72 us  [first_sums(): pl.pallas_call(first_kernel, out_shape=jax.ShapeDtypeStruct(SUMS, jnp.flo...]
  transfers between devices with their start and end apart: 3 -> 3, of which waited for: 2 -> 2; matrix products, arithmetic and copies ran while one was open for 0% -> 0% of each run, Pallas kernels for 11% -> 8%
where the time goes in v5:
time: 45.4 us; the launch traced here: 44.6 us
  starting transfers between devices  18.5 us (41%)
  waiting for transfers between devices  15.3 us (34%)
  Pallas kernels  10.8 us (24%)
    all_to_all x1, waiting for transfers between devices, body(): lax.all_to_all(images, ('y', 'x'), split_axis=0, concat_axis=0, tiled=True)  10.2 us
    all_to_all x1, starting transfers between devices, body(): lax.all_to_all(packed, 'chan', split_axis=0, concat_axis=0, tiled=True)  7.4 us
    all_to_all x1, starting transfers between devices, body(): lax.all_to_all(images, ('y', 'x'), split_axis=0, concat_axis=0, tiled=True)  6.75 us
    all_to_all x1, waiting for transfers between devices, body(): lax.all_to_all(packed, 'chan', split_axis=0, concat_axis=0, tiled=True)  5.07 us
    pallas_call x1, Pallas kernels, make_images(): pl.pallas_call(last_kernel, out_shape=jax.ShapeDtypeStruct((PEERS, OUT_RO...  4.54 us
    ppermute x1, starting transfers between devices, body(): lax.ppermute(own, 'zh', [(h, HALVES - 1 - h) for h in range(HALVES)])  4.3 us
    pallas_call x1, Pallas kernels, first_sums(): pl.pallas_call(first_kernel, out_shape=jax.ShapeDtypeStruct(SUMS, jnp.flo...  3.72 us
    pallas_call x1, Pallas kernels, pack(): pl.pallas_call(pack_kernel, out_shape=jax.ShapeDtypeStruct((GROUPS, 4 * R...  1.55 us
  transfers between devices with their start and end apart: 3, of which 2 were waited for; matrix products, arithmetic and copies ran while one was open for 0% of the time, Pallas kernels for 8%

profile of v5, /device:TPU:1, one launch (start us, length us, event | category | flops | bytes accessed | tf_op | source)
XLA Modules:
  0.0 44.6 jit_solution(504893310861463637)
XLA Ops:
  0.0 1.5 %pack.1 = f32[8,16,128]{2,1,0:T(8,128)} custom-call(bf16[2,4,1024]{2,1,0:T(4,128)(2,1)} %vis_ref.1, bf16[4,1024]{1,0:T(4,128)(2,1)} %weight_ref.1, f32[2,512]{1,0:T(2,128)} %pos_ref.1, s32[2,4]{1,0:T(2,128)} %pair_ref.1), custom_call_target="tpu_custom_call" | custom-call | tf_op jit(solution)/shard_map/pack/pallas_call | solution.py:235
  1.6 7.4 %all-to-all-start = ((f32[8,16,128]{2,1,0:T(8,128)}), f32[8,16,128]{2,1,0:T(8,128)S(1)}, u32[]{:S(2)}, u32[]{:S(2)}) async-start(f32[8,16,128]{2,1,0:T(8,128)} %pack.1), calls=%async_computation | async-start | bytes 131072 | tf_op jit(solution)/shard_map/all_to_all | solution.py:303
  9.0 0.0 copy-start
  9.0 5.1 %all-to-all-done.data_ref = f32[8,16,128]{2,1,0:T(8,128)S(1)} async-done(((f32[8,16,128]{2,1,0:T(8,128)}), f32[8,16,128]{2,1,0:T(8,128)S(1)}, u32[]{:S(2)}, u32[]{:S(2)}) %all-to-all-start) | async-done | bytes 65568 | tf_op jit(solution)/shard_map/all_to_all | solution.py:303
  14.0 4.3 %collective-permute-start = (f32[8,16,128]{2,1,0:T(8,128)S(1)}, f32[8,16,128]{2,1,0:T(8,128)S(1)}, u32[]{:S(2)}, u32[]{:S(2)}) collective-permute-start(f32[8,16,128]{2,1,0:T(8,128)S(1)} %all-to-all-done.data_ref), channel_id=1, source_target_pairs={{0,4},{4,0},{1,5},{5,1},{2,6},{6,2},{3,7},{7,3},{8,12},{12,8},{9,1... | collective-permute-start | bytes 196616 | tf_op jit(solution)/shard_map/ppermute | solution.py:304
  18.3 0.0 copy-done
  18.3 3.7 %first_sums.1.earlier_ref = f32[2,512,256]{2,1,0:T(8,128)S(1)} custom-call(s32[1]{0:T(128)} %bitcast.1.half_ref, s32[2,2]{1,0:T(2,128)S(1)} %copy-done, f32[8,16,128]{2,1,0:T(8,128)S(1)} %all-to-all-done.data_ref), custom_call_target="tpu_custom_call" | custom-call | flops 2147483648 | bytes 1048576 | tf_op jit(solution)/shard_map/first_sums/pallas_call | solution.py:259
  22.1 0.0 collective-permute-done.data_ref
  22.1 4.5 %images.1 = bf16[16,16,1024]{2,1,0:T(8,128)(2,1)} custom-call(s32[1]{0:T(128)} %bitcast.1.half_ref, s32[2,2]{1,0:T(2,128)S(1)} %copy-done, f32[8,16,128]{2,1,0:T(8,128)S(1)} %collective-permute-done.data_ref, f32[2,512,256]{2,1,0:T(8,128)S(1)} %first_sums.1.earlier_ref), custom_call_target="tpu_custom_call" | custom-call | flops 2147483648 | bytes 1048576 | tf_op jit(solution)/shard_map/images/pallas_call | solution.py:272
  26.6 6.8 %all-to-all-start.1 = ((bf16[16,16,1024]{2,1,0:T(8,128)(2,1)}), bf16[16,16,1024]{2,1,0:T(8,128)(2,1)S(1)}, u32[]{:S(2)}, u32[]{:S(2)}) async-start(bf16[16,16,1024]{2,1,0:T(8,128)(2,1)} %images.1), calls=%async_computation.1 | async-start | bytes 1048576 | tf_op jit(solution)/shard_map/all_to_all | solution.py:307
  33.4 10.2 %all-to-all-done.1.data_ref = bf16[16,16,1024]{2,1,0:T(8,128)(2,1)S(1)} async-done(((bf16[16,16,1024]{2,1,0:T(8,128)(2,1)}), bf16[16,16,1024]{2,1,0:T(8,128)(2,1)S(1)}, u32[]{:S(2)}, u32[]{:S(2)}) %all-to-all-start.1) | async-done | bytes 524320 | tf_op jit(solution)/shard_map/all_to_all | solution.py:307
  43.6 1.0 %combine.1 = f32[1,16,1024]{2,1,0:T(8,128)} custom-call(s32[1]{0:T(128)} %bitcast.place_ref, bf16[16,16,1024]{2,1,0:T(8,128)(2,1)S(1)} %all-to-all-done.1.data_ref), custom_call_target="tpu_custom_call" | custom-call | tf_op jit(solution)/shard_map/combine/pallas_call | solution.py:289
Async XLA Ops:
  1.6 12.5 %all-to-all-start = ((f32[8,16,128]{2,1,0:T(8,128)}), f32[8,16,128]{2,1,0:T(8,128)S(1)}, u32[]{:S(2)}, u32[]{:S(2)}) async-start(f32[8,16,128]{2,1,0:T(8,128)} %pack.1), calls=%async_computation | async-start | bytes 131072 | tf_op jit(solution)/shard_map/all_to_all | solution.py:303
  9.0 9.4 %copy-start = (s32[2,2]{1,0:T(2,128)S(1)}, s32[2,2]{1,0:T(2,128)}, u32[]{:S(2)}) copy-start(s32[2,2]{1,0:T(2,128)} %shift_ref.3) | copy-start | bytes 52
  14.0 8.0 %collective-permute-start = (f32[8,16,128]{2,1,0:T(8,128)S(1)}, f32[8,16,128]{2,1,0:T(8,128)S(1)}, u32[]{:S(2)}, u32[]{:S(2)}) collective-permute-start(f32[8,16,128]{2,1,0:T(8,128)S(1)} %all-to-all-done.data_ref), channel_id=1, source_target_pairs={{0,4},{4,0},{1,5},{5,1},{2,6},{6,2},{3,7},{7,3},{8,12},{12,8},{9,1... | collective-permute-start | bytes 196616 | tf_op jit(solution)/shard_map/ppermute | solution.py:304
  26.6 17.0 %all-to-all-start.1 = ((bf16[16,16,1024]{2,1,0:T(8,128)(2,1)}), bf16[16,16,1024]{2,1,0:T(8,128)(2,1)S(1)}, u32[]{:S(2)}, u32[]{:S(2)}) async-start(bf16[16,16,1024]{2,1,0:T(8,128)(2,1)} %images.1), calls=%async_computation.1 | async-start | bytes 1048576 | tf_op jit(solution)/shard_map/all_to_all | solution.py:307

commit v6 on v5

--- a/solution.py
+++ b/solution.py
@@ -83,15 +83,15 @@
     return ur * c - ui * s, ur * s + ui * c
 
 
-def first_kernel(half_ref, shift_ref, data_ref, out_ref, table, *panels):
-    for i, sums in enumerate(image_sums(half_ref, shift_ref, data_ref, table, panels)):
+def first_kernel(half_ref, shift_ref, data_ref, out_ref, table, starts, *panels):
+    for i, sums in enumerate(image_sums(half_ref, shift_ref, data_ref, table, starts, panels)):
         out_ref[i] = sums
 
 
 def last_kernel(
-    half_ref, shift_ref, data_ref, earlier_ref, out_ref, table, acc, *panels
+    half_ref, shift_ref, data_ref, earlier_ref, out_ref, table, starts, acc, *panels
 ):
-    for i, sums in enumerate(image_sums(half_ref, shift_ref, data_ref, table, panels)):
+    for i, sums in enumerate(image_sums(half_ref, shift_ref, data_ref, table, starts, panels)):
         acc[i] = sums + earlier_ref[i]
     for f in range(FACETS):
         for r in range(RUNS):
@@ -107,7 +107,7 @@
                         out_ref[r * 4 + place, :, column : column + HALF] = values.astype(jnp.bfloat16)
 
 
-def image_sums(half_ref, shift_ref, data_ref, table, panels):
+def image_sums(half_ref, shift_ref, data_ref, table, starts, panels):
     for s in range(GROUPS):
         for a, t in enumerate((PHASED, PHASED + 1, EAST, NORTH)):
             table[t, s * READ_ROWS : (s + 1) * READ_ROWS, :] = data_ref[
@@ -130,17 +130,19 @@
                     phased = rotate(phased, next_run)
                 at = PHASED + 2 * (f * RUNS + r)
                 table[at, rows, :], table[at + 1, rows, :] = phased
-        for t, turns in (
-            (C8E, east * (8.0 / PIX)),
-            (C8N, north * (8.0 / PIX)),
-            (C64N, north * (64.0 / PIX)),
-        ):
-            cos, sin = cos_sin(turns)
-            table[t, rows, :] = cos
-            table[t + 1, rows, :] = sin
-
-    offsets = lax.broadcasted_iota(jnp.int32, (8, LANES), 0).astype(jnp.float32) + 0.5
-    offsets = offsets * (1.0 / PIX)
+        table[C64N, rows, :], table[S64N, rows, :] = cos_sin(north * (64.0 / PIX))
+        for place, turns in enumerate((east, north)):
+            first = now = cos_sin(turns * (0.5 / PIX))
+            step = rotate(first, first)
+            twice = 2.0 * step[0]
+            before = now[0], -now[1]
+            for j in range(8):
+                if j:
+                    before, now = now, tuple(twice * b - a for a, b in zip(before, now))
+                for part in range(2):
+                    starts[place * 2 + part, pl.ds(i * 64 + j, 8, stride=8), :] = now[part]
+            t = (C8E, C8N)[place]
+            table[t, rows, :], table[t + 1, rows, :] = rotate(now, first)
 
     panels = [panels[i : i + 4] for i in range(0, len(panels), 4)]
     for block, (left_cos, left_sin, right_cos, right_sin) in enumerate(panels):
@@ -151,7 +153,8 @@
         def put(ref, at, first, second):
             ref[at : at + 16, :] = jnp.concatenate([first, second], axis=0).astype(jnp.bfloat16)
 
-        base = cos_sin(row(EAST) * offsets)
+        here = slice(block * 8, (block + 1) * 8)
+        base = starts[0, here, :], starts[1, here, :]
         turn = (row(C8E), row(S8E))
         wave = [base, rotate(base, turn)]
         twice = 2.0 * turn[0]
@@ -169,7 +172,7 @@
                     put(left_sin, at + j * 8, real * s0, real * s1)
                     put(left_sin, at + HALF + j * 8, imag * c0, imag * c1)
 
-        start = cos_sin(row(NORTH) * offsets)
+        start = starts[2, here, :], starts[3, here, :]
         turn = (row(C8N), row(S8N))
         next_run = (row(C64N), row(S64N))
         anchors = [(start, rotate(start, turn))]
@@ -246,6 +249,7 @@
     flops=2 * math.prod(SUMS) * BLOCKS * LANES, bytes_accessed=4 * math.prod(SUMS), transcendentals=0
 )
 TABLE_SCRATCH = pltpu.VMEM((TABLE, BLOCKS, LANES), jnp.float32)
+START_SCRATCH = pltpu.VMEM((4, BLOCKS * 8, LANES), jnp.float32)
 PANELS = [
     pltpu.VMEM((FACETS * HALF, LANES), jnp.bfloat16),
     pltpu.VMEM((FACETS * HALF, LANES), jnp.bfloat16),
@@ -261,7 +265,7 @@
         out_shape=jax.ShapeDtypeStruct(SUMS, jnp.float32),
         in_specs=[SMEM, SMEM, VMEM],
         out_specs=VMEM,
-        scratch_shapes=[TABLE_SCRATCH, *PANELS],
+        scratch_shapes=[TABLE_SCRATCH, START_SCRATCH, *PANELS],
         compiler_params=IMAGE_PARAMS,
         cost_estimate=ROWS_COST,
         name="first_sums",
@@ -276,6 +280,7 @@
         out_specs=VMEM,
         scratch_shapes=[
             TABLE_SCRATCH,
+            START_SCRATCH,
             pltpu.VMEM(SUMS, jnp.float32),
             *PANELS,
         ],

time: 45.4 us -> 44.9 us (0.989)
  the two profiles are of different devices: /device:TPU:1 before, /device:TPU:32 now
where the time goes in v6:
time: 44.9 us; the launch traced here: 44.6 us
  starting transfers between devices  17.6 us (39%)
  waiting for transfers between devices  17 us (38%)
  Pallas kernels  9.92 us (22%)
    all_to_all x1, waiting for transfers between devices, body(): lax.all_to_all(images, ('y', 'x'), split_axis=0, concat_axis=0, tiled=True)  11.2 us
    all_to_all x1, starting transfers between devices, body(): lax.all_to_all(images, ('y', 'x'), split_axis=0, concat_axis=0, tiled=True)  7.04 us
    all_to_all x1, starting transfers between devices, body(): lax.all_to_all(packed, 'chan', split_axis=0, concat_axis=0, tiled=True)  6.01 us
    all_to_all x1, waiting for transfers between devices, body(): lax.all_to_all(packed, 'chan', split_axis=0, concat_axis=0, tiled=True)  4.63 us
    ppermute x1, starting transfers between devices, body(): lax.ppermute(own, 'zh', [(h, HALVES - 1 - h) for h in range(HALVES)])  4.58 us
    pallas_call x1, Pallas kernels, make_images(): pl.pallas_call(last_kernel, out_shape=jax.ShapeDtypeStruct((PEERS, OUT_RO...  4.1 us
    pallas_call x1, Pallas kernels, first_sums(): pl.pallas_call(first_kernel, out_shape=jax.ShapeDtypeStruct(SUMS, jnp.flo...  3.28 us
    pallas_call x1, Pallas kernels, pack(): pl.pallas_call(pack_kernel, out_shape=jax.ShapeDtypeStruct((GROUPS, 4 * R...  1.55 us
  transfers between devices with their start and end apart: 3, of which 3 were waited for; matrix products, arithmetic and copies ran while one was open for 0% of the time, Pallas kernels for 7%

profile of v6, /device:TPU:32, one launch (start us, length us, event | category | flops | bytes accessed | tf_op | source)
XLA Modules:
  0.0 44.6 jit_solution(2893461086799364692)
XLA Ops:
  0.0 1.5 %pack.1 = f32[8,16,128]{2,1,0:T(8,128)} custom-call(bf16[2,4,1024]{2,1,0:T(4,128)(2,1)} %vis_ref.1, bf16[4,1024]{1,0:T(4,128)(2,1)} %weight_ref.1, f32[2,512]{1,0:T(2,128)} %pos_ref.1, s32[2,4]{1,0:T(2,128)} %pair_ref.1), custom_call_target="tpu_custom_call" | custom-call | tf_op jit(solution)/shard_map/pack/pallas_call | solution.py:238
  1.6 6.0 %all-to-all-start = ((f32[8,16,128]{2,1,0:T(8,128)}), f32[8,16,128]{2,1,0:T(8,128)S(1)}, u32[]{:S(2)}, u32[]{:S(2)}) async-start(f32[8,16,128]{2,1,0:T(8,128)} %pack.1), calls=%async_computation | async-start | bytes 131072 | tf_op jit(solution)/shard_map/all_to_all | solution.py:308
  7.6 0.0 copy-start
  7.6 4.6 %all-to-all-done.data_ref = f32[8,16,128]{2,1,0:T(8,128)S(1)} async-done(((f32[8,16,128]{2,1,0:T(8,128)}), f32[8,16,128]{2,1,0:T(8,128)S(1)}, u32[]{:S(2)}, u32[]{:S(2)}) %all-to-all-start) | async-done | bytes 65568 | tf_op jit(solution)/shard_map/all_to_all | solution.py:308
  12.2 4.6 %collective-permute-start = (f32[8,16,128]{2,1,0:T(8,128)S(1)}, f32[8,16,128]{2,1,0:T(8,128)S(1)}, u32[]{:S(2)}, u32[]{:S(2)}) collective-permute-start(f32[8,16,128]{2,1,0:T(8,128)S(1)} %all-to-all-done.data_ref), channel_id=1, source_target_pairs={{0,4},{4,0},{1,5},{5,1},{2,6},{6,2},{3,7},{7,3},{8,12},{12,8},{9,1... | collective-permute-start | bytes 196616 | tf_op jit(solution)/shard_map/ppermute | solution.py:309
  16.8 0.0 copy-done
  16.8 3.3 %first_sums.1.earlier_ref = f32[2,512,256]{2,1,0:T(8,128)S(1)} custom-call(s32[1]{0:T(128)} %bitcast.1.half_ref, s32[2,2]{1,0:T(2,128)S(1)} %copy-done, f32[8,16,128]{2,1,0:T(8,128)S(1)} %all-to-all-done.data_ref), custom_call_target="tpu_custom_call" | custom-call | flops 2147483648 | bytes 1048576 | tf_op jit(solution)/shard_map/first_sums/pallas_call | solution.py:263
  20.1 1.2 %collective-permute-done.data_ref = f32[8,16,128]{2,1,0:T(8,128)S(1)} collective-permute-done((f32[8,16,128]{2,1,0:T(8,128)S(1)}, f32[8,16,128]{2,1,0:T(8,128)S(1)}, u32[]{:S(2)}, u32[]{:S(2)}) %collective-permute-start) | collective-permute-done | bytes 65568 | tf_op jit(solution)/shard_map/ppermute | solution.py:309
  21.2 4.1 %images.1 = bf16[16,16,1024]{2,1,0:T(8,128)(2,1)} custom-call(s32[1]{0:T(128)} %bitcast.1.half_ref, s32[2,2]{1,0:T(2,128)S(1)} %copy-done, f32[8,16,128]{2,1,0:T(8,128)S(1)} %collective-permute-done.data_ref, f32[2,512,256]{2,1,0:T(8,128)S(1)} %first_sums.1.earlier_ref), custom_call_target="tpu_custom_call" | custom-call | flops 2147483648 | bytes 1048576 | tf_op jit(solution)/shard_map/images/pallas_call | solution.py:276
  25.3 7.0 %all-to-all-start.1 = ((bf16[16,16,1024]{2,1,0:T(8,128)(2,1)}), bf16[16,16,1024]{2,1,0:T(8,128)(2,1)S(1)}, u32[]{:S(2)}, u32[]{:S(2)}) async-start(bf16[16,16,1024]{2,1,0:T(8,128)(2,1)} %images.1), calls=%async_computation.1 | async-start | bytes 1048576 | tf_op jit(solution)/shard_map/all_to_all | solution.py:312
  32.4 11.2 %all-to-all-done.1.data_ref = bf16[16,16,1024]{2,1,0:T(8,128)(2,1)S(1)} async-done(((bf16[16,16,1024]{2,1,0:T(8,128)(2,1)}), bf16[16,16,1024]{2,1,0:T(8,128)(2,1)S(1)}, u32[]{:S(2)}, u32[]{:S(2)}) %all-to-all-start.1) | async-done | bytes 524320 | tf_op jit(solution)/shard_map/all_to_all | solution.py:312
  43.6 1.0 %combine.1 = f32[1,16,1024]{2,1,0:T(8,128)} custom-call(s32[1]{0:T(128)} %bitcast.place_ref, bf16[16,16,1024]{2,1,0:T(8,128)(2,1)S(1)} %all-to-all-done.1.data_ref), custom_call_target="tpu_custom_call" | custom-call | tf_op jit(solution)/shard_map/combine/pallas_call | solution.py:294
Async XLA Ops:
  1.6 10.6 %all-to-all-start = ((f32[8,16,128]{2,1,0:T(8,128)}), f32[8,16,128]{2,1,0:T(8,128)S(1)}, u32[]{:S(2)}, u32[]{:S(2)}) async-start(f32[8,16,128]{2,1,0:T(8,128)} %pack.1), calls=%async_computation | async-start | bytes 131072 | tf_op jit(solution)/shard_map/all_to_all | solution.py:308
  7.6 9.2 %copy-start = (s32[2,2]{1,0:T(2,128)S(1)}, s32[2,2]{1,0:T(2,128)}, u32[]{:S(2)}) copy-start(s32[2,2]{1,0:T(2,128)} %shift_ref.3) | copy-start | bytes 52
  12.2 9.0 %collective-permute-start = (f32[8,16,128]{2,1,0:T(8,128)S(1)}, f32[8,16,128]{2,1,0:T(8,128)S(1)}, u32[]{:S(2)}, u32[]{:S(2)}) collective-permute-start(f32[8,16,128]{2,1,0:T(8,128)S(1)} %all-to-all-done.data_ref), channel_id=1, source_target_pairs={{0,4},{4,0},{1,5},{5,1},{2,6},{6,2},{3,7},{7,3},{8,12},{12,8},{9,1... | collective-permute-start | bytes 196616 | tf_op jit(solution)/shard_map/ppermute | solution.py:309
  25.3 18.3 %all-to-all-start.1 = ((bf16[16,16,1024]{2,1,0:T(8,128)(2,1)}), bf16[16,16,1024]{2,1,0:T(8,128)(2,1)S(1)}, u32[]{:S(2)}, u32[]{:S(2)}) async-start(bf16[16,16,1024]{2,1,0:T(8,128)(2,1)} %images.1), calls=%async_computation.1 | async-start | bytes 1048576 | tf_op jit(solution)/shard_map/all_to_all | solution.py:312

commit v7 on v6

--- a/solution.py
+++ b/solution.py
@@ -20,7 +20,8 @@
 STEPS = RUN_ROWS // 8
 RUN_HALF = RUN_ROWS // 2
 HALVES = 2
-BLOCKS = GROUPS * READ_ROWS
+SOURCES = GROUPS * HALVES
+BLOCKS = SOURCES * READ_ROWS
 PEERS = 16
 OUT_ROWS = 16
 COS_COEF = (
@@ -71,7 +72,8 @@
     for a, values in enumerate((real, imag, *spans)):
         for g in range(GROUPS):
             part = values[:, g * LANES : (g + 1) * LANES]
-            out_ref[g, a * READ_ROWS : (a + 1) * READ_ROWS, :] = part
+            for h in range(HALVES):
+                out_ref[g * HALVES + h, a * READ_ROWS : (a + 1) * READ_ROWS, :] = part
 
 
 PHASED = 0
@@ -83,16 +85,9 @@
     return ur * c - ui * s, ur * s + ui * c
 
 
-def first_kernel(half_ref, shift_ref, data_ref, out_ref, table, starts, *panels):
+def image_kernel(half_ref, shift_ref, data_ref, out_ref, table, starts, acc, *panels):
     for i, sums in enumerate(image_sums(half_ref, shift_ref, data_ref, table, starts, panels)):
-        out_ref[i] = sums
-
-
-def last_kernel(
-    half_ref, shift_ref, data_ref, earlier_ref, out_ref, table, starts, acc, *panels
-):
-    for i, sums in enumerate(image_sums(half_ref, shift_ref, data_ref, table, starts, panels)):
-        acc[i] = sums + earlier_ref[i]
+        acc[i] = sums
     for f in range(FACETS):
         for r in range(RUNS):
             at = (f * RUNS + r) * RUN_HALF
@@ -108,7 +103,7 @@
 
 
 def image_sums(half_ref, shift_ref, data_ref, table, starts, panels):
-    for s in range(GROUPS):
+    for s in range(SOURCES):
         for a, t in enumerate((PHASED, PHASED + 1, EAST, NORTH)):
             table[t, s * READ_ROWS : (s + 1) * READ_ROWS, :] = data_ref[
                 s, a * READ_ROWS : (a + 1) * READ_ROWS, :
@@ -237,7 +232,7 @@
 def pack(visibility, weights, positions, station_pairs):
     return pl.pallas_call(
         pack_kernel,
-        out_shape=jax.ShapeDtypeStruct((GROUPS, 4 * READ_ROWS, LANES), jnp.float32),
+        out_shape=jax.ShapeDtypeStruct((SOURCES, 4 * READ_ROWS, LANES), jnp.float32),
         in_specs=[VMEM, VMEM, SMEM, SMEM],
         out_specs=VMEM,
         name="pack",
@@ -256,27 +251,14 @@
     pltpu.VMEM((HALF, LANES), jnp.bfloat16),
     pltpu.VMEM((HALF, LANES), jnp.bfloat16),
 ] * BLOCKS
-IMAGE_PARAMS = pltpu.CompilerParams(vmem_limit_bytes=32 * 1024 * 1024)
-
-
-def first_sums(half, facet_shift, arrived):
+IMAGE_PARAMS = pltpu.CompilerParams(vmem_limit_bytes=48 * 1024 * 1024)
+
+
+def make_images(half, facet_shift, arrived):
     return pl.pallas_call(
-        first_kernel,
-        out_shape=jax.ShapeDtypeStruct(SUMS, jnp.float32),
+        image_kernel,
+        out_shape=jax.ShapeDtypeStruct((PEERS, OUT_ROWS, FACETS * PIX), jnp.bfloat16),
         in_specs=[SMEM, SMEM, VMEM],
-        out_specs=VMEM,
-        scratch_shapes=[TABLE_SCRATCH, START_SCRATCH, *PANELS],
-        compiler_params=IMAGE_PARAMS,
-        cost_estimate=ROWS_COST,
-        name="first_sums",
-    )(half, facet_shift, arrived)
-
-
-def make_images(half, facet_shift, arrived, earlier):
-    return pl.pallas_call(
-        last_kernel,
-        out_shape=jax.ShapeDtypeStruct((PEERS, OUT_ROWS, FACETS * PIX), jnp.bfloat16),
-        in_specs=[SMEM, SMEM, VMEM, VMEM],
         out_specs=VMEM,
         scratch_shapes=[
             TABLE_SCRATCH,
@@ -287,7 +269,7 @@
         compiler_params=IMAGE_PARAMS,
         cost_estimate=ROWS_COST,
         name="images",
-    )(half, facet_shift, arrived, earlier)
+    )(half, facet_shift, arrived)
 
 
 def combine(scale, place, parts):
@@ -305,10 +287,8 @@
     half = lax.axis_index("zh").astype(jnp.int32).reshape(1)
     place = lax.axis_index("x").astype(jnp.int32).reshape(1)
     packed = pack(visibility, weights, positions, station_pairs)
-    own = lax.all_to_all(packed, "chan", split_axis=0, concat_axis=0, tiled=True)
-    other = lax.ppermute(own, "zh", [(h, HALVES - 1 - h) for h in range(HALVES)])
-    earlier = first_sums(half, facet_shift, own)
-    images = make_images(half, facet_shift, other, earlier)
+    arrived = lax.all_to_all(packed, ("chan", "zh"), split_axis=0, concat_axis=0, tiled=True)
+    images = make_images(half, facet_shift, arrived)
     parts = lax.all_to_all(
         images, ("y", "x"), split_axis=0, concat_axis=0, tiled=True
     )

time: 44.9 us -> 45.7 us (1.018)
  the two profiles are of different devices: /device:TPU:32 before, /device:TPU:1 now
where the time goes in v7:
time: 45.7 us; the launch traced here: 45.4 us
  waiting for transfers between devices  19.5 us (43%)
  starting transfers between devices  16.7 us (37%)
  Pallas kernels  9.15 us (20%)
    all_to_all x1, waiting for transfers between devices, body(): lax.all_to_all(images, ('y', 'x'), split_axis=0, concat_axis=0, tiled=True)  10.5 us
    all_to_all x1, starting transfers between devices, body(): lax.all_to_all(packed, ('chan', 'zh'), split_axis=0, concat_axis=0, tiled...  9.98 us
    all_to_all x1, waiting for transfers between devices, body(): lax.all_to_all(packed, ('chan', 'zh'), split_axis=0, concat_axis=0, tiled...  8.95 us
    all_to_all x1, starting transfers between devices, body(): lax.all_to_all(images, ('y', 'x'), split_axis=0, concat_axis=0, tiled=True)  6.75 us
    pallas_call x1, Pallas kernels, make_images(): pl.pallas_call(image_kernel, out_shape=jax.ShapeDtypeStruct((PEERS, OUT_R...  6.59 us
    pallas_call x1, Pallas kernels, pack(): pl.pallas_call(pack_kernel, out_shape=jax.ShapeDtypeStruct((SOURCES, 4 *...  1.57 us
    pallas_call x1, Pallas kernels, combine(): pl.pallas_call(functools.partial(combine_kernel, scale), out_shape=jax.Sh...  0.99 us
  transfers between devices with their start and end apart: 2, of which 2 were waited for; matrix products, arithmetic and copies ran while one was open for 0% of the time, Pallas kernels for 0%

profile of v7, /device:TPU:1, one launch (start us, length us, event | category | flops | bytes accessed | tf_op | source)
XLA Modules:
  0.0 45.4 jit_solution(17548945319128796681)
XLA Ops:
  0.0 1.6 %pack.1 = f32[16,16,128]{2,1,0:T(8,128)} custom-call(bf16[2,4,1024]{2,1,0:T(4,128)(2,1)} %vis_ref.1, bf16[4,1024]{1,0:T(4,128)(2,1)} %weight_ref.1, f32[2,512]{1,0:T(2,128)} %pos_ref.1, s32[2,4]{1,0:T(2,128)} %pair_ref.1), custom_call_target="tpu_custom_call" | custom-call | tf_op jit(solution)/shard_map/pack/pallas_call | solution.py:233
  1.6 10.0 %all-to-all-start = ((f32[16,16,128]{2,1,0:T(8,128)}), f32[16,16,128]{2,1,0:T(8,128)S(1)}, u32[]{:S(2)}, u32[]{:S(2)}) async-start(f32[16,16,128]{2,1,0:T(8,128)} %pack.1), calls=%async_computation | async-start | bytes 262144 | tf_op jit(solution)/shard_map/all_to_all | solution.py:290
  11.6 0.0 copy-start
  11.6 8.9 %all-to-all-done.data_ref = f32[16,16,128]{2,1,0:T(8,128)S(1)} async-done(((f32[16,16,128]{2,1,0:T(8,128)}), f32[16,16,128]{2,1,0:T(8,128)S(1)}, u32[]{:S(2)}, u32[]{:S(2)}) %all-to-all-start) | async-done | bytes 131104 | tf_op jit(solution)/shard_map/all_to_all | solution.py:290
  20.5 0.0 copy-done
  20.5 6.6 %images.1 = bf16[16,16,1024]{2,1,0:T(8,128)(2,1)} custom-call(s32[1]{0:T(128)} %bitcast.1.half_ref, s32[2,2]{1,0:T(2,128)S(1)} %copy-done, f32[16,16,128]{2,1,0:T(8,128)S(1)} %all-to-all-done.data_ref), custom_call_target="tpu_custom_call" | custom-call | flops 4294967296 | bytes 1048576 | tf_op jit(solution)/shard_map/images/pallas_call | solution.py:258
  27.1 6.8 %all-to-all-start.1 = ((bf16[16,16,1024]{2,1,0:T(8,128)(2,1)}), bf16[16,16,1024]{2,1,0:T(8,128)(2,1)S(1)}, u32[]{:S(2)}, u32[]{:S(2)}) async-start(bf16[16,16,1024]{2,1,0:T(8,128)(2,1)} %images.1), calls=%async_computation.1 | async-start | bytes 1048576 | tf_op jit(solution)/shard_map/all_to_all | solution.py:292
  33.9 10.5 %all-to-all-done.1.data_ref = bf16[16,16,1024]{2,1,0:T(8,128)(2,1)S(1)} async-done(((bf16[16,16,1024]{2,1,0:T(8,128)(2,1)}), bf16[16,16,1024]{2,1,0:T(8,128)(2,1)S(1)}, u32[]{:S(2)}, u32[]{:S(2)}) %all-to-all-start.1) | async-done | bytes 524320 | tf_op jit(solution)/shard_map/all_to_all | solution.py:292
  44.4 1.0 %combine.1 = f32[1,16,1024]{2,1,0:T(8,128)} custom-call(s32[1]{0:T(128)} %bitcast.place_ref, bf16[16,16,1024]{2,1,0:T(8,128)(2,1)S(1)} %all-to-all-done.1.data_ref), custom_call_target="tpu_custom_call" | custom-call | tf_op jit(solution)/shard_map/combine/pallas_call | solution.py:276
Async XLA Ops:
  1.6 18.9 %all-to-all-start = ((f32[16,16,128]{2,1,0:T(8,128)}), f32[16,16,128]{2,1,0:T(8,128)S(1)}, u32[]{:S(2)}, u32[]{:S(2)}) async-start(f32[16,16,128]{2,1,0:T(8,128)} %pack.1), calls=%async_computation | async-start | bytes 262144 | tf_op jit(solution)/shard_map/all_to_all | solution.py:290
  11.6 9.0 %copy-start = (s32[2,2]{1,0:T(2,128)S(1)}, s32[2,2]{1,0:T(2,128)}, u32[]{:S(2)}) copy-start(s32[2,2]{1,0:T(2,128)} %shift_ref.1) | copy-start | bytes 52
  27.1 17.3 %all-to-all-start.1 = ((bf16[16,16,1024]{2,1,0:T(8,128)(2,1)}), bf16[16,16,1024]{2,1,0:T(8,128)(2,1)S(1)}, u32[]{:S(2)}, u32[]{:S(2)}) async-start(bf16[16,16,1024]{2,1,0:T(8,128)(2,1)} %images.1), calls=%async_computation.1 | async-start | bytes 1048576 | tf_op jit(solution)/shard_map/all_to_all | solution.py:292

commit v8 on v6

--- a/solution.py
+++ b/solution.py
@@ -55,27 +55,29 @@
 
 def pack_kernel(vis_ref, weight_ref, pos_ref, pair_ref, out_ref):
     weight = weight_ref[...].astype(jnp.float32)
-    real = weight * vis_ref[0].astype(jnp.float32)
-    imag = weight * vis_ref[1].astype(jnp.float32)
-    shape = (READ_ROWS, CHANNELS)
-    channel = lax.broadcasted_iota(jnp.int32, shape, 1).astype(jnp.float32)
-    frequency = 1.0 + channel / CHANNELS
+    real = vis_ref[0].astype(jnp.float32)
+    imag = vis_ref[1].astype(jnp.float32)
+    shape = (READ_ROWS, LANES)
     row = lax.broadcasted_iota(jnp.int32, shape, 0)
-    spans = []
+    lane = lax.broadcasted_iota(jnp.int32, shape, 1)
+    spans = jnp.zeros(shape, jnp.float32)
     for axis in range(2):
-        span = jnp.zeros(shape, jnp.float32)
+        rest = jnp.zeros(shape, jnp.float32)
         for b in range(READ_ROWS):
             value = pos_ref[axis, pair_ref[0, b]] - pos_ref[axis, pair_ref[1, b]]
-            span = jnp.where(row == b, value, span)
-        spans.append(span * frequency)
-    for a, values in enumerate((real, imag, *spans)):
-        for g in range(GROUPS):
-            part = values[:, g * LANES : (g + 1) * LANES]
-            out_ref[g, a * READ_ROWS : (a + 1) * READ_ROWS, :] = part
+            rest = jnp.where(row == b, value, rest)
+        for i in range(3):
+            piece = rest.astype(jnp.bfloat16).astype(jnp.float32)
+            spans = jnp.where(lane == axis * 3 + i, piece, spans)
+            rest = rest - piece
+    for g in range(GROUPS):
+        lanes = slice(g * LANES, (g + 1) * LANES)
+        tile = [real[:, lanes], imag[:, lanes], weight[:, lanes], spans]
+        out_ref[g] = jnp.concatenate(tile, axis=0).astype(jnp.bfloat16)
 
 
 PHASED = 0
-EAST, NORTH, C8E, S8E, C8N, S8N, C64N, S64N, TABLE = range(2 * FACETS * RUNS, 2 * FACETS * RUNS + 9)
+WEIGHT, SPANS, C8E, S8E, C8N, S8N, C64N, S64N, TABLE = range(2 * FACETS * RUNS, 2 * FACETS * RUNS + 9)
 
 
 def rotate(u, turn):
@@ -83,15 +85,15 @@
     return ur * c - ui * s, ur * s + ui * c
 
 
-def first_kernel(half_ref, shift_ref, data_ref, out_ref, table, starts, *panels):
-    for i, sums in enumerate(image_sums(half_ref, shift_ref, data_ref, table, starts, panels)):
+def first_kernel(place_ref, shift_ref, data_ref, out_ref, table, starts, *panels):
+    for i, sums in enumerate(image_sums(place_ref, shift_ref, data_ref, table, starts, panels)):
         out_ref[i] = sums
 
 
 def last_kernel(
-    half_ref, shift_ref, data_ref, earlier_ref, out_ref, table, starts, acc, *panels
+    place_ref, shift_ref, data_ref, earlier_ref, out_ref, table, starts, acc, *panels
 ):
-    for i, sums in enumerate(image_sums(half_ref, shift_ref, data_ref, table, starts, panels)):
+    for i, sums in enumerate(image_sums(place_ref, shift_ref, data_ref, table, starts, panels)):
         acc[i] = sums + earlier_ref[i]
     for f in range(FACETS):
         for r in range(RUNS):
@@ -107,19 +109,26 @@
                         out_ref[r * 4 + place, :, column : column + HALF] = values.astype(jnp.bfloat16)
 
 
-def image_sums(half_ref, shift_ref, data_ref, table, starts, panels):
+def image_sums(place_ref, shift_ref, data_ref, table, starts, panels):
     for s in range(GROUPS):
-        for a, t in enumerate((PHASED, PHASED + 1, EAST, NORTH)):
-            table[t, s * READ_ROWS : (s + 1) * READ_ROWS, :] = data_ref[
-                s, a * READ_ROWS : (a + 1) * READ_ROWS, :
+        tile = data_ref[s].astype(jnp.float32)
+        for a, t in enumerate((PHASED, PHASED + 1, WEIGHT, SPANS)):
+            table[t, s * READ_ROWS : (s + 1) * READ_ROWS, :] = tile[
+                a * READ_ROWS : (a + 1) * READ_ROWS, :
             ]
-    base_row = (half_ref[0] * RUN_ROWS - HALF).astype(jnp.float32) + (RUN_HALF - 0.5)
-
+    base_row = ((place_ref[0] % HALVES) * RUN_ROWS - HALF).astype(jnp.float32) + (RUN_HALF - 0.5)
+
+    channel = (place_ref[0] // HALVES) * LANES + lax.broadcasted_iota(jnp.int32, (8, LANES), 1)
+    frequency = 1.0 + channel.astype(jnp.float32) / CHANNELS
     for i in range(BLOCKS // 8):
         rows = slice(i * 8, (i + 1) * 8)
-        east = table[EAST, rows, :]
-        north = table[NORTH, rows, :]
-        seen = table[PHASED, rows, :], table[PHASED + 1, rows, :]
+        spans = table[SPANS, rows, :]
+        east, north = (
+            (spans[:, a : a + 1] + spans[:, a + 1 : a + 2] + spans[:, a + 2 : a + 3]) * frequency
+            for a in (0, 3)
+        )
+        weight = table[WEIGHT, rows, :]
+        seen = weight * table[PHASED, rows, :], weight * table[PHASED + 1, rows, :]
         next_run = cos_sin(east * (2.0 * RUN_ROWS / PIX))
         for f in range(FACETS):
             left = (shift_ref[0, f].astype(jnp.float32) + base_row) * (1.0 / PIX)
@@ -237,7 +246,7 @@
 def pack(visibility, weights, positions, station_pairs):
     return pl.pallas_call(
         pack_kernel,
-        out_shape=jax.ShapeDtypeStruct((GROUPS, 4 * READ_ROWS, LANES), jnp.float32),
+        out_shape=jax.ShapeDtypeStruct((GROUPS, 4 * READ_ROWS, LANES), jnp.bfloat16),
         in_specs=[VMEM, VMEM, SMEM, SMEM],
         out_specs=VMEM,
         name="pack",
@@ -302,7 +311,7 @@
 
 
 def body(visibility, weights, positions, station_pairs, facet_shift):
-    half = lax.axis_index("zh").astype(jnp.int32).reshape(1)
+    half = (lax.axis_index("chan") * HALVES + lax.axis_index("zh")).astype(jnp.int32).reshape(1)
     place = lax.axis_index("x").astype(jnp.int32).reshape(1)
     packed = pack(visibility, weights, positions, station_pairs)
     own = lax.all_to_all(packed, "chan", split_axis=0, concat_axis=0, tiled=True)

time: 44.9 us -> 44 us (0.980)
  the two profiles are of different devices: /device:TPU:32 before, /device:TPU:1 now
where the time goes in v8:
time: 44 us; the launch traced here: 43.7 us
  starting transfers between devices  18.4 us (42%)
  waiting for transfers between devices  15.2 us (35%)
  Pallas kernels  10 us (23%)
    all_to_all x1, waiting for transfers between devices, body(): lax.all_to_all(images, ('y', 'x'), split_axis=0, concat_axis=0, tiled=True)  10.3 us
    all_to_all x1, starting transfers between devices, body(): lax.all_to_all(packed, 'chan', split_axis=0, concat_axis=0, tiled=True)  7.4 us
    all_to_all x1, starting transfers between devices, body(): lax.all_to_all(images, ('y', 'x'), split_axis=0, concat_axis=0, tiled=True)  6.75 us
    all_to_all x1, waiting for transfers between devices, body(): lax.all_to_all(packed, 'chan', split_axis=0, concat_axis=0, tiled=True)  4.97 us
    ppermute x1, starting transfers between devices, body(): lax.ppermute(own, 'zh', [(h, HALVES - 1 - h) for h in range(HALVES)])  4.29 us
    pallas_call x1, Pallas kernels, make_images(): pl.pallas_call(last_kernel, out_shape=jax.ShapeDtypeStruct((PEERS, OUT_RO...  4.16 us
    pallas_call x1, Pallas kernels, first_sums(): pl.pallas_call(first_kernel, out_shape=jax.ShapeDtypeStruct(SUMS, jnp.flo...  3.34 us
    pallas_call x1, Pallas kernels, pack(): pl.pallas_call(pack_kernel, out_shape=jax.ShapeDtypeStruct((GROUPS, 4 * R...  1.54 us
  transfers between devices with their start and end apart: 3, of which 2 were waited for; matrix products, arithmetic and copies ran while one was open for 0% of the time, Pallas kernels for 8%

profile of v8, /device:TPU:1, one launch (start us, length us, event | category | flops | bytes accessed | tf_op | source)
XLA Modules:
  0.0 43.7 jit_solution(13252826987782788738)
XLA Ops:
  0.0 1.5 %pack.1 = bf16[8,16,128]{2,1,0:T(8,128)(2,1)} custom-call(bf16[2,4,1024]{2,1,0:T(4,128)(2,1)} %vis_ref.1, bf16[4,1024]{1,0:T(4,128)(2,1)} %weight_ref.1, f32[2,512]{1,0:T(2,128)} %pos_ref.1, s32[2,4]{1,0:T(2,128)} %pair_ref.1), custom_call_target="tpu_custom_call" | custom-call | tf_op jit(solution)/shard_map/pack/pallas_call | solution.py:247
  1.5 7.4 %all-to-all-start = ((bf16[8,16,128]{2,1,0:T(8,128)(2,1)}), bf16[8,16,128]{2,1,0:T(8,128)(2,1)S(1)}, u32[]{:S(2)}, u32[]{:S(2)}) async-start(bf16[8,16,128]{2,1,0:T(8,128)(2,1)} %pack.1), calls=%async_computation | async-start | bytes 65536 | tf_op jit(solution)/shard_map/all_to_all | solution.py:317
  8.9 0.0 copy-start
  8.9 5.0 %all-to-all-done.data_ref = bf16[8,16,128]{2,1,0:T(8,128)(2,1)S(1)} async-done(((bf16[8,16,128]{2,1,0:T(8,128)(2,1)}), bf16[8,16,128]{2,1,0:T(8,128)(2,1)S(1)}, u32[]{:S(2)}, u32[]{:S(2)}) %all-to-all-start) | async-done | bytes 32800 | tf_op jit(solution)/shard_map/all_to_all | solution.py:317
  13.9 4.3 %collective-permute-start = (bf16[8,16,128]{2,1,0:T(8,128)(2,1)S(1)}, bf16[8,16,128]{2,1,0:T(8,128)(2,1)S(1)}, u32[]{:S(2)}, u32[]{:S(2)}) collective-permute-start(bf16[8,16,128]{2,1,0:T(8,128)(2,1)S(1)} %all-to-all-done.data_ref), channel_id=1, source_target_pairs={{0,4},{4,0},{1,5},{5,1},{2,6},{6,2},{3,7},{7,3},{8,12},{12,8},{9,1... | collective-permute-start | bytes 98312 | tf_op jit(solution)/shard_map/ppermute | solution.py:318
  18.2 0.0 copy-done
  18.2 3.3 %first_sums.1.earlier_ref = f32[2,512,256]{2,1,0:T(8,128)S(1)} custom-call(s32[1]{0:T(128)} %bitcast.1.place_ref, s32[2,2]{1,0:T(2,128)S(1)} %copy-done, bf16[8,16,128]{2,1,0:T(8,128)(2,1)S(1)} %all-to-all-done.data_ref), custom_call_target="tpu_custom_call" | custom-call | flops 2147483648 | bytes 1048576 | tf_op jit(solution)/shard_map/first_sums/pallas_call | solution.py:272
  21.6 0.0 collective-permute-done.data_ref
  21.6 4.2 %images.1 = bf16[16,16,1024]{2,1,0:T(8,128)(2,1)} custom-call(s32[1]{0:T(128)} %bitcast.1.place_ref, s32[2,2]{1,0:T(2,128)S(1)} %copy-done, bf16[8,16,128]{2,1,0:T(8,128)(2,1)S(1)} %collective-permute-done.data_ref, f32[2,512,256]{2,1,0:T(8,128)S(1)} %first_sums.1.earlier_ref), custom_call_target="tpu_custom_call" | custom-call | flops 2147483648 | bytes 1048576 | tf_op jit(solution)/shard_map/images/pallas_call | solution.py:285
  25.7 6.8 %all-to-all-start.1 = ((bf16[16,16,1024]{2,1,0:T(8,128)(2,1)}), bf16[16,16,1024]{2,1,0:T(8,128)(2,1)S(1)}, u32[]{:S(2)}, u32[]{:S(2)}) async-start(bf16[16,16,1024]{2,1,0:T(8,128)(2,1)} %images.1), calls=%async_computation.1 | async-start | bytes 1048576 | tf_op jit(solution)/shard_map/all_to_all | solution.py:321
  32.5 10.3 %all-to-all-done.1.data_ref = bf16[16,16,1024]{2,1,0:T(8,128)(2,1)S(1)} async-done(((bf16[16,16,1024]{2,1,0:T(8,128)(2,1)}), bf16[16,16,1024]{2,1,0:T(8,128)(2,1)S(1)}, u32[]{:S(2)}, u32[]{:S(2)}) %all-to-all-start.1) | async-done | bytes 524320 | tf_op jit(solution)/shard_map/all_to_all | solution.py:321
  42.8 1.0 %combine.1 = f32[1,16,1024]{2,1,0:T(8,128)} custom-call(s32[1]{0:T(128)} %bitcast.place_ref, bf16[16,16,1024]{2,1,0:T(8,128)(2,1)S(1)} %all-to-all-done.1.data_ref), custom_call_target="tpu_custom_call" | custom-call | tf_op jit(solution)/shard_map/combine/pallas_call | solution.py:303
Async XLA Ops:
  1.5 12.4 %all-to-all-start = ((bf16[8,16,128]{2,1,0:T(8,128)(2,1)}), bf16[8,16,128]{2,1,0:T(8,128)(2,1)S(1)}, u32[]{:S(2)}, u32[]{:S(2)}) async-start(bf16[8,16,128]{2,1,0:T(8,128)(2,1)} %pack.1), calls=%async_computation | async-start | bytes 65536 | tf_op jit(solution)/shard_map/all_to_all | solution.py:317
  8.9 9.3 %copy-start = (s32[2,2]{1,0:T(2,128)S(1)}, s32[2,2]{1,0:T(2,128)}, u32[]{:S(2)}) copy-start(s32[2,2]{1,0:T(2,128)} %shift_ref.3) | copy-start | bytes 52
  13.9 7.6 %collective-permute-start = (bf16[8,16,128]{2,1,0:T(8,128)(2,1)S(1)}, bf16[8,16,128]{2,1,0:T(8,128)(2,1)S(1)}, u32[]{:S(2)}, u32[]{:S(2)}) collective-permute-start(bf16[8,16,128]{2,1,0:T(8,128)(2,1)S(1)} %all-to-all-done.data_ref), channel_id=1, source_target_pairs={{0,4},{4,0},{1,5},{5,1},{2,6},{6,2},{3,7},{7,3},{8,12},{12,8},{9,1... | collective-permute-start | bytes 98312 | tf_op jit(solution)/shard_map/ppermute | solution.py:318
  25.7 17.0 %all-to-all-start.1 = ((bf16[16,16,1024]{2,1,0:T(8,128)(2,1)}), bf16[16,16,1024]{2,1,0:T(8,128)(2,1)S(1)}, u32[]{:S(2)}, u32[]{:S(2)}) async-start(bf16[16,16,1024]{2,1,0:T(8,128)(2,1)} %images.1), calls=%async_computation.1 | async-start | bytes 1048576 | tf_op jit(solution)/shard_map/all_to_all | solution.py:321

commit v9 on v8

--- a/solution.py
+++ b/solution.py
@@ -15,14 +15,18 @@
 GROUPS = 8
 LANES = 128
 READ_ROWS = 4
-RUN_ROWS = 64
-RUNS = 4
-STEPS = RUN_ROWS // 8
-RUN_HALF = RUN_ROWS // 2
 HALVES = 2
-BLOCKS = GROUPS * READ_ROWS
-PEERS = 16
+PAIRS = 2
+ROWS_Y = 4
 OUT_ROWS = 16
+RUNS = ROWS_Y * PAIRS
+RUN_HALF = OUT_ROWS // 2
+PART_ROWS = FACETS * RUNS * RUN_HALF
+COLUMN_RUN = 64
+COLUMN_RUNS = HALF // COLUMN_RUN
+STEPS = COLUMN_RUN // 8
+SOURCES = GROUPS * PAIRS
+BLOCKS = SOURCES * READ_ROWS
 COS_COEF = (
     1.0, -19.739208221435547, 64.93939208984375, -85.45665740966797,
     60.242130279541016, -26.4046688079834, 7.800131797790527, -1.4531123638153076,
@@ -73,11 +77,13 @@
     for g in range(GROUPS):
         lanes = slice(g * LANES, (g + 1) * LANES)
         tile = [real[:, lanes], imag[:, lanes], weight[:, lanes], spans]
-        out_ref[g] = jnp.concatenate(tile, axis=0).astype(jnp.bfloat16)
+        tile = jnp.concatenate(tile, axis=0).astype(jnp.bfloat16)
+        for pair in range(PAIRS):
+            out_ref[g * PAIRS + pair] = tile
 
 
 PHASED = 0
-WEIGHT, SPANS, C8E, S8E, C8N, S8N, C64N, S64N, TABLE = range(2 * FACETS * RUNS, 2 * FACETS * RUNS + 9)
+WEIGHT, SPANS, C8N, S8N, C64N, S64N, TABLE = range(2 * FACETS * RUNS, 2 * FACETS * RUNS + 7)
 
 
 def rotate(u, turn):
@@ -100,25 +106,27 @@
             at = (f * RUNS + r) * RUN_HALF
             for i in range(2):
                 column = (f * 2 + i) * HALF
-                for k in range(RUN_HALF // OUT_ROWS):
-                    rows = slice(at + k * OUT_ROWS, at + (k + 1) * OUT_ROWS)
-                    rows_imag = slice(at + HALF + k * OUT_ROWS, at + HALF + (k + 1) * OUT_ROWS)
-                    a, b = acc[i, rows], acc[i, rows_imag]
-                    below, above = (a - b, a + b) if i == 0 else (b + a, b - a)
-                    for place, values in ((2 + k, below), (1 - k, above)):
-                        out_ref[r * 4 + place, :, column : column + HALF] = values.astype(jnp.bfloat16)
+                a = acc[i, at : at + RUN_HALF]
+                b = acc[i, PART_ROWS + at : PART_ROWS + at + RUN_HALF]
+                above, below = (a + b, a - b) if i == 0 else (b - a, b + a)
+                out_ref[r, :, column : column + HALF] = jnp.concatenate(
+                    [above, below], axis=0
+                ).astype(jnp.bfloat16)
 
 
 def image_sums(place_ref, shift_ref, data_ref, table, starts, panels):
-    for s in range(GROUPS):
+    for s in range(SOURCES):
         tile = data_ref[s].astype(jnp.float32)
         for a, t in enumerate((PHASED, PHASED + 1, WEIGHT, SPANS)):
             table[t, s * READ_ROWS : (s + 1) * READ_ROWS, :] = tile[
                 a * READ_ROWS : (a + 1) * READ_ROWS, :
             ]
-    base_row = ((place_ref[0] % HALVES) * RUN_ROWS - HALF).astype(jnp.float32) + (RUN_HALF - 0.5)
-
-    channel = (place_ref[0] // HALVES) * LANES + lax.broadcasted_iota(jnp.int32, (8, LANES), 1)
+    pair = place_ref[0] % PAIRS
+    half = (place_ref[0] // PAIRS) % HALVES
+    group = place_ref[0] // (PAIRS * HALVES)
+    first_row = half * PAIRS * (PAIRS * OUT_ROWS) + pair * OUT_ROWS - HALF
+    base_row = first_row.astype(jnp.float32) + (RUN_HALF - 0.5)
+    channel = group * LANES + lax.broadcasted_iota(jnp.int32, (8, LANES), 1)
     frequency = 1.0 + channel.astype(jnp.float32) / CHANNELS
     for i in range(BLOCKS // 8):
         rows = slice(i * 8, (i + 1) * 8)
@@ -129,16 +137,18 @@
         )
         weight = table[WEIGHT, rows, :]
         seen = weight * table[PHASED, rows, :], weight * table[PHASED + 1, rows, :]
-        next_run = cos_sin(east * (2.0 * RUN_ROWS / PIX))
+        to_next_y = cos_sin(east * (HALVES * PAIRS * PAIRS * OUT_ROWS / PIX))
+        to_next_x = cos_sin(east * (PAIRS * OUT_ROWS / PIX))
         for f in range(FACETS):
             left = (shift_ref[0, f].astype(jnp.float32) + base_row) * (1.0 / PIX)
             right = (shift_ref[1, f].astype(jnp.float32) - 0.5) * (1.0 / PIX)
             phased = rotate(seen, cos_sin(frac(east * left) + frac(north * right)))
-            for r in range(RUNS):
-                if r:
-                    phased = rotate(phased, next_run)
-                at = PHASED + 2 * (f * RUNS + r)
-                table[at, rows, :], table[at + 1, rows, :] = phased
+            for y in range(ROWS_Y):
+                if y:
+                    phased = rotate(phased, to_next_y)
+                for x, values in enumerate((phased, rotate(phased, to_next_x))):
+                    at = PHASED + 2 * (f * RUNS + y * PAIRS + x)
+                    table[at, rows, :], table[at + 1, rows, :] = values
         table[C64N, rows, :], table[S64N, rows, :] = cos_sin(north * (64.0 / PIX))
         for place, turns in enumerate((east, north)):
             first = now = cos_sin(turns * (0.5 / PIX))
@@ -150,8 +160,8 @@
                     before, now = now, tuple(twice * b - a for a, b in zip(before, now))
                 for part in range(2):
                     starts[place * 2 + part, pl.ds(i * 64 + j, 8, stride=8), :] = now[part]
-            t = (C8E, C8N)[place]
-            table[t, rows, :], table[t + 1, rows, :] = rotate(now, first)
+            if place:
+                table[C8N, rows, :], table[S8N, rows, :] = rotate(now, first)
 
     panels = [panels[i : i + 4] for i in range(0, len(panels), 4)]
     for block, (left_cos, left_sin, right_cos, right_sin) in enumerate(panels):
@@ -163,23 +173,16 @@
             ref[at : at + 16, :] = jnp.concatenate([first, second], axis=0).astype(jnp.bfloat16)
 
         here = slice(block * 8, (block + 1) * 8)
-        base = starts[0, here, :], starts[1, here, :]
-        turn = (row(C8E), row(S8E))
-        wave = [base, rotate(base, turn)]
-        twice = 2.0 * turn[0]
-        for _ in range(2, RUN_HALF // 8):
-            wave.append(tuple(twice * b - a for a, b in zip(wave[-2], wave[-1])))
-        for f in range(FACETS):
-            for r in range(RUNS):
-                index = PHASED + 2 * (f * RUNS + r)
-                real, imag = row(index), row(index + 1)
-                at = (f * RUNS + r) * RUN_HALF
-                for j in range(0, RUN_HALF // 8, 2):
-                    (c0, s0), (c1, s1) = wave[j], wave[j + 1]
-                    put(left_cos, at + j * 8, real * c0, real * c1)
-                    put(left_cos, at + HALF + j * 8, imag * s0, imag * s1)
-                    put(left_sin, at + j * 8, real * s0, real * s1)
-                    put(left_sin, at + HALF + j * 8, imag * c0, imag * c1)
+        cos, sin = starts[0, here, :], starts[1, here, :]
+        for pair in range(0, FACETS * RUNS, 2):
+            (r0, i0), (r1, i1) = (
+                (row(PHASED + 2 * k), row(PHASED + 2 * k + 1)) for k in (pair, pair + 1)
+            )
+            at = pair * RUN_HALF
+            put(left_cos, at, r0 * cos, r1 * cos)
+            put(left_cos, PART_ROWS + at, i0 * sin, i1 * sin)
+            put(left_sin, at, r0 * sin, r1 * sin)
+            put(left_sin, PART_ROWS + at, i0 * cos, i1 * cos)
 
         start = starts[2, here, :], starts[3, here, :]
         turn = (row(C8N), row(S8N))
@@ -187,7 +190,7 @@
         anchors = [(start, rotate(start, turn))]
         anchors.append(tuple(rotate(u, next_run) for u in anchors[0]))
         twice = 2.0 * next_run[0]
-        for _ in range(2, RUNS):
+        for _ in range(2, COLUMN_RUNS):
             anchors.append(
                 tuple(
                     tuple(twice * b - a for a, b in zip(old, new))
@@ -202,7 +205,7 @@
                     if j:
                         before = twice * now - before
                         now = twice * before - now
-                    put(ref, r * RUN_ROWS + j * 8, before, now)
+                    put(ref, r * COLUMN_RUN + j * 8, before, now)
 
     left_cos, left_sin, right_cos, right_sin = (
         jnp.concatenate([ref[...] for ref in refs], axis=1) for refs in zip(*panels)
@@ -212,13 +215,14 @@
         yield lax.dot_general(left, right, contract, preferred_element_type=jnp.float32)
 
 
-def combine_kernel(scale, place_ref, data_ref, out_ref):
-    shape = (OUT_ROWS, PEERS * OUT_ROWS)
+def combine_kernel(scale, data_ref, out_ref):
+    shape = (OUT_ROWS, RUNS * OUT_ROWS)
     out_row = lax.broadcasted_iota(jnp.int32, shape, 0)
     sent_row = lax.broadcasted_iota(jnp.int32, shape, 1) % OUT_ROWS
-    wanted = jnp.where(place_ref[0] < 2, OUT_ROWS - 1 - out_row, out_row)
+    wanted = jnp.where(out_row < RUN_HALF, RUN_HALF - 1 - out_row, out_row)
     pick = (sent_row == wanted).astype(jnp.bfloat16)
-    total = jnp.dot(pick, data_ref[...].reshape(PEERS * OUT_ROWS, FACETS * PIX), preferred_element_type=jnp.float32) * scale
+    data = data_ref[...].reshape(RUNS * OUT_ROWS, FACETS * PIX)
+    total = jnp.dot(pick, data, preferred_element_type=jnp.float32) * scale
     flip = (
         lax.broadcasted_iota(jnp.int32, (HALF, HALF), 0)
         + lax.broadcasted_iota(jnp.int32, (HALF, HALF), 1)
@@ -246,22 +250,22 @@
 def pack(visibility, weights, positions, station_pairs):
     return pl.pallas_call(
         pack_kernel,
-        out_shape=jax.ShapeDtypeStruct((GROUPS, 4 * READ_ROWS, LANES), jnp.bfloat16),
+        out_shape=jax.ShapeDtypeStruct((SOURCES, 4 * READ_ROWS, LANES), jnp.bfloat16),
         in_specs=[VMEM, VMEM, SMEM, SMEM],
         out_specs=VMEM,
         name="pack",
     )(visibility, weights, positions, station_pairs)
 
 
-SUMS = (2, FACETS * HALF, HALF)
+SUMS = (2, 2 * PART_ROWS, HALF)
 ROWS_COST = pl.CostEstimate(
     flops=2 * math.prod(SUMS) * BLOCKS * LANES, bytes_accessed=4 * math.prod(SUMS), transcendentals=0
 )
 TABLE_SCRATCH = pltpu.VMEM((TABLE, BLOCKS, LANES), jnp.float32)
 START_SCRATCH = pltpu.VMEM((4, BLOCKS * 8, LANES), jnp.float32)
 PANELS = [
-    pltpu.VMEM((FACETS * HALF, LANES), jnp.bfloat16),
-    pltpu.VMEM((FACETS * HALF, LANES), jnp.bfloat16),
+    pltpu.VMEM((2 * PART_ROWS, LANES), jnp.bfloat16),
+    pltpu.VMEM((2 * PART_ROWS, LANES), jnp.bfloat16),
     pltpu.VMEM((HALF, LANES), jnp.bfloat16),
     pltpu.VMEM((HALF, LANES), jnp.bfloat16),
 ] * BLOCKS
@@ -284,7 +288,7 @@
 def make_images(half, facet_shift, arrived, earlier):
     return pl.pallas_call(
         last_kernel,
-        out_shape=jax.ShapeDtypeStruct((PEERS, OUT_ROWS, FACETS * PIX), jnp.bfloat16),
+        out_shape=jax.ShapeDtypeStruct((RUNS, OUT_ROWS, FACETS * PIX), jnp.bfloat16),
         in_specs=[SMEM, SMEM, VMEM, VMEM],
         out_specs=VMEM,
         scratch_shapes=[
@@ -299,35 +303,36 @@
     )(half, facet_shift, arrived, earlier)
 
 
-def combine(scale, place, parts):
+def combine(scale, parts):
     return pl.pallas_call(
         functools.partial(combine_kernel, scale),
         out_shape=jax.ShapeDtypeStruct((1, OUT_ROWS, FACETS * PIX), jnp.float32),
-        in_specs=[SMEM, VMEM],
+        in_specs=[VMEM],
         out_specs=VMEM,
         compiler_params=pltpu.CompilerParams(vmem_limit_bytes=8 * 1024 * 1024),
         name="combine",
-    )(place, parts)
+    )(parts)
 
 
 def body(visibility, weights, positions, station_pairs, facet_shift):
-    half = (lax.axis_index("chan") * HALVES + lax.axis_index("zh")).astype(jnp.int32).reshape(1)
-    place = lax.axis_index("x").astype(jnp.int32).reshape(1)
+    place = lax.axis_index("chan") * HALVES + lax.axis_index("zh")
+    place = (place * PAIRS + lax.axis_index("xl")).astype(jnp.int32).reshape(1)
     packed = pack(visibility, weights, positions, station_pairs)
-    own = lax.all_to_all(packed, "chan", split_axis=0, concat_axis=0, tiled=True)
+    own = lax.all_to_all(packed, ("chan", "xl"), split_axis=0, concat_axis=0, tiled=True)
     other = lax.ppermute(own, "zh", [(h, HALVES - 1 - h) for h in range(HALVES)])
-    earlier = first_sums(half, facet_shift, own)
-    images = make_images(half, facet_shift, other, earlier)
+    earlier = first_sums(place, facet_shift, own)
+    images = make_images(place, facet_shift, other, earlier)
     parts = lax.all_to_all(
-        images, ("y", "x"), split_axis=0, concat_axis=0, tiled=True
+        images, ("y", "xh"), split_axis=0, concat_axis=0, tiled=True
     )
     scale = 1.0 / math.sqrt(READ_ROWS * GROUPS * 32 * LANES)
-    return combine(scale, place, parts)
+    return combine(scale, parts)
 
 
 def solution(mesh):
-    fine = Mesh(mesh.devices.reshape(GROUPS, 4, HALVES, 4), ("chan", "y", "zh", "x"))
-    line = ("y", "zh", "x")
+    shape = (GROUPS, ROWS_Y, HALVES, PAIRS, PAIRS)
+    line = ("y", "zh", "xh", "xl")
+    fine = Mesh(mesh.devices.reshape(shape), ("chan", *line))
     in_specs = (
         P(None, ("chan", *line), None),
         P(("chan", *line), None),

time: 44 us -> 46.2 us (1.050)
  blocking collectives: 0 us -> 13.8 us
  waiting for transfers between devices: 15.2 us -> 6.38 us
  starting transfers between devices: 18.4 us -> 12.6 us
  Pallas kernels: 10 us -> 13.1 us
    all_to_all x0 -> x1, blocking collectives: none -> 13.8 us  [body(): lax.all_to_all(images, ('y', 'xh'), split_axis=0, concat_axis=0, tiled=True)]
    all_to_all x2 -> x1, waiting for transfers between devices: 15.2 us -> 6.37 us  [body(): lax.all_to_all(packed, ('chan', 'xl'), split_axis=0, concat_axis=0, tiled...]
    all_to_all x2 -> x1, starting transfers between devices: 14.2 us -> 8.35 us  [body(): lax.all_to_all(packed, ('chan', 'xl'), split_axis=0, concat_axis=0, tiled...]
    pallas_call x1, Pallas kernels: 3.34 us -> 5.29 us  [first_sums(): pl.pallas_call(first_kernel, out_shape=jax.ShapeDtypeStruct(SUMS, jnp.flo...]
    pallas_call x2, Pallas kernels: 5.7 us -> 6.86 us  [the longest x1 5.31 us: make_images(): pl.pallas_call(last_kernel, out_shape=jax.ShapeDtypeStruct((RUNS, OUT_ROW...]
  transfers between devices with their start and end apart: 3 -> 2, of which waited for: 2 -> 1; matrix products, arithmetic and copies ran while one was open for 0% -> 0% of each run, Pallas kernels for 8% -> 12%
where the time goes in v9:
time: 46.2 us; the launch traced here: 45.9 us
  blocking collectives  13.8 us (30%)
  Pallas kernels  13.1 us (28%)
  starting transfers between devices  12.6 us (27%)
  waiting for transfers between devices  6.38 us (14%)
    all_to_all x1, blocking collectives, body(): lax.all_to_all(images, ('y', 'xh'), split_axis=0, concat_axis=0, tiled=True)  13.8 us
    all_to_all x1, starting transfers between devices, body(): lax.all_to_all(packed, ('chan', 'xl'), split_axis=0, concat_axis=0, tiled...  8.35 us
    all_to_all x1, waiting for transfers between devices, body(): lax.all_to_all(packed, ('chan', 'xl'), split_axis=0, concat_axis=0, tiled...  6.37 us
    pallas_call x1, Pallas kernels, make_images(): pl.pallas_call(last_kernel, out_shape=jax.ShapeDtypeStruct((RUNS, OUT_ROW...  5.31 us
    pallas_call x1, Pallas kernels, first_sums(): pl.pallas_call(first_kernel, out_shape=jax.ShapeDtypeStruct(SUMS, jnp.flo...  5.29 us
    ppermute x1, starting transfers between devices, body(): lax.ppermute(own, 'zh', [(h, HALVES - 1 - h) for h in range(HALVES)])  4.21 us
    pallas_call x1, Pallas kernels, pack(): pl.pallas_call(pack_kernel, out_shape=jax.ShapeDtypeStruct((SOURCES, 4 *...  1.56 us
    pallas_call x1, Pallas kernels, combine(): pl.pallas_call(functools.partial(combine_kernel, scale), out_shape=jax.Sh...  0.95 us
  transfers between devices with their start and end apart: 2, of which 1 were waited for; matrix products, arithmetic and copies ran while one was open for 0% of the time, Pallas kernels for 12%

profile of v9, /device:TPU:1, one launch (start us, length us, event | category | flops | bytes accessed | tf_op | source)
XLA Modules:
  0.0 45.9 jit_solution(3042497857026433994)
XLA Ops:
  0.0 1.6 %pack.1 = bf16[16,16,128]{2,1,0:T(8,128)(2,1)} custom-call(bf16[2,4,1024]{2,1,0:T(4,128)(2,1)} %vis_ref.1, bf16[4,1024]{1,0:T(4,128)(2,1)} %weight_ref.1, f32[2,512]{1,0:T(2,128)} %pos_ref.1, s32[2,4]{1,0:T(2,128)} %pair_ref.1), custom_call_target="tpu_custom_call" | custom-call | tf_op jit(solution)/shard_map/pack/pallas_call | solution.py:251
  1.6 8.3 %all-to-all-start = ((bf16[16,16,128]{2,1,0:T(8,128)(2,1)}), bf16[16,16,128]{2,1,0:T(8,128)(2,1)S(1)}, u32[]{:S(2)}, u32[]{:S(2)}) async-start(bf16[16,16,128]{2,1,0:T(8,128)(2,1)} %pack.1), calls=%async_computation | async-start | bytes 131072 | tf_op jit(solution)/shard_map/all_to_all | solution.py:321
  9.9 0.0 copy-start
  9.9 6.4 %all-to-all-done.data_ref = bf16[16,16,128]{2,1,0:T(8,128)(2,1)S(1)} async-done(((bf16[16,16,128]{2,1,0:T(8,128)(2,1)}), bf16[16,16,128]{2,1,0:T(8,128)(2,1)S(1)}, u32[]{:S(2)}, u32[]{:S(2)}) %all-to-all-start) | async-done | bytes 65568 | tf_op jit(solution)/shard_map/all_to_all | solution.py:321
  16.3 4.2 %collective-permute-start = (bf16[16,16,128]{2,1,0:T(8,128)(2,1)S(1)}, bf16[16,16,128]{2,1,0:T(8,128)(2,1)S(1)}, u32[]{:S(2)}, u32[]{:S(2)}) collective-permute-start(bf16[16,16,128]{2,1,0:T(8,128)(2,1)S(1)} %all-to-all-done.data_ref), channel_id=1, source_target_pairs={{0,4},{4,0},{1,5},{5,1},{2,6},{6,2},{3,7},{7,3},{8,12},{12,8},{9,1... | collective-permute-start | bytes 196616 | tf_op jit(solution)/shard_map/ppermute | solution.py:322
  20.5 0.0 copy-done
  20.5 5.3 %first_sums.1.earlier_ref = f32[2,256,256]{2,1,0:T(8,128)S(1)} custom-call(s32[1]{0:T(128)} %bitcast.place_ref, s32[2,2]{1,0:T(2,128)S(1)} %copy-done, bf16[16,16,128]{2,1,0:T(8,128)(2,1)S(1)} %all-to-all-done.data_ref), custom_call_target="tpu_custom_call" | custom-call | flops 2147483648 | bytes 524288 | tf_op jit(solution)/shard_map/first_sums/pallas_call | solution.py:276
  25.8 0.0 collective-permute-done.data_ref
  25.8 5.3 %images.1 = bf16[8,16,1024]{2,1,0:T(8,128)(2,1)S(1)} custom-call(s32[1]{0:T(128)} %bitcast.place_ref, s32[2,2]{1,0:T(2,128)S(1)} %copy-done, bf16[16,16,128]{2,1,0:T(8,128)(2,1)S(1)} %collective-permute-done.data_ref, f32[2,256,256]{2,1,0:T(8,128)S(1)} %first_sums.1.earlier_ref), custom_call_target="tpu_custom_call" | custom-call | flops 2147483648 | bytes 524288 | tf_op jit(solution)/shard_map/images/pallas_call | solution.py:289
  31.1 13.8 %all_to_all.10.data_ref = bf16[8,16,1024]{2,1,0:T(8,128)(2,1)S(1)} all-to-all(bf16[8,16,1024]{2,1,0:T(8,128)(2,1)S(1)} %images.1), channel_id=1, replica_groups=mesh['chan'=8,'y'=4,'zh'=2,'xh'=2,'xl'=2] {'y','xh'}, dimensions={0} | all-to-all | bytes 524288 | tf_op jit(solution)/shard_map/all_to_all | solution.py:325
  44.9 1.0 %combine.1 = f32[1,16,1024]{2,1,0:T(8,128)} custom-call(bf16[8,16,1024]{2,1,0:T(8,128)(2,1)S(1)} %all_to_all.10.data_ref), custom_call_target="tpu_custom_call" | custom-call | tf_op jit(solution)/shard_map/combine/pallas_call | solution.py:307
Async XLA Ops:
  1.6 14.7 %all-to-all-start = ((bf16[16,16,128]{2,1,0:T(8,128)(2,1)}), bf16[16,16,128]{2,1,0:T(8,128)(2,1)S(1)}, u32[]{:S(2)}, u32[]{:S(2)}) async-start(bf16[16,16,128]{2,1,0:T(8,128)(2,1)} %pack.1), calls=%async_computation | async-start | bytes 131072 | tf_op jit(solution)/shard_map/all_to_all | solution.py:321
  9.9 10.6 %copy-start = (s32[2,2]{1,0:T(2,128)S(1)}, s32[2,2]{1,0:T(2,128)}, u32[]{:S(2)}) copy-start(s32[2,2]{1,0:T(2,128)} %shift_ref.3) | copy-start | bytes 52
  16.3 9.5 %collective-permute-start = (bf16[16,16,128]{2,1,0:T(8,128)(2,1)S(1)}, bf16[16,16,128]{2,1,0:T(8,128)(2,1)S(1)}, u32[]{:S(2)}, u32[]{:S(2)}) collective-permute-start(bf16[16,16,128]{2,1,0:T(8,128)(2,1)S(1)} %all-to-all-done.data_ref), channel_id=1, source_target_pairs={{0,4},{4,0},{1,5},{5,1},{2,6},{6,2},{3,7},{7,3},{8,12},{12,8},{9,1... | collective-permute-start | bytes 196616 | tf_op jit(solution)/shard_map/ppermute | solution.py:322

commit v10 on v8

--- a/solution.py
+++ b/solution.py
@@ -20,7 +20,8 @@
 STEPS = RUN_ROWS // 8
 RUN_HALF = RUN_ROWS // 2
 HALVES = 2
-BLOCKS = GROUPS * READ_ROWS
+SOURCES = GROUPS * HALVES
+BLOCKS = SOURCES * READ_ROWS
 PEERS = 16
 OUT_ROWS = 16
 COS_COEF = (
@@ -73,7 +74,9 @@
     for g in range(GROUPS):
         lanes = slice(g * LANES, (g + 1) * LANES)
         tile = [real[:, lanes], imag[:, lanes], weight[:, lanes], spans]
-        out_ref[g] = jnp.concatenate(tile, axis=0).astype(jnp.bfloat16)
+        tile = jnp.concatenate(tile, axis=0).astype(jnp.bfloat16)
+        for h in range(HALVES):
+            out_ref[g * HALVES + h] = tile
 
 
 PHASED = 0
@@ -85,16 +88,9 @@
     return ur * c - ui * s, ur * s + ui * c
 
 
-def first_kernel(place_ref, shift_ref, data_ref, out_ref, table, starts, *panels):
+def image_kernel(place_ref, shift_ref, data_ref, out_ref, table, starts, acc, *panels):
     for i, sums in enumerate(image_sums(place_ref, shift_ref, data_ref, table, starts, panels)):
-        out_ref[i] = sums
-
-
-def last_kernel(
-    place_ref, shift_ref, data_ref, earlier_ref, out_ref, table, starts, acc, *panels
-):
-    for i, sums in enumerate(image_sums(place_ref, shift_ref, data_ref, table, starts, panels)):
-        acc[i] = sums + earlier_ref[i]
+        acc[i] = sums
     for f in range(FACETS):
         for r in range(RUNS):
             at = (f * RUNS + r) * RUN_HALF
@@ -110,7 +106,7 @@
 
 
 def image_sums(place_ref, shift_ref, data_ref, table, starts, panels):
-    for s in range(GROUPS):
+    for s in range(SOURCES):
         tile = data_ref[s].astype(jnp.float32)
         for a, t in enumerate((PHASED, PHASED + 1, WEIGHT, SPANS)):
             table[t, s * READ_ROWS : (s + 1) * READ_ROWS, :] = tile[
@@ -246,7 +242,7 @@
 def pack(visibility, weights, positions, station_pairs):
     return pl.pallas_call(
         pack_kernel,
-        out_shape=jax.ShapeDtypeStruct((GROUPS, 4 * READ_ROWS, LANES), jnp.bfloat16),
+        out_shape=jax.ShapeDtypeStruct((SOURCES, 4 * READ_ROWS, LANES), jnp.bfloat16),
         in_specs=[VMEM, VMEM, SMEM, SMEM],
         out_specs=VMEM,
         name="pack",
@@ -265,27 +261,14 @@
     pltpu.VMEM((HALF, LANES), jnp.bfloat16),
     pltpu.VMEM((HALF, LANES), jnp.bfloat16),
 ] * BLOCKS
-IMAGE_PARAMS = pltpu.CompilerParams(vmem_limit_bytes=32 * 1024 * 1024)
-
-
-def first_sums(half, facet_shift, arrived):
+IMAGE_PARAMS = pltpu.CompilerParams(vmem_limit_bytes=48 * 1024 * 1024)
+
+
+def make_images(half, facet_shift, arrived):
     return pl.pallas_call(
-        first_kernel,
-        out_shape=jax.ShapeDtypeStruct(SUMS, jnp.float32),
+        image_kernel,
+        out_shape=jax.ShapeDtypeStruct((PEERS, OUT_ROWS, FACETS * PIX), jnp.bfloat16),
         in_specs=[SMEM, SMEM, VMEM],
-        out_specs=VMEM,
-        scratch_shapes=[TABLE_SCRATCH, START_SCRATCH, *PANELS],
-        compiler_params=IMAGE_PARAMS,
-        cost_estimate=ROWS_COST,
-        name="first_sums",
-    )(half, facet_shift, arrived)
-
-
-def make_images(half, facet_shift, arrived, earlier):
-    return pl.pallas_call(
-        last_kernel,
-        out_shape=jax.ShapeDtypeStruct((PEERS, OUT_ROWS, FACETS * PIX), jnp.bfloat16),
-        in_specs=[SMEM, SMEM, VMEM, VMEM],
         out_specs=VMEM,
         scratch_shapes=[
             TABLE_SCRATCH,
@@ -296,7 +279,7 @@
         compiler_params=IMAGE_PARAMS,
         cost_estimate=ROWS_COST,
         name="images",
-    )(half, facet_shift, arrived, earlier)
+    )(half, facet_shift, arrived)
 
 
 def combine(scale, place, parts):
@@ -314,10 +297,8 @@
     half = (lax.axis_index("chan") * HALVES + lax.axis_index("zh")).astype(jnp.int32).reshape(1)
     place = lax.axis_index("x").astype(jnp.int32).reshape(1)
     packed = pack(visibility, weights, positions, station_pairs)
-    own = lax.all_to_all(packed, "chan", split_axis=0, concat_axis=0, tiled=True)
-    other = lax.ppermute(own, "zh", [(h, HALVES - 1 - h) for h in range(HALVES)])
-    earlier = first_sums(half, facet_shift, own)
-    images = make_images(half, facet_shift, other, earlier)
+    arrived = lax.all_to_all(packed, ("chan", "zh"), split_axis=0, concat_axis=0, tiled=True)
+    images = make_images(half, facet_shift, arrived)
     parts = lax.all_to_all(
         images, ("y", "x"), split_axis=0, concat_axis=0, tiled=True
     )

time: 44 us -> 44.3 us (level)
  waiting for transfers between devices: 15.2 us -> 18.2 us
  starting transfers between devices: 18.4 us -> 16.7 us
  Pallas kernels: 10 us -> 9.05 us
    ppermute x1 -> x0, starting transfers between devices: 4.29 us -> none  [body(): lax.ppermute(own, 'zh', [(h, HALVES - 1 - h) for h in range(HALVES)])]
    all_to_all x1, waiting for transfers between devices: 4.97 us -> 7.63 us  [body(): lax.all_to_all(packed, ('chan', 'zh'), split_axis=0, concat_axis=0, tiled...]
    all_to_all x1, starting transfers between devices: 7.4 us -> 9.98 us  [body(): lax.all_to_all(packed, ('chan', 'zh'), split_axis=0, concat_axis=0, tiled...]
    pallas_call x3 -> x2, Pallas kernels: 9.05 us -> 8.06 us  [the longest x1 6.5 us: make_images(): pl.pallas_call(image_kernel, out_shape=jax.ShapeDtypeStruct((PEERS, OUT_R...]
  transfers between devices with their start and end apart: 3 -> 2, of which waited for: 2 -> 2; matrix products, arithmetic and copies ran while one was open for 0% -> 0% of each run, Pallas kernels for 8% -> 0%
where the time goes in v10:
time: 44.3 us; the launch traced here: 44 us
  waiting for transfers between devices  18.2 us (41%)
  starting transfers between devices  16.7 us (38%)
  Pallas kernels  9.05 us (20%)
    all_to_all x1, waiting for transfers between devices, body(): lax.all_to_all(images, ('y', 'x'), split_axis=0, concat_axis=0, tiled=True)  10.6 us
    all_to_all x1, starting transfers between devices, body(): lax.all_to_all(packed, ('chan', 'zh'), split_axis=0, concat_axis=0, tiled...  9.98 us
    all_to_all x1, waiting for transfers between devices, body(): lax.all_to_all(packed, ('chan', 'zh'), split_axis=0, concat_axis=0, tiled...  7.63 us
    all_to_all x1, starting transfers between devices, body(): lax.all_to_all(images, ('y', 'x'), split_axis=0, concat_axis=0, tiled=True)  6.75 us
    pallas_call x1, Pallas kernels, make_images(): pl.pallas_call(image_kernel, out_shape=jax.ShapeDtypeStruct((PEERS, OUT_R...  6.5 us
    pallas_call x1, Pallas kernels, pack(): pl.pallas_call(pack_kernel, out_shape=jax.ShapeDtypeStruct((SOURCES, 4 *...  1.56 us
    pallas_call x1, Pallas kernels, combine(): pl.pallas_call(functools.partial(combine_kernel, scale), out_shape=jax.Sh...  0.99 us
  transfers between devices with their start and end apart: 2, of which 2 were waited for; matrix products, arithmetic and copies ran while one was open for 0% of the time, Pallas kernels for 0%

profile of v10, /device:TPU:1, one launch (start us, length us, event | category | flops | bytes accessed | tf_op | source)
XLA Modules:
  0.0 44.0 jit_solution(11659363557710491852)
XLA Ops:
  0.0 1.6 %pack.1 = bf16[16,16,128]{2,1,0:T(8,128)(2,1)} custom-call(bf16[2,4,1024]{2,1,0:T(4,128)(2,1)} %vis_ref.1, bf16[4,1024]{1,0:T(4,128)(2,1)} %weight_ref.1, f32[2,512]{1,0:T(2,128)} %pos_ref.1, s32[2,4]{1,0:T(2,128)} %pair_ref.1), custom_call_target="tpu_custom_call" | custom-call | tf_op jit(solution)/shard_map/pack/pallas_call | solution.py:243
  1.6 10.0 %all-to-all-start = ((bf16[16,16,128]{2,1,0:T(8,128)(2,1)}), bf16[16,16,128]{2,1,0:T(8,128)(2,1)S(1)}, u32[]{:S(2)}, u32[]{:S(2)}) async-start(bf16[16,16,128]{2,1,0:T(8,128)(2,1)} %pack.1), calls=%async_computation | async-start | bytes 131072 | tf_op jit(solution)/shard_map/all_to_all | solution.py:300
  11.5 0.0 copy-start
  11.6 7.6 %all-to-all-done.data_ref = bf16[16,16,128]{2,1,0:T(8,128)(2,1)S(1)} async-done(((bf16[16,16,128]{2,1,0:T(8,128)(2,1)}), bf16[16,16,128]{2,1,0:T(8,128)(2,1)S(1)}, u32[]{:S(2)}, u32[]{:S(2)}) %all-to-all-start) | async-done | bytes 65568 | tf_op jit(solution)/shard_map/all_to_all | solution.py:300
  19.2 0.0 copy-done
  19.2 6.5 %images.1 = bf16[16,16,1024]{2,1,0:T(8,128)(2,1)} custom-call(s32[1]{0:T(128)} %bitcast.1.place_ref, s32[2,2]{1,0:T(2,128)S(1)} %copy-done, bf16[16,16,128]{2,1,0:T(8,128)(2,1)S(1)} %all-to-all-done.data_ref), custom_call_target="tpu_custom_call" | custom-call | flops 4294967296 | bytes 1048576 | tf_op jit(solution)/shard_map/images/pallas_call | solution.py:268
  25.7 6.8 %all-to-all-start.1 = ((bf16[16,16,1024]{2,1,0:T(8,128)(2,1)}), bf16[16,16,1024]{2,1,0:T(8,128)(2,1)S(1)}, u32[]{:S(2)}, u32[]{:S(2)}) async-start(bf16[16,16,1024]{2,1,0:T(8,128)(2,1)} %images.1), calls=%async_computation.1 | async-start | bytes 1048576 | tf_op jit(solution)/shard_map/all_to_all | solution.py:302
  32.4 10.6 %all-to-all-done.1.data_ref = bf16[16,16,1024]{2,1,0:T(8,128)(2,1)S(1)} async-done(((bf16[16,16,1024]{2,1,0:T(8,128)(2,1)}), bf16[16,16,1024]{2,1,0:T(8,128)(2,1)S(1)}, u32[]{:S(2)}, u32[]{:S(2)}) %all-to-all-start.1) | async-done | bytes 524320 | tf_op jit(solution)/shard_map/all_to_all | solution.py:302
  43.0 1.0 %combine.1 = f32[1,16,1024]{2,1,0:T(8,128)} custom-call(s32[1]{0:T(128)} %bitcast.place_ref, bf16[16,16,1024]{2,1,0:T(8,128)(2,1)S(1)} %all-to-all-done.1.data_ref), custom_call_target="tpu_custom_call" | custom-call | tf_op jit(solution)/shard_map/combine/pallas_call | solution.py:286
Async XLA Ops:
  1.6 17.6 %all-to-all-start = ((bf16[16,16,128]{2,1,0:T(8,128)(2,1)}), bf16[16,16,128]{2,1,0:T(8,128)(2,1)S(1)}, u32[]{:S(2)}, u32[]{:S(2)}) async-start(bf16[16,16,128]{2,1,0:T(8,128)(2,1)} %pack.1), calls=%async_computation | async-start | bytes 131072 | tf_op jit(solution)/shard_map/all_to_all | solution.py:300
  11.5 7.6 %copy-start = (s32[2,2]{1,0:T(2,128)S(1)}, s32[2,2]{1,0:T(2,128)}, u32[]{:S(2)}) copy-start(s32[2,2]{1,0:T(2,128)} %shift_ref.1) | copy-start | bytes 52
  25.7 17.4 %all-to-all-start.1 = ((bf16[16,16,1024]{2,1,0:T(8,128)(2,1)}), bf16[16,16,1024]{2,1,0:T(8,128)(2,1)S(1)}, u32[]{:S(2)}, u32[]{:S(2)}) async-start(bf16[16,16,1024]{2,1,0:T(8,128)(2,1)} %images.1), calls=%async_computation.1 | async-start | bytes 1048576 | tf_op jit(solution)/shard_map/all_to_all | solution.py:302

commit v11 on v8

--- a/solution.py
+++ b/solution.py
@@ -106,7 +106,8 @@
                     a, b = acc[i, rows], acc[i, rows_imag]
                     below, above = (a - b, a + b) if i == 0 else (b + a, b - a)
                     for place, values in ((2 + k, below), (1 - k, above)):
-                        out_ref[r * 4 + place, :, column : column + HALF] = values.astype(jnp.bfloat16)
+                        chunk = (place % 2) * 8 + r * 2 + place // 2
+                        out_ref[chunk, :, column : column + HALF] = values.astype(jnp.bfloat16)
 
 
 def image_sums(place_ref, shift_ref, data_ref, table, starts, panels):
@@ -312,22 +313,22 @@
 
 def body(visibility, weights, positions, station_pairs, facet_shift):
     half = (lax.axis_index("chan") * HALVES + lax.axis_index("zh")).astype(jnp.int32).reshape(1)
-    place = lax.axis_index("x").astype(jnp.int32).reshape(1)
+    place = (2 * lax.axis_index("xh") + lax.axis_index("xl")).astype(jnp.int32).reshape(1)
     packed = pack(visibility, weights, positions, station_pairs)
     own = lax.all_to_all(packed, "chan", split_axis=0, concat_axis=0, tiled=True)
     other = lax.ppermute(own, "zh", [(h, HALVES - 1 - h) for h in range(HALVES)])
     earlier = first_sums(half, facet_shift, own)
     images = make_images(half, facet_shift, other, earlier)
     parts = lax.all_to_all(
-        images, ("y", "x"), split_axis=0, concat_axis=0, tiled=True
+        images, ("xl", "y", "xh"), split_axis=0, concat_axis=0, tiled=True
     )
     scale = 1.0 / math.sqrt(READ_ROWS * GROUPS * 32 * LANES)
     return combine(scale, place, parts)
 
 
 def solution(mesh):
-    fine = Mesh(mesh.devices.reshape(GROUPS, 4, HALVES, 4), ("chan", "y", "zh", "x"))
-    line = ("y", "zh", "x")
+    line = ("y", "zh", "xh", "xl")
+    fine = Mesh(mesh.devices.reshape(GROUPS, 4, HALVES, 2, 2), ("chan", *line))
     in_specs = (
         P(None, ("chan", *line), None),
         P(("chan", *line), None),

time: 44 us -> 43.4 us (0.986); the launches traced: 43.7 us -> 42.6 us
  waiting for transfers between devices: 15.2 us -> 14.1 us
    all_to_all x1, waiting for transfers between devices: 10.3 us -> 9.16 us  [body(): lax.all_to_all(images, ('xl', 'y', 'xh'), split_axis=0, concat_axis=0, ti...]
where the time goes in v11:
time: 43.4 us; the launch traced here: 42.6 us
  starting transfers between devices  18.4 us (42%)
  waiting for transfers between devices  14.1 us (32%)
  Pallas kernels  10 us (23%)
    all_to_all x1, waiting for transfers between devices, body(): lax.all_to_all(images, ('xl', 'y', 'xh'), split_axis=0, concat_axis=0, ti...  9.16 us
    all_to_all x1, starting transfers between devices, body(): lax.all_to_all(packed, 'chan', split_axis=0, concat_axis=0, tiled=True)  7.4 us
    all_to_all x1, starting transfers between devices, body(): lax.all_to_all(images, ('xl', 'y', 'xh'), split_axis=0, concat_axis=0, ti...  6.75 us
    all_to_all x1, waiting for transfers between devices, body(): lax.all_to_all(packed, 'chan', split_axis=0, concat_axis=0, tiled=True)  4.97 us
    ppermute x1, starting transfers between devices, body(): lax.ppermute(own, 'zh', [(h, HALVES - 1 - h) for h in range(HALVES)])  4.29 us
    pallas_call x1, Pallas kernels, make_images(): pl.pallas_call(last_kernel, out_shape=jax.ShapeDtypeStruct((PEERS, OUT_RO...  4.16 us
    pallas_call x1, Pallas kernels, first_sums(): pl.pallas_call(first_kernel, out_shape=jax.ShapeDtypeStruct(SUMS, jnp.flo...  3.34 us
    pallas_call x1, Pallas kernels, pack(): pl.pallas_call(pack_kernel, out_shape=jax.ShapeDtypeStruct((GROUPS, 4 * R...  1.54 us
  transfers between devices with their start and end apart: 3, of which 2 were waited for; matrix products, arithmetic and copies ran while one was open for 0% of the time, Pallas kernels for 8%

profile of v11, /device:TPU:1, one launch (start us, length us, event | category | flops | bytes accessed | tf_op | source)
XLA Modules:
  0.0 42.6 jit_solution(12204058790841782759)
XLA Ops:
  0.0 1.5 %pack.1 = bf16[8,16,128]{2,1,0:T(8,128)(2,1)} custom-call(bf16[2,4,1024]{2,1,0:T(4,128)(2,1)} %vis_ref.1, bf16[4,1024]{1,0:T(4,128)(2,1)} %weight_ref.1, f32[2,512]{1,0:T(2,128)} %pos_ref.1, s32[2,4]{1,0:T(2,128)} %pair_ref.1), custom_call_target="tpu_custom_call" | custom-call | tf_op jit(solution)/shard_map/pack/pallas_call | solution.py:248
  1.5 7.4 %all-to-all-start = ((bf16[8,16,128]{2,1,0:T(8,128)(2,1)}), bf16[8,16,128]{2,1,0:T(8,128)(2,1)S(1)}, u32[]{:S(2)}, u32[]{:S(2)}) async-start(bf16[8,16,128]{2,1,0:T(8,128)(2,1)} %pack.1), calls=%async_computation | async-start | bytes 65536 | tf_op jit(solution)/shard_map/all_to_all | solution.py:318
  8.9 0.0 copy-start
  8.9 5.0 %all-to-all-done.data_ref = bf16[8,16,128]{2,1,0:T(8,128)(2,1)S(1)} async-done(((bf16[8,16,128]{2,1,0:T(8,128)(2,1)}), bf16[8,16,128]{2,1,0:T(8,128)(2,1)S(1)}, u32[]{:S(2)}, u32[]{:S(2)}) %all-to-all-start) | async-done | bytes 32800 | tf_op jit(solution)/shard_map/all_to_all | solution.py:318
  13.9 4.3 %collective-permute-start = (bf16[8,16,128]{2,1,0:T(8,128)(2,1)S(1)}, bf16[8,16,128]{2,1,0:T(8,128)(2,1)S(1)}, u32[]{:S(2)}, u32[]{:S(2)}) collective-permute-start(bf16[8,16,128]{2,1,0:T(8,128)(2,1)S(1)} %all-to-all-done.data_ref), channel_id=1, source_target_pairs={{0,4},{4,0},{1,5},{5,1},{2,6},{6,2},{3,7},{7,3},{8,12},{12,8},{9,1... | collective-permute-start | bytes 98312 | tf_op jit(solution)/shard_map/ppermute | solution.py:319
  18.2 0.0 copy-done
  18.2 3.3 %first_sums.1.earlier_ref = f32[2,512,256]{2,1,0:T(8,128)S(1)} custom-call(s32[1]{0:T(128)} %bitcast.1.place_ref, s32[2,2]{1,0:T(2,128)S(1)} %copy-done, bf16[8,16,128]{2,1,0:T(8,128)(2,1)S(1)} %all-to-all-done.data_ref), custom_call_target="tpu_custom_call" | custom-call | flops 2147483648 | bytes 1048576 | tf_op jit(solution)/shard_map/first_sums/pallas_call | solution.py:273
  21.6 0.0 collective-permute-done.data_ref
  21.6 4.2 %images.1 = bf16[16,16,1024]{2,1,0:T(8,128)(2,1)} custom-call(s32[1]{0:T(128)} %bitcast.1.place_ref, s32[2,2]{1,0:T(2,128)S(1)} %copy-done, bf16[8,16,128]{2,1,0:T(8,128)(2,1)S(1)} %collective-permute-done.data_ref, f32[2,512,256]{2,1,0:T(8,128)S(1)} %first_sums.1.earlier_ref), custom_call_target="tpu_custom_call" | custom-call | flops 2147483648 | bytes 1048576 | tf_op jit(solution)/shard_map/images/pallas_call | solution.py:286
  25.7 6.8 %all-to-all-start.1 = ((bf16[16,16,1024]{2,1,0:T(8,128)(2,1)}), bf16[16,16,1024]{2,1,0:T(8,128)(2,1)S(1)}, u32[]{:S(2)}, u32[]{:S(2)}) async-start(bf16[16,16,1024]{2,1,0:T(8,128)(2,1)} %images.1), calls=%async_computation.1 | async-start | bytes 1048576 | tf_op jit(solution)/shard_map/all_to_all | solution.py:322
  32.5 9.2 %all-to-all-done.1.data_ref = bf16[16,16,1024]{2,1,0:T(8,128)(2,1)S(1)} async-done(((bf16[16,16,1024]{2,1,0:T(8,128)(2,1)}), bf16[16,16,1024]{2,1,0:T(8,128)(2,1)S(1)}, u32[]{:S(2)}, u32[]{:S(2)}) %all-to-all-start.1) | async-done | bytes 524320 | tf_op jit(solution)/shard_map/all_to_all | solution.py:322
  41.7 1.0 %combine.1 = f32[1,16,1024]{2,1,0:T(8,128)} custom-call(s32[1]{0:T(128)} %bitcast.place_ref, bf16[16,16,1024]{2,1,0:T(8,128)(2,1)S(1)} %all-to-all-done.1.data_ref), custom_call_target="tpu_custom_call" | custom-call | tf_op jit(solution)/shard_map/combine/pallas_call | solution.py:304
Async XLA Ops:
  1.5 12.4 %all-to-all-start = ((bf16[8,16,128]{2,1,0:T(8,128)(2,1)}), bf16[8,16,128]{2,1,0:T(8,128)(2,1)S(1)}, u32[]{:S(2)}, u32[]{:S(2)}) async-start(bf16[8,16,128]{2,1,0:T(8,128)(2,1)} %pack.1), calls=%async_computation | async-start | bytes 65536 | tf_op jit(solution)/shard_map/all_to_all | solution.py:318
  8.9 9.3 %copy-start = (s32[2,2]{1,0:T(2,128)S(1)}, s32[2,2]{1,0:T(2,128)}, u32[]{:S(2)}) copy-start(s32[2,2]{1,0:T(2,128)} %shift_ref.3) | copy-start | bytes 52
  13.9 7.6 %collective-permute-start = (bf16[8,16,128]{2,1,0:T(8,128)(2,1)S(1)}, bf16[8,16,128]{2,1,0:T(8,128)(2,1)S(1)}, u32[]{:S(2)}, u32[]{:S(2)}) collective-permute-start(bf16[8,16,128]{2,1,0:T(8,128)(2,1)S(1)} %all-to-all-done.data_ref), channel_id=1, source_target_pairs={{0,4},{4,0},{1,5},{5,1},{2,6},{6,2},{3,7},{7,3},{8,12},{12,8},{9,1... | collective-permute-start | bytes 98312 | tf_op jit(solution)/shard_map/ppermute | solution.py:319
  25.7 15.9 %all-to-all-start.1 = ((bf16[16,16,1024]{2,1,0:T(8,128)(2,1)}), bf16[16,16,1024]{2,1,0:T(8,128)(2,1)S(1)}, u32[]{:S(2)}, u32[]{:S(2)}) async-start(bf16[16,16,1024]{2,1,0:T(8,128)(2,1)} %images.1), calls=%async_computation.1 | async-start | bytes 1048576 | tf_op jit(solution)/shard_map/all_to_all | solution.py:322

commit v12 on v11

--- a/solution.py
+++ b/solution.py
@@ -73,7 +73,7 @@
     for g in range(GROUPS):
         lanes = slice(g * LANES, (g + 1) * LANES)
         tile = [real[:, lanes], imag[:, lanes], weight[:, lanes], spans]
-        out_ref[g] = jnp.concatenate(tile, axis=0).astype(jnp.bfloat16)
+        out_ref[(g % 2) * (GROUPS // 2) + g // 2] = jnp.concatenate(tile, axis=0).astype(jnp.bfloat16)
 
 
 PHASED = 0
@@ -312,10 +312,10 @@
 
 
 def body(visibility, weights, positions, station_pairs, facet_shift):
-    half = (lax.axis_index("chan") * HALVES + lax.axis_index("zh")).astype(jnp.int32).reshape(1)
+    half = (lax.axis_index(("zl", "core")) * HALVES + lax.axis_index("zh")).astype(jnp.int32).reshape(1)
     place = (2 * lax.axis_index("xh") + lax.axis_index("xl")).astype(jnp.int32).reshape(1)
     packed = pack(visibility, weights, positions, station_pairs)
-    own = lax.all_to_all(packed, "chan", split_axis=0, concat_axis=0, tiled=True)
+    own = lax.all_to_all(packed, ("core", "zl"), split_axis=0, concat_axis=0, tiled=True)
     other = lax.ppermute(own, "zh", [(h, HALVES - 1 - h) for h in range(HALVES)])
     earlier = first_sums(half, facet_shift, own)
     images = make_images(half, facet_shift, other, earlier)
@@ -328,13 +328,13 @@
 
 def solution(mesh):
     line = ("y", "zh", "xh", "xl")
-    fine = Mesh(mesh.devices.reshape(GROUPS, 4, HALVES, 2, 2), ("chan", *line))
+    fine = Mesh(mesh.devices.reshape(GROUPS // 2, 2, 4, HALVES, 2, 2), ("zl", "core", *line))
     in_specs = (
-        P(None, ("chan", *line), None),
-        P(("chan", *line), None),
+        P(None, ("zl", "core", *line), None),
+        P(("zl", "core", *line), None),
         P(),
-        P(None, ("chan", *line)),
+        P(None, ("zl", "core", *line)),
         P(),
     )
-    out_specs = P("chan", line, None)
+    out_specs = P(("zl", "core"), line, None)
     return jax.shard_map(body, mesh=fine, in_specs=in_specs, out_specs=out_specs, check_vma=False)

time: 43.4 us -> 43.8 us (level)
  waiting for transfers between devices: 14.1 us -> 14.6 us
where the time goes in v12:
time: 43.8 us; the launch traced here: 43.1 us
  starting transfers between devices  18.4 us (42%)
  waiting for transfers between devices  14.6 us (33%)
  Pallas kernels  10 us (23%)
    all_to_all x1, waiting for transfers between devices, body(): lax.all_to_all(images, ('xl', 'y', 'xh'), split_axis=0, concat_axis=0, ti...  9.18 us
    all_to_all x1, starting transfers between devices, body(): lax.all_to_all(packed, ('core', 'zl'), split_axis=0, concat_axis=0, tiled...  7.4 us
    all_to_all x1, starting transfers between devices, body(): lax.all_to_all(images, ('xl', 'y', 'xh'), split_axis=0, concat_axis=0, ti...  6.75 us
    all_to_all x1, waiting for transfers between devices, body(): lax.all_to_all(packed, ('core', 'zl'), split_axis=0, concat_axis=0, tiled...  5.39 us
    ppermute x1, starting transfers between devices, body(): lax.ppermute(own, 'zh', [(h, HALVES - 1 - h) for h in range(HALVES)])  4.27 us
    pallas_call x1, Pallas kernels, make_images(): pl.pallas_call(last_kernel, out_shape=jax.ShapeDtypeStruct((PEERS, OUT_RO...  4.16 us
    pallas_call x1, Pallas kernels, first_sums(): pl.pallas_call(first_kernel, out_shape=jax.ShapeDtypeStruct(SUMS, jnp.flo...  3.34 us
    pallas_call x1, Pallas kernels, pack(): pl.pallas_call(pack_kernel, out_shape=jax.ShapeDtypeStruct((GROUPS, 4 * R...  1.54 us
  transfers between devices with their start and end apart: 3, of which 2 were waited for; matrix products, arithmetic and copies ran while one was open for 0% of the time, Pallas kernels for 8%

profile of v12, /device:TPU:1, one launch (start us, length us, event | category | flops | bytes accessed | tf_op | source)
XLA Modules:
  0.0 43.1 jit_solution(8109051410584660924)
XLA Ops:
  0.0 1.5 %pack.1 = bf16[8,16,128]{2,1,0:T(8,128)(2,1)} custom-call(bf16[2,4,1024]{2,1,0:T(4,128)(2,1)} %vis_ref.1, bf16[4,1024]{1,0:T(4,128)(2,1)} %weight_ref.1, f32[2,512]{1,0:T(2,128)} %pos_ref.1, s32[2,4]{1,0:T(2,128)} %pair_ref.1), custom_call_target="tpu_custom_call" | custom-call | tf_op jit(solution)/shard_map/pack/pallas_call | solution.py:248
  1.5 7.4 %all-to-all-start = ((bf16[8,16,128]{2,1,0:T(8,128)(2,1)}), bf16[8,16,128]{2,1,0:T(8,128)(2,1)S(1)}, u32[]{:S(2)}, u32[]{:S(2)}) async-start(bf16[8,16,128]{2,1,0:T(8,128)(2,1)} %pack.1), calls=%async_computation | async-start | bytes 65536 | tf_op jit(solution)/shard_map/all_to_all | solution.py:318
  8.9 0.0 copy-start
  8.9 5.4 %all-to-all-done.data_ref = bf16[8,16,128]{2,1,0:T(8,128)(2,1)S(1)} async-done(((bf16[8,16,128]{2,1,0:T(8,128)(2,1)}), bf16[8,16,128]{2,1,0:T(8,128)(2,1)S(1)}, u32[]{:S(2)}, u32[]{:S(2)}) %all-to-all-start) | async-done | bytes 32800 | tf_op jit(solution)/shard_map/all_to_all | solution.py:318
  14.3 4.3 %collective-permute-start = (bf16[8,16,128]{2,1,0:T(8,128)(2,1)S(1)}, bf16[8,16,128]{2,1,0:T(8,128)(2,1)S(1)}, u32[]{:S(2)}, u32[]{:S(2)}) collective-permute-start(bf16[8,16,128]{2,1,0:T(8,128)(2,1)S(1)} %all-to-all-done.data_ref), channel_id=1, source_target_pairs={{0,4},{4,0},{1,5},{5,1},{2,6},{6,2},{3,7},{7,3},{8,12},{12,8},{9,1... | collective-permute-start | bytes 98312 | tf_op jit(solution)/shard_map/ppermute | solution.py:319
  18.6 0.0 copy-done
  18.6 3.3 %first_sums.1.earlier_ref = f32[2,512,256]{2,1,0:T(8,128)S(1)} custom-call(s32[1]{0:T(128)} %bitcast.1.place_ref, s32[2,2]{1,0:T(2,128)S(1)} %copy-done, bf16[8,16,128]{2,1,0:T(8,128)(2,1)S(1)} %all-to-all-done.data_ref), custom_call_target="tpu_custom_call" | custom-call | flops 2147483648 | bytes 1048576 | tf_op jit(solution)/shard_map/first_sums/pallas_call | solution.py:273
  22.0 0.0 collective-permute-done.data_ref
  22.0 4.2 %images.1 = bf16[16,16,1024]{2,1,0:T(8,128)(2,1)} custom-call(s32[1]{0:T(128)} %bitcast.1.place_ref, s32[2,2]{1,0:T(2,128)S(1)} %copy-done, bf16[8,16,128]{2,1,0:T(8,128)(2,1)S(1)} %collective-permute-done.data_ref, f32[2,512,256]{2,1,0:T(8,128)S(1)} %first_sums.1.earlier_ref), custom_call_target="tpu_custom_call" | custom-call | flops 2147483648 | bytes 1048576 | tf_op jit(solution)/shard_map/images/pallas_call | solution.py:286
  26.1 6.8 %all-to-all-start.1 = ((bf16[16,16,1024]{2,1,0:T(8,128)(2,1)}), bf16[16,16,1024]{2,1,0:T(8,128)(2,1)S(1)}, u32[]{:S(2)}, u32[]{:S(2)}) async-start(bf16[16,16,1024]{2,1,0:T(8,128)(2,1)} %images.1), calls=%async_computation.1 | async-start | bytes 1048576 | tf_op jit(solution)/shard_map/all_to_all | solution.py:322
  32.9 9.2 %all-to-all-done.1.data_ref = bf16[16,16,1024]{2,1,0:T(8,128)(2,1)S(1)} async-done(((bf16[16,16,1024]{2,1,0:T(8,128)(2,1)}), bf16[16,16,1024]{2,1,0:T(8,128)(2,1)S(1)}, u32[]{:S(2)}, u32[]{:S(2)}) %all-to-all-start.1) | async-done | bytes 524320 | tf_op jit(solution)/shard_map/all_to_all | solution.py:322
  42.1 1.0 %combine.1 = f32[1,16,1024]{2,1,0:T(8,128)} custom-call(s32[1]{0:T(128)} %bitcast.place_ref, bf16[16,16,1024]{2,1,0:T(8,128)(2,1)S(1)} %all-to-all-done.1.data_ref), custom_call_target="tpu_custom_call" | custom-call | tf_op jit(solution)/shard_map/combine/pallas_call | solution.py:304
Async XLA Ops:
  1.5 12.8 %all-to-all-start = ((bf16[8,16,128]{2,1,0:T(8,128)(2,1)}), bf16[8,16,128]{2,1,0:T(8,128)(2,1)S(1)}, u32[]{:S(2)}, u32[]{:S(2)}) async-start(bf16[8,16,128]{2,1,0:T(8,128)(2,1)} %pack.1), calls=%async_computation | async-start | bytes 65536 | tf_op jit(solution)/shard_map/all_to_all | solution.py:318
  8.9 9.7 %copy-start = (s32[2,2]{1,0:T(2,128)S(1)}, s32[2,2]{1,0:T(2,128)}, u32[]{:S(2)}) copy-start(s32[2,2]{1,0:T(2,128)} %shift_ref.3) | copy-start | bytes 52
  14.3 7.6 %collective-permute-start = (bf16[8,16,128]{2,1,0:T(8,128)(2,1)S(1)}, bf16[8,16,128]{2,1,0:T(8,128)(2,1)S(1)}, u32[]{:S(2)}, u32[]{:S(2)}) collective-permute-start(bf16[8,16,128]{2,1,0:T(8,128)(2,1)S(1)} %all-to-all-done.data_ref), channel_id=1, source_target_pairs={{0,4},{4,0},{1,5},{5,1},{2,6},{6,2},{3,7},{7,3},{8,12},{12,8},{9,1... | collective-permute-start | bytes 98312 | tf_op jit(solution)/shard_map/ppermute | solution.py:319
  26.1 16.0 %all-to-all-start.1 = ((bf16[16,16,1024]{2,1,0:T(8,128)(2,1)}), bf16[16,16,1024]{2,1,0:T(8,128)(2,1)S(1)}, u32[]{:S(2)}, u32[]{:S(2)}) async-start(bf16[16,16,1024]{2,1,0:T(8,128)(2,1)} %images.1), calls=%async_computation.1 | async-start | bytes 1048576 | tf_op jit(solution)/shard_map/all_to_all | solution.py:322

commit v13 on v11

--- a/solution.py
+++ b/solution.py
@@ -106,7 +106,7 @@
                     a, b = acc[i, rows], acc[i, rows_imag]
                     below, above = (a - b, a + b) if i == 0 else (b + a, b - a)
                     for place, values in ((2 + k, below), (1 - k, above)):
-                        chunk = (place % 2) * 8 + r * 2 + place // 2
+                        chunk = place % 2 * 8 + r % 2 * 4 + place // 2 * 2 + r // 2
                         out_ref[chunk, :, column : column + HALF] = values.astype(jnp.bfloat16)
 
 
@@ -320,15 +320,15 @@
     earlier = first_sums(half, facet_shift, own)
     images = make_images(half, facet_shift, other, earlier)
     parts = lax.all_to_all(
-        images, ("xl", "y", "xh"), split_axis=0, concat_axis=0, tiled=True
+        images, ("xl", "yl", "xh", "yh"), split_axis=0, concat_axis=0, tiled=True
     )
     scale = 1.0 / math.sqrt(READ_ROWS * GROUPS * 32 * LANES)
     return combine(scale, place, parts)
 
 
 def solution(mesh):
-    line = ("y", "zh", "xh", "xl")
-    fine = Mesh(mesh.devices.reshape(GROUPS, 4, HALVES, 2, 2), ("chan", *line))
+    line = ("yh", "yl", "zh", "xh", "xl")
+    fine = Mesh(mesh.devices.reshape(GROUPS, 2, 2, HALVES, 2, 2), ("chan", *line))
     in_specs = (
         P(None, ("chan", *line), None),
         P(("chan", *line), None),

time: 43.4 us -> 44 us (1.014)
  waiting for transfers between devices: 14.1 us -> 14.9 us
    all_to_all x1, waiting for transfers between devices: 9.16 us -> 9.89 us  [body(): lax.all_to_all(images, ('xl', 'yl', 'xh', 'yh'), split_axis=0, concat_axi...]
where the time goes in v13:
time: 44 us; the launch traced here: 43.4 us
  starting transfers between devices  18.4 us (42%)
  waiting for transfers between devices  14.9 us (34%)
  Pallas kernels  10 us (23%)
    all_to_all x1, waiting for transfers between devices, body(): lax.all_to_all(images, ('xl', 'yl', 'xh', 'yh'), split_axis=0, concat_axi...  9.89 us
    all_to_all x1, starting transfers between devices, body(): lax.all_to_all(packed, 'chan', split_axis=0, concat_axis=0, tiled=True)  7.4 us
    all_to_all x1, starting transfers between devices, body(): lax.all_to_all(images, ('xl', 'yl', 'xh', 'yh'), split_axis=0, concat_axi...  6.75 us
    all_to_all x1, waiting for transfers between devices, body(): lax.all_to_all(packed, 'chan', split_axis=0, concat_axis=0, tiled=True)  4.97 us
    ppermute x1, starting transfers between devices, body(): lax.ppermute(own, 'zh', [(h, HALVES - 1 - h) for h in range(HALVES)])  4.29 us
    pallas_call x1, Pallas kernels, make_images(): pl.pallas_call(last_kernel, out_shape=jax.ShapeDtypeStruct((PEERS, OUT_RO...  4.16 us
    pallas_call x1, Pallas kernels, first_sums(): pl.pallas_call(first_kernel, out_shape=jax.ShapeDtypeStruct(SUMS, jnp.flo...  3.34 us
    pallas_call x1, Pallas kernels, pack(): pl.pallas_call(pack_kernel, out_shape=jax.ShapeDtypeStruct((GROUPS, 4 * R...  1.54 us
  transfers between devices with their start and end apart: 3, of which 2 were waited for; matrix products, arithmetic and copies ran while one was open for 0% of the time, Pallas kernels for 8%

profile of v13, /device:TPU:1, one launch (start us, length us, event | category | flops | bytes accessed | tf_op | source)
XLA Modules:
  0.0 43.4 jit_solution(7057022655871655803)
XLA Ops:
  0.0 1.5 %pack.1 = bf16[8,16,128]{2,1,0:T(8,128)(2,1)} custom-call(bf16[2,4,1024]{2,1,0:T(4,128)(2,1)} %vis_ref.1, bf16[4,1024]{1,0:T(4,128)(2,1)} %weight_ref.1, f32[2,512]{1,0:T(2,128)} %pos_ref.1, s32[2,4]{1,0:T(2,128)} %pair_ref.1), custom_call_target="tpu_custom_call" | custom-call | tf_op jit(solution)/shard_map/pack/pallas_call | solution.py:248
  1.5 7.4 %all-to-all-start = ((bf16[8,16,128]{2,1,0:T(8,128)(2,1)}), bf16[8,16,128]{2,1,0:T(8,128)(2,1)S(1)}, u32[]{:S(2)}, u32[]{:S(2)}) async-start(bf16[8,16,128]{2,1,0:T(8,128)(2,1)} %pack.1), calls=%async_computation | async-start | bytes 65536 | tf_op jit(solution)/shard_map/all_to_all | solution.py:318
  8.9 0.0 copy-start
  8.9 5.0 %all-to-all-done.data_ref = bf16[8,16,128]{2,1,0:T(8,128)(2,1)S(1)} async-done(((bf16[8,16,128]{2,1,0:T(8,128)(2,1)}), bf16[8,16,128]{2,1,0:T(8,128)(2,1)S(1)}, u32[]{:S(2)}, u32[]{:S(2)}) %all-to-all-start) | async-done | bytes 32800 | tf_op jit(solution)/shard_map/all_to_all | solution.py:318
  13.9 4.3 %collective-permute-start = (bf16[8,16,128]{2,1,0:T(8,128)(2,1)S(1)}, bf16[8,16,128]{2,1,0:T(8,128)(2,1)S(1)}, u32[]{:S(2)}, u32[]{:S(2)}) collective-permute-start(bf16[8,16,128]{2,1,0:T(8,128)(2,1)S(1)} %all-to-all-done.data_ref), channel_id=1, source_target_pairs={{0,4},{4,0},{1,5},{5,1},{2,6},{6,2},{3,7},{7,3},{8,12},{12,8},{9,1... | collective-permute-start | bytes 98312 | tf_op jit(solution)/shard_map/ppermute | solution.py:319
  18.2 0.0 copy-done
  18.2 3.3 %first_sums.1.earlier_ref = f32[2,512,256]{2,1,0:T(8,128)S(1)} custom-call(s32[1]{0:T(128)} %bitcast.1.place_ref, s32[2,2]{1,0:T(2,128)S(1)} %copy-done, bf16[8,16,128]{2,1,0:T(8,128)(2,1)S(1)} %all-to-all-done.data_ref), custom_call_target="tpu_custom_call" | custom-call | flops 2147483648 | bytes 1048576 | tf_op jit(solution)/shard_map/first_sums/pallas_call | solution.py:273
  21.6 0.0 collective-permute-done.data_ref
  21.6 4.2 %images.1 = bf16[16,16,1024]{2,1,0:T(8,128)(2,1)} custom-call(s32[1]{0:T(128)} %bitcast.1.place_ref, s32[2,2]{1,0:T(2,128)S(1)} %copy-done, bf16[8,16,128]{2,1,0:T(8,128)(2,1)S(1)} %collective-permute-done.data_ref, f32[2,512,256]{2,1,0:T(8,128)S(1)} %first_sums.1.earlier_ref), custom_call_target="tpu_custom_call" | custom-call | flops 2147483648 | bytes 1048576 | tf_op jit(solution)/shard_map/images/pallas_call | solution.py:286
  25.7 6.8 %all-to-all-start.1 = ((bf16[16,16,1024]{2,1,0:T(8,128)(2,1)}), bf16[16,16,1024]{2,1,0:T(8,128)(2,1)S(1)}, u32[]{:S(2)}, u32[]{:S(2)}) async-start(bf16[16,16,1024]{2,1,0:T(8,128)(2,1)} %images.1), calls=%async_computation.1 | async-start | bytes 1048576 | tf_op jit(solution)/shard_map/all_to_all | solution.py:322
  32.5 9.9 %all-to-all-done.1.data_ref = bf16[16,16,1024]{2,1,0:T(8,128)(2,1)S(1)} async-done(((bf16[16,16,1024]{2,1,0:T(8,128)(2,1)}), bf16[16,16,1024]{2,1,0:T(8,128)(2,1)S(1)}, u32[]{:S(2)}, u32[]{:S(2)}) %all-to-all-start.1) | async-done | bytes 524320 | tf_op jit(solution)/shard_map/all_to_all | solution.py:322
  42.4 1.0 %combine.1 = f32[1,16,1024]{2,1,0:T(8,128)} custom-call(s32[1]{0:T(128)} %bitcast.place_ref, bf16[16,16,1024]{2,1,0:T(8,128)(2,1)S(1)} %all-to-all-done.1.data_ref), custom_call_target="tpu_custom_call" | custom-call | tf_op jit(solution)/shard_map/combine/pallas_call | solution.py:304
Async XLA Ops:
  1.5 12.4 %all-to-all-start = ((bf16[8,16,128]{2,1,0:T(8,128)(2,1)}), bf16[8,16,128]{2,1,0:T(8,128)(2,1)S(1)}, u32[]{:S(2)}, u32[]{:S(2)}) async-start(bf16[8,16,128]{2,1,0:T(8,128)(2,1)} %pack.1), calls=%async_computation | async-start | bytes 65536 | tf_op jit(solution)/shard_map/all_to_all | solution.py:318
  8.9 9.3 %copy-start = (s32[2,2]{1,0:T(2,128)S(1)}, s32[2,2]{1,0:T(2,128)}, u32[]{:S(2)}) copy-start(s32[2,2]{1,0:T(2,128)} %shift_ref.3) | copy-start | bytes 52
  13.9 7.6 %collective-permute-start = (bf16[8,16,128]{2,1,0:T(8,128)(2,1)S(1)}, bf16[8,16,128]{2,1,0:T(8,128)(2,1)S(1)}, u32[]{:S(2)}, u32[]{:S(2)}) collective-permute-start(bf16[8,16,128]{2,1,0:T(8,128)(2,1)S(1)} %all-to-all-done.data_ref), channel_id=1, source_target_pairs={{0,4},{4,0},{1,5},{5,1},{2,6},{6,2},{3,7},{7,3},{8,12},{12,8},{9,1... | collective-permute-start | bytes 98312 | tf_op jit(solution)/shard_map/ppermute | solution.py:319
  25.7 16.7 %all-to-all-start.1 = ((bf16[16,16,1024]{2,1,0:T(8,128)(2,1)}), bf16[16,16,1024]{2,1,0:T(8,128)(2,1)S(1)}, u32[]{:S(2)}, u32[]{:S(2)}) async-start(bf16[16,16,1024]{2,1,0:T(8,128)(2,1)} %images.1), calls=%async_computation.1 | async-start | bytes 1048576 | tf_op jit(solution)/shard_map/all_to_all | solution.py:322
